TPU v7x, 128 devices: a whole 4x4x4 slice. The times are simulated.
128 devices in a mesh: ctx: 16 (over y, z_lo, core), head: 8 (over z_hi, x).
Axes of the slice: x: 4, y: 4, z: 4 (z_hi: 2, z_lo: 2; z = z_hi * 2 + z_lo), core: 2. Of those that a mesh axis runs over, the one named last changes fastest.
Arguments:
- q_nope: bfloat16 [1024, 8192], P('ctx', 'head'), may hold values from -0.59765625 to 0.59765625
- q_rope: bfloat16 [1024, 4096], P('ctx', 'head'), may hold values from -6 to 6
- w_uk: bfloat16 [64, 128, 512], P('head'), may hold values from -0.5 to 0.5
- w_uv: bfloat16 [64, 512, 128], P('head'), may hold values from -0.25 to 0.25
- w_o: bfloat16 [8192, 7168], P('head'), may hold values from -0.0625 to 0.0625
- latent_cache: bfloat16 [576, 16384], P(None, 'ctx'), may hold values from -36 to 36
- group_start: int32 [1], replicated, may hold values from 4096 to 15360
Outputs:
- attention_out: bfloat16 [1024, 7168], P('ctx', 'head')
All inputs are finite; a program needn't handle non-finite values.
Results may differ from a plain program's by a relative error of at most 0.02.
Values may be sent and summed in bfloat16 or wider, within the bound.
No kernel may reach another device: no remote copies, remote signals or barrier semaphores. Data moves between devices by JAX's collectives and lax.ppermute only.
A program may use at most 128 MiB of HBM per device.

v0:
```python
import math

import jax
import jax.numpy as jnp
from jax import lax
from jax.sharding import PartitionSpec as P

LATENT = 512
ROPE = 64
NOPE = 128
VDIM = 128


masked_score = -1e30


def score_scale():
    return (NOPE + ROPE) ** (-0.5) * (0.1 * math.log(32.0) + 1.0) ** 2


def absorb_queries(q_nope, q_rope, w_uk):
    local_heads = w_uk.shape[0]
    tokens_here = q_nope.shape[0]
    nope_part = q_nope.reshape(tokens_here, local_heads, NOPE)
    latent_query = jnp.einsum(
        "thn,hnl->thl", nope_part, w_uk, preferred_element_type=jnp.float32
    ).astype(jnp.bfloat16)
    rope_part = q_rope.reshape(tokens_here, local_heads, ROPE)
    return jnp.concatenate([latent_query, rope_part], axis=2)


def block_scores_of(query_rows, row_position, key_block, key_start):
    scores = jnp.dot(query_rows, key_block, preferred_element_type=jnp.float32) * score_scale()
    key_position = key_start + jnp.arange(key_block.shape[1], dtype=jnp.int32)
    visible = key_position[None, :] <= row_position[:, None]
    return (jnp.where(visible, scores, masked_score), visible)


def latent_product(weights, key_block):
    return lax.dot_general(
        weights.astype(jnp.bfloat16),
        key_block[:LATENT],
        (((1,), (1,)), ((), ())),
        preferred_element_type=jnp.float32,
    )


def online_update(running, query_rows, row_position, key_block, key_start):
    best_sofar, denominator, numerator = running
    scores, visible = block_scores_of(query_rows, row_position, key_block, key_start)
    new_best = jnp.maximum(best_sofar, jnp.max(scores, axis=1))
    decay_factor = jnp.exp(best_sofar - new_best)
    weights = jnp.where(visible, jnp.exp(scores - new_best[:, None]), 0.0)
    denominator = denominator * decay_factor + jnp.sum(weights, axis=1)
    numerator = numerator * decay_factor[:, None] + latent_product(weights, key_block)
    return (new_best, denominator, numerator)


def value_heads(latent_out, w_uv):
    leading = latent_out.astype(jnp.bfloat16)
    remainder = (latent_out - leading.astype(jnp.float32)).astype(jnp.bfloat16)
    first_term = jnp.einsum("thl,hlv->thv", leading, w_uv, preferred_element_type=jnp.float32)
    second_term = jnp.einsum("thl,hlv->thv", remainder, w_uv, preferred_element_type=jnp.float32)
    return first_term + second_term


def on_device(q_nope, q_rope, w_uk, w_uv, w_o, latent_cache, group_start):
    local_heads = w_uk.shape[0]
    tokens_here = q_nope.shape[0]
    queries = absorb_queries(q_nope, q_rope, w_uk)
    query_width = queries.shape[2]
    query_rows = queries.reshape(tokens_here * local_heads, query_width)
    first_token = group_start[0] + lax.axis_index("ctx") * tokens_here
    token_position = first_token + jnp.arange(tokens_here, dtype=jnp.int32)
    row_position = jnp.repeat(token_position, local_heads)
    row_total = query_rows.shape[0]
    initial = (
        jnp.full((row_total,), masked_score, jnp.float32),
        jnp.zeros((row_total,), jnp.float32),
        jnp.zeros((row_total, LATENT), jnp.float32),
    )
    cache_piece = lax.all_gather(latent_cache, "ctx", axis=1, tiled=True)
    span_keys = cache_piece.shape[1]
    step_keys = math.gcd(span_keys, 1024)

    def advance(position, current):
        key_block = lax.dynamic_slice_in_dim(cache_piece, position * step_keys, step_keys, 1)
        key_start = position * step_keys
        return online_update(current, query_rows, row_position, key_block, key_start)

    best_all, denominator, numerator = lax.fori_loop(0, span_keys // step_keys, advance, initial)
    latent_out = (numerator / denominator[:, None]).reshape(tokens_here, local_heads, LATENT)
    head_values = value_heads(latent_out, w_uv)
    head_out = head_values.reshape(tokens_here, local_heads * VDIM).astype(jnp.bfloat16)
    mixed_columns = lax.psum_scatter(
        lax.dot_general(
            w_o, head_out, (((0,), (1,)), ((), ())), preferred_element_type=jnp.float32
        ).astype(jnp.bfloat16),
        "head",
        scatter_dimension=0,
        tiled=True,
    ).astype(jnp.float32)
    return mixed_columns.T.astype(jnp.bfloat16)


def solution(mesh):
    placed = (
        P("ctx", "head"),
        P("ctx", "head"),
        P("head", None, None),
        P("head", None, None),
        P("head", None),
        P(None, "ctx"),
        P(),
    )
    return jax.shard_map(
        on_device, mesh=mesh, in_specs=placed, out_specs=P("ctx", "head"), check_vma=False
    )
```

profile of v0, /device:TPU:0, one launch (start us, length us, event | category | flops | bytes accessed | tf_op | source)
XLA Modules:
  0.0 301.5 jit_solution(1039286162593460201)
XLA Ops:
  10.6 102.4 %all-gather.2.cloned.1.call-done = bf16[576,16384]{1,0:T(8,128)(2,1)} async-done(((bf16[576,1024]{1,0:T(8,128)(2,1)}), bf16[576,16384]{1,0:T(8,128)(2,1)}) %all-gather.2.cloned.1.call-update) | async-done | bytes 18874384 | tf_op jit(solution)/shard_map/all_gather | solution.py:82
  113.0 91.6 %while.18 = (s32[]{:T(128)}, f32[512]{0:T(512)S(1)}, f32[512]{0:T(512)S(1)}, f32[512,512]{1,0:T(8,128)S(1)}, bf16[576,16384]{1,0:T(8,128)(2,1)}, /*index=5*/bf16...) while((s32[]{:T(128)}, f32[512]{0:T(512)S(1)}, ...), condition=%wide.region_3.4_spmd.clone, body=%wide.region_0.3_spmd.clone.sunk | while | flops 1150029312 | bytes 11268539 | solution.py:91
  116.2 2.5 convolution_add_fusion.3
  121.9 2.5 convolution_add_fusion.3
  124.6 2.4 fusion.45
  127.6 2.5 convolution_add_fusion.3
  133.4 2.5 convolution_add_fusion.3
  136.1 2.3 fusion.45
  139.1 2.5 convolution_add_fusion.3
  141.8 2.3 fusion.45
  144.8 2.5 convolution_add_fusion.3
  150.5 2.5 convolution_add_fusion.3
  156.3 2.5 convolution_add_fusion.3
  162.0 2.5 convolution_add_fusion.3
  164.7 2.3 fusion.45
  167.7 2.5 convolution_add_fusion.3
  173.4 2.5 convolution_add_fusion.3
  179.2 2.5 convolution_add_fusion.3
  184.9 2.5 convolution_add_fusion.3
  190.6 2.5 convolution_add_fusion.3
  196.4 2.5 convolution_add_fusion.3
  202.1 2.5 convolution_add_fusion.3
  207.3 7.9 %fusion.21 = bf16[7168,64]{0,1:T(8,128)(2,1)S(1)} fusion(bf16[1024,7168]{1,0:T(8,128)(2,1)} %param.13, bf16[8,8,8,128]{3,2,1,0:T(8,128)(2,1)S(1)} %fusion.24), kind=kOutput, calls=%fused_computation.28 | convolution fusion | flops 939982848 | bytes 15728640 | tf_op jit(solution)/shard_map/dot_general | solution.py:96
  216.9 76.1 %reduce-scatter.4.cloned.1.call-done = bf16[896,64]{1,0:T(8,128)(2,1)} async-done(((bf16[7168,64]{1,0:T(8,128)(2,1)}), bf16[896,64]{1,0:T(8,128)(2,1)}) %reduce-scatter.4.cloned.1.call-update) | async-done | bytes 114704
  (145 shorter events, 50.5 us)
Async XLA Ops:
  6.5 2.4 copy-start
  6.5 106.5 %all-gather.2.cloned.1.call-start = ((), (), s32[]{:S(2)}) async-start(), calls=%async_computation.1 | async-start | bytes 20054016 | tf_op jit(solution)/shard_map/all_gather | solution.py:82
  7.3 285.7 %reduce-scatter.4.cloned.1.call-start = ((), (), s32[]{:S(2)}) async-start(), calls=%async_computation.2 | async-start | bytes 2064384
  204.6 1.2 copy-start.1
Sparse Core Ops, SparseCore 0:
  9.0 103.9 all-gather.1
  217.0 75.8 reduce-scatter.3
where the time goes:
time: 303 us; the launch traced here: 301 us
  waiting for transfers between devices  179 us (59%)
  matrix products  88.2 us (29%)
  between operations  14.2 us (5%)
  other arithmetic  10.6 us (3%)
  local copies, waits for them, and re-layouts  8.39 us (3%)
    all_gather x1, waiting for transfers between devices, on_device(): cache_piece = lax.all_gather(latent_cache, 'ctx', axis=1, tiled=True)  102 us
    unnamed x3, waiting for transfers between devices  76.8 us
    dot_general x16, matrix products, latent_product(): lax.dot_general(weights.astype(jnp.bfloat16), key_block[:LATENT], (((1,),...  40.1 us
    dot_general x16, matrix products, block_scores_of(): jnp.dot(query_rows, key_block, preferred_element_type=jnp.float32)  37.5 us
    reduce_sum x16, other arithmetic, online_update(): denominator = denominator * decay_factor + jnp.sum(weights, axis=1)  9.93 us
    dot_general x1, matrix products, on_device(): lax.dot_general(w_o, head_out, (((0,), (1,)), ((), ())), preferred_elemen...  7.91 us
  transfers between devices with their start and end apart: 2, of which 2 were waited for; matrix products, arithmetic and copies ran while one was open for 1% of the time, Pallas kernels for 0%

commit v1 on v0

v1 whole, which is shorter than its diff:
```python
import functools
import math

import jax
import jax.numpy as jnp
from jax import lax
from jax.experimental import pallas as pl
from jax.experimental.pallas import tpu as pltpu
from jax.sharding import PartitionSpec as P

LATENT = 512
ROPE = 64
NOPE = 128
VDIM = 128
HALF = 4
SLOTS = 1024
TOK = 64
PIECE = 2 * TOK
ROWS = PIECE + 16
STEP = 256

F32 = jnp.float32
BF16 = jnp.bfloat16
MASKED = -1e30
SCALE2 = (NOPE + ROPE) ** (-0.5) * (0.1 * math.log(32.0) + 1.0) ** 2 * math.log2(math.e)
VMEM = 56 << 20

CORE = [(i, i ^ 1) for i in range(16)]
ZLO = [(i, i ^ 2) for i in range(16)]
YP = [(i, (i + 4) % 16) for i in range(16)]
YM = [(i, (i - 4) % 16) for i in range(16)]
Y2 = [(i, (i + 8) % 16) for i in range(16)]
XP = [(i, (i // 4) * 4 + (i + 1) % 4) for i in range(8)]
XM = [(i, (i // 4) * 4 + (i - 1) % 4) for i in range(8)]
X2 = [(i, (i // 4) * 4 + (i + 2) % 4) for i in range(8)]
ZHI = [(i, i ^ 4) for i in range(8)]


def to_ctx(array, pairs):
    return lax.ppermute(array, "ctx", pairs)


def to_head(array, pairs):
    return lax.ppermute(array, "head", pairs)


def keys_values_kernel(where_ref, cache_ref, uk_ref, uv_ref, key_ref, val_ref):
    latent = cache_ref[:LATENT]
    rope = cache_ref[LATENT:]
    uk = uk_ref[...].reshape(HALF * NOPE, LATENT)
    keys = jnp.dot(uk, latent, preferred_element_type=F32).astype(BF16)
    uv = jnp.concatenate([uv_ref[h] for h in range(HALF)], axis=1)
    vals = jnp.dot(latent.T, uv, preferred_element_type=F32).astype(BF16)
    blank = jnp.zeros_like(rope)
    ones = jnp.ones((SLOTS, VDIM), BF16)
    for h in range(HALF):
        key_ref[h, :NOPE] = keys[h * NOPE : (h + 1) * NOPE]
        key_ref[h, NOPE : NOPE + ROPE] = rope if h % 2 == 0 else blank
        key_ref[h, NOPE + ROPE :] = blank if h % 2 == 0 else rope
        val_ref[h, :, :VDIM] = vals[:, h * VDIM : (h + 1) * VDIM]
        val_ref[h, :, VDIM:] = ones


def keys_values(where, cache, w_uk, w_uv):
    whole = lambda shape: pl.BlockSpec(shape, lambda i, w: (0,) * len(shape))
    return pl.pallas_call(
        keys_values_kernel,
        grid_spec=pltpu.PrefetchScalarGridSpec(
            num_scalar_prefetch=1,
            grid=(1,),
            in_specs=[
                whole((LATENT + ROPE, SLOTS)),
                pl.BlockSpec((HALF, NOPE, LATENT), lambda i, w: (w[1], 0, 0)),
                pl.BlockSpec((HALF, LATENT, VDIM), lambda i, w: (w[1], 0, 0)),
            ],
            out_specs=[whole((HALF, 256, SLOTS)), whole((HALF, SLOTS, 256))],
        ),
        out_shape=[
            jax.ShapeDtypeStruct((HALF, 256, SLOTS), BF16),
            jax.ShapeDtypeStruct((HALF, SLOTS, 256), BF16),
        ],
        cost_estimate=pl.CostEstimate(
            flops=4 * HALF * NOPE * LATENT * SLOTS, bytes_accessed=6 << 20, transcendentals=0
        ),
        compiler_params=pltpu.CompilerParams(vmem_limit_bytes=VMEM),
        name="keys_values",
    )(where, cache, w_uk, w_uv)


def split3(x):
    a = x.astype(BF16)
    r = x - a.astype(F32)
    b = r.astype(BF16)
    return a, b, (r - b.astype(F32)).astype(BF16)


def store_piece(o_ref, out, lse):
    o_ref[:PIECE] = out.astype(BF16)
    row = lse.T[:1]
    a, b, c = split3(row)
    index = lax.broadcasted_iota(jnp.int32, (16, PIECE), 0)
    spread = lambda v: jnp.broadcast_to(v.astype(F32), (16, PIECE))
    pick = jnp.where(index == 0, spread(a), jnp.where(index == 1, spread(b), jnp.where(index == 2, spread(c), 0.0)))
    o_ref[PIECE:] = pick.astype(BF16)


def attention_kernel(n, where_ref, *refs):
    q_refs, (k0, v0, k1, v1), o_refs = refs[: 2 * n], refs[2 * n : 2 * n + 4], refs[2 * n + 4 :]
    start = where_ref[0]
    core = where_ref[1]
    chip = where_ref[2]
    first = chip * (2 * SLOTS)
    rows = n * PIECE
    q = jnp.concatenate(
        [jnp.concatenate([q_refs[2 * i][...], q_refs[2 * i + 1][...]], axis=1) for i in range(n)], axis=0
    )
    blocks = ((k0, v0, first + core * SLOTS), (k1, v1, first + (1 - core) * SLOTS))

    def positions():
        place = lax.broadcasted_iota(jnp.int32, (PIECE, 1), 0)
        mine = place < TOK
        inner = jnp.where(mine, place, place - TOK)
        side = jnp.where(mine, core, 1 - core)
        local = start + inner + side * TOK
        return jnp.concatenate([local + where_ref[3 + i] * PIECE for i in range(n)], axis=0)

    def scores(k, c):
        return jnp.dot(q, k[0, :, c * STEP : (c + 1) * STEP], preferred_element_type=F32) * SCALE2

    def seen(pos, base, c):
        key = base + c * STEP + lax.broadcasted_iota(jnp.int32, (1, STEP), 1)
        return key <= pos

    def finish(acc, shift):
        total = acc[:, VDIM:]
        none = total == 0.0
        safe = jnp.where(none, 1.0, total)
        out = acc[:, :VDIM] / safe
        lse = jnp.where(none, MASKED, jnp.log2(safe) + shift)
        for i in range(n):
            store_piece(o_refs[i], out[i * PIECE : (i + 1) * PIECE], lse[i * PIECE : (i + 1) * PIECE])

    def quick(masked):
        pos = positions() if masked else None
        acc = None
        for k, v, base in blocks:
            for c in range(SLOTS // STEP):
                p = jnp.exp2(scores(k, c))
                if masked:
                    p = jnp.where(seen(pos, base, c), p, 0.0)
                term = jnp.dot(p.astype(BF16), v[0, c * STEP : (c + 1) * STEP], preferred_element_type=F32)
                acc = term if acc is None else acc + term
        total = acc[:, VDIM:]
        good = (total > 1e-27) & (total < 1e30)
        if masked:
            good = good | (pos < first)
        finish(acc, 0.0)
        return jnp.min(good.astype(F32))

    def careful():
        pos = positions()
        best = jnp.full((rows, 1), MASKED, F32)
        for k, v, base in blocks:
            for c in range(SLOTS // STEP):
                s = jnp.where(seen(pos, base, c), scores(k, c), MASKED)
                best = jnp.maximum(best, jnp.max(s, axis=1, keepdims=True))
        acc = jnp.zeros((rows, 2 * VDIM), F32)
        for k, v, base in blocks:
            for c in range(SLOTS // STEP):
                p = jnp.where(seen(pos, base, c), jnp.exp2(scores(k, c) - best), 0.0)
                acc += jnp.dot(p.astype(BF16), v[0, c * STEP : (c + 1) * STEP], preferred_element_type=F32)
        finish(acc, best)

    everything = first + 2 * SLOTS - 1 <= start
    nothing = first > start + 16 * TOK - 1

    @pl.when(nothing)
    def _():
        for o in o_refs:
            store_piece(o, jnp.zeros((PIECE, VDIM), F32), jnp.full((PIECE, VDIM), MASKED, F32))

    @pl.when(everything)
    def _():
        good = quick(False)

        @pl.when(good < 0.5)
        def _():
            careful()

    @pl.when(jnp.logical_not(everything | nothing))
    def _():
        good = quick(True)

        @pl.when(good < 0.5)
        def _():
            careful()


def attention(where, pieces, own, other):
    n = len(pieces)
    q_specs = []
    q_args = []
    for piece in pieces:
        q_specs += [
            pl.BlockSpec((PIECE, NOPE), lambda h, w: (0, h)),
            pl.BlockSpec((PIECE, 2 * ROPE), lambda h, w: (0, HALF + h // 2)),
        ]
        q_args += [piece, piece]
    kv_specs = [
        pl.BlockSpec((1, 256, SLOTS), lambda h, w: (h, 0, 0)),
        pl.BlockSpec((1, SLOTS, 256), lambda h, w: (h, 0, 0)),
    ] * 2
    return pl.pallas_call(
        functools.partial(attention_kernel, n),
        grid_spec=pltpu.PrefetchScalarGridSpec(
            num_scalar_prefetch=1,
            grid=(HALF,),
            in_specs=q_specs + kv_specs,
            out_specs=[pl.BlockSpec((ROWS, VDIM), lambda h, w: (0, h))] * n,
        ),
        out_shape=[jax.ShapeDtypeStruct((ROWS, HALF * VDIM), BF16)] * n,
        cost_estimate=pl.CostEstimate(
            flops=2 * HALF * n * PIECE * 2 * SLOTS * 512,
            bytes_accessed=8 << 20,
            transcendentals=HALF * n * PIECE * 2 * SLOTS,
        ),
        compiler_params=pltpu.CompilerParams(vmem_limit_bytes=VMEM),
        name="attention",
    )(where, *q_args, *own, *other)


def join_kernel(n, last, *refs):
    pieces, o_ref = refs[:n], refs[n]
    logs = [sum(p[PIECE + j : PIECE + j + 1].astype(F32) for j in range(3)) for p in pieces]
    best = functools.reduce(jnp.maximum, logs)
    shares = [jnp.exp2(v - best) for v in logs]
    total = sum(shares)
    stack = jnp.concatenate([s / total for s in shares] + [best + jnp.log2(total)], axis=0)
    for h in range(HALF):
        lanes = slice(h * VDIM, (h + 1) * VDIM)
        part = stack[:, lanes]
        part = jnp.concatenate([part, jnp.zeros((8 - n - 1, PIECE), F32)], axis=0) if n < 7 else part
        cols = part.T
        out = sum(p[:PIECE, lanes].astype(F32) * cols[:, i : i + 1] for i, p in enumerate(pieces))
        o_ref[:PIECE, lanes] = out.astype(BF16)
    if not last:
        a, b, c = split3(stack[n : n + 1])
        o_ref[PIECE:] = jnp.concatenate(
            [a.astype(F32), b.astype(F32), c.astype(F32), jnp.zeros((13, HALF * VDIM), F32)], axis=0
        ).astype(BF16)


def join(pieces, last=False):
    n = len(pieces)
    width = HALF * VDIM
    rows = PIECE if last else ROWS
    return pl.pallas_call(
        functools.partial(join_kernel, n, last),
        grid=(1,),
        in_specs=[pl.BlockSpec((ROWS, width), lambda i, b=b: (b, 0)) for _, b in pieces],
        out_specs=pl.BlockSpec((rows, width), lambda i: (0, 0)),
        out_shape=jax.ShapeDtypeStruct((rows, width), BF16),
        cost_estimate=pl.CostEstimate(flops=1 << 20, bytes_accessed=1 << 20, transcendentals=4096),
        name="join",
    )(*[a for a, _ in pieces])


def project_kernel(where_ref, mine_ref, theirs_ref, top_ref, low_ref, o_ref):
    acc = jnp.dot(mine_ref[...], top_ref[...], preferred_element_type=F32)
    acc += jnp.dot(theirs_ref[...], low_ref[...], preferred_element_type=F32)
    o_ref[...] = acc.astype(BF16)


def project(where, mine, theirs, w_o, step):
    wide = w_o.shape[1] // 8
    width = HALF * VDIM

    def column(j, w):
        return jnp.where(j == 0, w[8], 1 - w[8]) * 4 + (w[7] + step) % 4

    return pl.pallas_call(
        project_kernel,
        grid_spec=pltpu.PrefetchScalarGridSpec(
            num_scalar_prefetch=1,
            grid=(2,),
            in_specs=[
                pl.BlockSpec((TOK, width), lambda j, w: (0, 0)),
                pl.BlockSpec((TOK, width), lambda j, w: (0, 0)),
                pl.BlockSpec((width, wide), lambda j, w: (w[1], column(j, w))),
                pl.BlockSpec((width, wide), lambda j, w: (1 - w[1], column(j, w))),
            ],
            out_specs=pl.BlockSpec((TOK, wide), lambda j, w: (j, 0)),
        ),
        out_shape=jax.ShapeDtypeStruct((2 * TOK, wide), BF16),
        cost_estimate=pl.CostEstimate(
            flops=2 * 2 * 256 * wide * 1024, bytes_accessed=4 << 20, transcendentals=0
        ),
        name="project",
    )(where, mine, theirs, w_o, w_o)


def on_device(q_nope, q_rope, w_uk, w_uv, w_o, latent_cache, group_start):
    ctx = lax.axis_index("ctx")
    head = lax.axis_index("head")
    core = ctx % 2
    chip = ctx // 2
    y = chip // 2
    z = chip % 2
    place = lambda dy, flip: ((y + dy) % 4) * 2 + (z ^ flip)
    spots = lambda *chips: jnp.stack(
        [group_start[0], core, chip, *chips, head % 4, head // 4]
    ).astype(jnp.int32)
    near = spots(place(0, 0), place(0, 1), place(1, 0), place(3, 0))
    far = spots(place(1, 1), place(3, 1), place(2, 0), place(2, 1))

    def half(side):
        return jnp.concatenate(
            [
                lax.dynamic_slice_in_dim(q_nope, side * (HALF * NOPE), HALF * NOPE, 1),
                lax.dynamic_slice_in_dim(q_rope, side * (HALF * ROPE), HALF * ROPE, 1),
            ],
            axis=1,
        )

    given = to_ctx(half(1 - core), CORE)
    cache_other = to_ctx(latent_cache, CORE)
    u = jnp.concatenate([half(core), given], axis=0)
    w = to_ctx(u, ZLO)
    d_u = to_ctx(u, Y2)
    m_u = to_ctx(u, YP)
    p_u = to_ctx(u, YM)
    m_w = to_ctx(w, YP)
    p_w = to_ctx(w, YM)
    d_w = to_ctx(d_u, ZLO)

    own = keys_values(near, latent_cache, w_uk, w_uv)
    other = keys_values(near, cache_other, w_uk, w_uv)
    r_u, r_w, r_pu, r_mu = attention(near, [u, w, p_u, m_u], own, other)
    r_pw, r_mw, r_du, r_dw = attention(far, [p_w, m_w, d_u, d_w], own, other)

    across = to_ctx(r_dw, ZLO)
    from_d = to_ctx(join([(r_du, 0), (across, 0)]), Y2)
    from_m = to_ctx(jnp.concatenate([r_pu, r_pw], axis=0), YP)
    from_p = to_ctx(jnp.concatenate([r_mu, r_mw], axis=0), YM)
    from_z = to_ctx(join([(r_w, 0), (from_m, 1), (from_p, 1)]), ZLO)
    values = join([(r_u, 0), (from_m, 0), (from_p, 0), (from_d, 0), (from_z, 0)], last=True)

    theirs = to_ctx(values[TOK:], CORE)
    mine = values[:TOK]
    out2 = to_head(project(near, mine, theirs, w_o, 2), X2)
    out1 = to_head(project(near, mine, theirs, w_o, 1), XP)
    out3 = to_head(project(near, mine, theirs, w_o, 3), XM)
    out0 = project(near, mine, theirs, w_o, 0)
    total = out0.astype(F32) + out1.astype(F32) + out2.astype(F32) + out3.astype(F32)
    back = to_head(total[TOK:].astype(BF16), ZHI)
    return (total[:TOK] + back.astype(F32)).astype(BF16)


def solution(mesh):
    placed = (
        P("ctx", "head"),
        P("ctx", "head"),
        P("head", None, None),
        P("head", None, None),
        P("head", None),
        P(None, "ctx"),
        P(),
    )
    return jax.shard_map(
        on_device, mesh=mesh, in_specs=placed, out_specs=P("ctx", "head"), check_vma=False
    )
```

time: 303 us -> 130 us (0.43)
  waiting for transfers between devices: 179 us -> 17.7 us
  matrix products: 88.2 us -> 0 us
  Pallas kernels: 0 us -> 73.6 us
  starting transfers between devices: 0.04 us -> 22.1 us
  between operations: 14.2 us -> 0.89 us
  other arithmetic: 10.6 us -> 3.6 us
    all_gather x1 -> x0, waiting for transfers between devices: 102 us -> none  [on_device(): cache_piece = lax.all_gather(latent_cache, 'ctx', axis=1, tiled=True)]
    dot_general x36 -> x0, matrix products: 88.2 us -> none  [the longest x16 40.1 us: latent_product(): lax.dot_general(weights.astype(jnp.bfloat16), key_block[:LATENT], (((1,),...]
    unnamed x3 -> x0, waiting for transfers between devices: 76.8 us -> none
    pallas_call x0 -> x11, Pallas kernels: none -> 73.6 us  [the longest x2 40.2 us: attention(): pl.pallas_call(functools.partial(attention_kernel, n), grid_spec=pltpu.Pr...]
    ppermute x0 -> x19, starting transfers between devices: none -> 22.1 us  [the longest x15 12.8 us: to_ctx(): return lax.ppermute(array, 'ctx', pairs)]
    ppermute x0 -> x19, waiting for transfers between devices: none -> 17.7 us  [the longest x15 12.9 us: to_ctx(): return lax.ppermute(array, 'ctx', pairs)]
    reduce_sum x16 -> x0, other arithmetic: 9.93 us -> none  [online_update(): denominator = denominator * decay_factor + jnp.sum(weights, axis=1)]
  transfers between devices with their start and end apart: 2 -> 19, of which waited for: 2 -> 7; matrix products, arithmetic and copies ran while one was open for 1% -> 3% of each run, Pallas kernels for 0% -> 37%
where the time goes in v1:
time: 130 us; the launch traced here: 128 us
  Pallas kernels  73.6 us (57%)
  starting transfers between devices  22.1 us (17%)
  waiting for transfers between devices  17.7 us (14%)
  local copies, waits for them, and re-layouts  10.1 us (8%)
  other arithmetic  3.6 us (3%)
    pallas_call x2, Pallas kernels, attention(): pl.pallas_call(functools.partial(attention_kernel, n), grid_spec=pltpu.Pr...  40.2 us
    pallas_call x4, Pallas kernels, project(): pl.pallas_call(project_kernel, grid_spec=pltpu.PrefetchScalarGridSpec(num...  15.3 us
    ppermute x15, waiting for transfers between devices, to_ctx(): return lax.ppermute(array, 'ctx', pairs)  12.9 us
    ppermute x15, starting transfers between devices, to_ctx(): return lax.ppermute(array, 'ctx', pairs)  12.8 us
    pallas_call x2, Pallas kernels, keys_values(): pl.pallas_call(keys_values_kernel, grid_spec=pltpu.PrefetchScalarGridSpec...  11.2 us
    ppermute x4, starting transfers between devices, to_head(): return lax.ppermute(array, 'head', pairs)  9.32 us
    pallas_call x3, Pallas kernels, join(): pl.pallas_call(functools.partial(join_kernel, n, last), grid=(1,), in_spe...  6.8 us
    unnamed x34, local copies, waits for them, and re-layouts  5.7 us
  transfers between devices with their start and end apart: 19, of which 7 were waited for; matrix products, arithmetic and copies ran while one was open for 3% of the time, Pallas kernels for 37%

profile of v1, /device:TPU:0, one launch (start us, length us, event | category | flops | bytes accessed | tf_op | source)
XLA Modules:
  0.0 128.0 jit_solution(8023676128314064841)
XLA Ops:
  3.2 2.1 %collective-permute-start.1 = (bf16[128,768]{1,0:T(8,128)(2,1)S(1)}, bf16[128,768]{1,0:T(8,128)(2,1)S(1)}, u32[]{:S(2)}, u32[]{:S(2)}) collective-permute-start(bf16[128,768]{1,0:T(8,128)(2,1)S(1)} %pad_maximum_fusion.2.refs_0_.refs_1_), channel_id=1, source_target_pairs={{0,16},{8,24},{16,0},{24,8},{32,48},{40,56},{48,32},{56,40},{64,80... | collective-permute-start | bytes 589832 | tf_op jit(solution)/shard_map/ppermute | solution.py:40
  5.3 3.2 %collective-permute-start.7 = (bf16[128,768]{1,0:T(8,128)(2,1)S(1)}, bf16[128,768]{1,0:T(8,128)(2,1)S(1)}, u32[]{:S(2)}, u32[]{:S(2)}) collective-permute-start(bf16[128,768]{1,0:T(8,128)(2,1)S(1)} %pad_maximum_fusion.2.refs_0_.refs_1_), channel_id=1, source_target_pairs={{0,64},{8,72},{16,80},{24,88},{32,96},{40,104},{48,112},{56,120},{... | collective-permute-start | bytes 589832 | tf_op jit(solution)/shard_map/ppermute | solution.py:40
  12.4 5.6 %keys_values.2 = (bf16[4,256,1024]{2,1,0:T(8,128)(2,1)}, bf16[4,1024,256]{2,1,0:T(8,128)(2,1)}) custom-call(s32[9]{0:T(128)} %stack.54.where_ref, bf16[576,1024]{1,0:T(8,128)(2,1)} %cache_ref.1, bf16[8,128,512]{2,1,0:T(8,128)(2,1)} %uk_ref.3, bf16[8,512,128]{2,1,0:T(8,128)(2,1)} %uv_ref.3), custom_call_target="tpu_custom_call" | custom-call | flops 1073741824 | bytes 6291456 | tf_op jit(solution)/shard_map/keys_values/pallas_call | solution.py:66
  18.1 2.3 %collective-permute-start.5 = (bf16[128,768]{1,0:T(8,128)(2,1)S(1)}, bf16[128,768]{1,0:T(8,128)(2,1)S(1)}, u32[]{:S(2)}, u32[]{:S(2)}) collective-permute-start(bf16[128,768]{1,0:T(8,128)(2,1)S(1)} %collective-permute-done.1.refs_2_.refs_3_), channel_id=1, source_target_pairs={{0,96},{8,104},{16,112},{24,120},{32,0},{40,8},{48,16},{56,24},{64... | collective-permute-start | bytes 589832 | tf_op jit(solution)/shard_map/ppermute | solution.py:40
  21.5 5.6 %keys_values.3 = (bf16[4,256,1024]{2,1,0:T(8,128)(2,1)}, bf16[4,1024,256]{2,1,0:T(8,128)(2,1)}) custom-call(s32[9]{0:T(128)} %stack.54.where_ref, bf16[576,1024]{1,0:T(8,128)(2,1)} %copy-done.9, bf16[8,128,512]{2,1,0:T(8,128)(2,1)} %uk_ref.3, bf16[8,512,128]{2,1,0:T(8,128)(2,1)} %uv_ref.3), custom_call_target="tpu_custom_call" | custom-call | flops 1073741824 | bytes 6291456 | tf_op jit(solution)/shard_map/keys_values/pallas_call | solution.py:66
  27.9 20.0 %attention.2 = (bf16[144,512]{1,0:T(8,128)(2,1)}, bf16[144,512]{1,0:T(8,128)(2,1)}, bf16[144,512]{1,0:T(8,128)(2,1)}, bf16[144,512]{1,0:T(8,128)(2,1)}) custom-call(s32[9]{0:T(128)} %stack.54.where_ref, bf16[128,768]{1,0:T(8,128)(2,1)} %copy-done.3, bf16[128,768]{1,0:T(8,128)(2,1)} %copy-done.3, bf16[128,768]{1,0:T(8,128)(2,1)} %copy-done.11, ...), custom_call_target="tpu_custom_call" | custom-call | flops 4294967296 | bytes 8388608 | tf_op jit(solution)/shard_map/attention/pallas_call | solution.py:213
  49.4 20.2 %attention.3 = (bf16[144,512]{1,0:T(8,128)(2,1)}, bf16[144,512]{1,0:T(8,128)(2,1)}, bf16[144,512]{1,0:T(8,128)(2,1)}, bf16[144,512]{1,0:T(8,128)(2,1)}) custom-call(s32[9]{0:T(128)} %stack.59.where_ref, bf16[128,768]{1,0:T(8,128)(2,1)} %copy-done.12, bf16[128,768]{1,0:T(8,128)(2,1)} %copy-done.12, bf16[128,768]{1,0:T(8,128)(2,1)} %copy-done.13, ...), custom_call_target="tpu_custom_call" | custom-call | flops 4294967296 | bytes 8388608 | tf_op jit(solution)/shard_map/attention/pallas_call | solution.py:213
  71.6 2.1 %collective-permute-start.9 = (bf16[288,512]{1,0:T(8,128)(2,1)S(1)}, bf16[288,512]{1,0:T(8,128)(2,1)S(1)}, u32[]{:S(2)}, u32[]{:S(2)}) collective-permute-start(bf16[288,512]{1,0:T(8,128)(2,1)S(1)} %pad_maximum_fusion), channel_id=1, source_target_pairs={{0,32},{8,40},{16,48},{24,56},{32,64},{40,72},{48,80},{56,88},{64,... | collective-permute-start | bytes 884744 | tf_op jit(solution)/shard_map/ppermute | solution.py:40
  73.7 5.4 %collective-permute-done.11.refs_1_ = bf16[144,512]{1,0:T(8,128)(2,1)S(1)} collective-permute-done((bf16[144,512]{1,0:T(8,128)(2,1)}, bf16[144,512]{1,0:T(8,128)(2,1)S(1)}, u32[]{:S(2)}, u32[]{:S(2)}) %collective-permute-start.11) | collective-permute-done | bytes 147488 | tf_op jit(solution)/shard_map/ppermute | solution.py:40
  79.7 2.1 %join.3 = bf16[144,512]{1,0:T(8,128)(2,1)} custom-call(bf16[144,512]{1,0:T(8,128)(2,1)} %get-tuple-element.26.refs_0_, bf16[144,512]{1,0:T(8,128)(2,1)} %copy-done.6), custom_call_target="tpu_custom_call" | custom-call | flops 1048576 | bytes 1048576 | tf_op jit(solution)/shard_map/join/pallas_call | solution.py:257
  82.6 2.2 %join.4 = bf16[144,512]{1,0:T(8,128)(2,1)} custom-call(bf16[144,512]{1,0:T(8,128)(2,1)} %get-tuple-element.28.refs_0_, bf16[288,512]{1,0:T(8,128)(2,1)} %copy-done.1, bf16[288,512]{1,0:T(8,128)(2,1)} %copy-done), custom_call_target="tpu_custom_call" | custom-call | flops 1048576 | bytes 1048576 | tf_op jit(solution)/shard_map/join/pallas_call | solution.py:257
  84.9 3.8 %collective-permute-done.12.refs_3_ = bf16[144,512]{1,0:T(8,128)(2,1)S(1)} collective-permute-done((bf16[144,512]{1,0:T(8,128)(2,1)}, bf16[144,512]{1,0:T(8,128)(2,1)S(1)}, u32[]{:S(2)}, u32[]{:S(2)}) %collective-permute-start.12) | collective-permute-done | bytes 147488 | tf_op jit(solution)/shard_map/ppermute | solution.py:40
  88.6 1.6 %collective-permute-done.13.refs_4_ = bf16[144,512]{1,0:T(8,128)(2,1)S(1)} collective-permute-done((bf16[144,512]{1,0:T(8,128)(2,1)}, bf16[144,512]{1,0:T(8,128)(2,1)S(1)}, u32[]{:S(2)}, u32[]{:S(2)}) %collective-permute-start.13) | collective-permute-done | bytes 147488 | tf_op jit(solution)/shard_map/ppermute | solution.py:40
  90.9 2.5 %join.5 = bf16[128,512]{1,0:T(8,128)(2,1)} custom-call(bf16[144,512]{1,0:T(8,128)(2,1)} %get-tuple-element.21.refs_0_, bf16[288,512]{1,0:T(8,128)(2,1)} %copy-done.1, bf16[288,512]{1,0:T(8,128)(2,1)} %copy-done, bf16[144,512]{1,0:T(8,128)(2,1)} %copy-done.4, bf16[144,512]{1,0:T(8,128)(2,1)} %copy-done.5), custom_call_target="tpu_custom_call" | custom-call | flops 1048576 | bytes 1048576 | tf_op jit(solution)/shard_map/join/pallas_call | solution.py:257
  93.4 1.5 %fusion.1 = (bf16[64,512]{1,0:T(8,128)(2,1)S(1)}, bf16[64,512]{1,0:T(8,128)(2,1)}) fusion(bf16[128,512]{1,0:T(8,128)(2,1)} %join.5), kind=kLoop, calls=%fused_computation.12 | loop fusion | bytes 262144 | tf_op jit(solution)/shard_map/slice | solution.py:348
  96.8 3.8 %project.5 = bf16[128,896]{1,0:T(8,128)(2,1)} custom-call(s32[9]{0:T(128)} %stack.54.where_ref, bf16[64,512]{1,0:T(8,128)(2,1)} %get-tuple-element.30.mine_ref, bf16[64,512]{1,0:T(8,128)(2,1)} %copy-done.2, bf16[1024,7168]{1,0:T(8,128)(2,1)} %low_ref.7, bf16[1024,7168]{1,0:T(8,128)(2,1)} %low_ref.7), custom_call_target="tpu_custom_call" | custom-call | flops 939524096 | bytes 4194304 | tf_op jit(solution)/shard_map/project/pallas_call | solution.py:281
  100.6 1.5 %collective-permute-start.15 = (bf16[128,896]{1,0:T(8,128)(2,1)}, bf16[128,896]{1,0:T(8,128)(2,1)S(1)}, u32[]{:S(2)}, u32[]{:S(2)}) collective-permute-start(bf16[128,896]{1,0:T(8,128)(2,1)} %project.5), channel_id=1, source_target_pairs={{0,1},{1,2},{2,3},{3,0},{4,5},{5,6},{6,7},{7,4},{8,9},{9,10},{10,1... | collective-permute-start | bytes 688136 | tf_op jit(solution)/shard_map/ppermute | solution.py:44
  102.1 3.8 %project.6 = bf16[128,896]{1,0:T(8,128)(2,1)} custom-call(s32[9]{0:T(128)} %stack.54.where_ref, bf16[64,512]{1,0:T(8,128)(2,1)} %get-tuple-element.30.mine_ref, bf16[64,512]{1,0:T(8,128)(2,1)} %copy-done.2, bf16[1024,7168]{1,0:T(8,128)(2,1)} %low_ref.7, bf16[1024,7168]{1,0:T(8,128)(2,1)} %low_ref.7), custom_call_target="tpu_custom_call" | custom-call | flops 939524096 | bytes 4194304 | tf_op jit(solution)/shard_map/project/pallas_call | solution.py:281
  105.9 2.7 %collective-permute-start.16 = (bf16[128,896]{1,0:T(8,128)(2,1)}, bf16[128,896]{1,0:T(8,128)(2,1)S(1)}, u32[]{:S(2)}, u32[]{:S(2)}) collective-permute-start(bf16[128,896]{1,0:T(8,128)(2,1)} %project.6), channel_id=1, source_target_pairs={{0,2},{1,3},{2,0},{3,1},{4,6},{5,7},{6,4},{7,5},{8,10},{9,11},{10,... | collective-permute-start | bytes 688136 | tf_op jit(solution)/shard_map/ppermute | solution.py:44
  108.7 3.8 %project.7 = bf16[128,896]{1,0:T(8,128)(2,1)} custom-call(s32[9]{0:T(128)} %stack.54.where_ref, bf16[64,512]{1,0:T(8,128)(2,1)} %get-tuple-element.30.mine_ref, bf16[64,512]{1,0:T(8,128)(2,1)} %copy-done.2, bf16[1024,7168]{1,0:T(8,128)(2,1)} %low_ref.7, bf16[1024,7168]{1,0:T(8,128)(2,1)} %low_ref.7), custom_call_target="tpu_custom_call" | custom-call | flops 939524096 | bytes 4194304 | tf_op jit(solution)/shard_map/project/pallas_call | solution.py:281
  113.9 3.8 %project.4 = bf16[128,896]{1,0:T(8,128)(2,1)} custom-call(s32[9]{0:T(128)} %stack.54.where_ref, bf16[64,512]{1,0:T(8,128)(2,1)} %get-tuple-element.30.mine_ref, bf16[64,512]{1,0:T(8,128)(2,1)} %copy-done.2, bf16[1024,7168]{1,0:T(8,128)(2,1)} %low_ref.7, bf16[1024,7168]{1,0:T(8,128)(2,1)} %low_ref.7), custom_call_target="tpu_custom_call" | custom-call | flops 939524096 | bytes 4194304 | tf_op jit(solution)/shard_map/project/pallas_call | solution.py:281
  117.8 2.0 %collective-permute-done.17 = bf16[128,896]{1,0:T(8,128)(2,1)S(1)} collective-permute-done((bf16[128,896]{1,0:T(8,128)(2,1)}, bf16[128,896]{1,0:T(8,128)(2,1)S(1)}, u32[]{:S(2)}, u32[]{:S(2)}) %collective-permute-start.17) | collective-permute-done | bytes 229408 | tf_op jit(solution)/shard_map/ppermute | solution.py:44
  120.9 3.7 %collective-permute-start.18 = (bf16[64,896]{1,0:T(8,128)(2,1)S(1)}, bf16[64,896]{1,0:T(8,128)(2,1)S(1)}, u32[]{:S(2)}, u32[]{:S(2)}) collective-permute-start(bf16[64,896]{1,0:T(8,128)(2,1)S(1)} %slice.25), channel_id=1, source_target_pairs={{0,4},{1,5},{2,6},{3,7},{4,0},{5,1},{6,2},{7,3},{8,12},{9,13},{10,... | collective-permute-start | bytes 344072 | tf_op jit(solution)/shard_map/ppermute | solution.py:44
  124.6 2.8 %collective-permute-done.18 = bf16[64,896]{1,0:T(8,128)(2,1)S(1)} collective-permute-done((bf16[64,896]{1,0:T(8,128)(2,1)S(1)}, bf16[64,896]{1,0:T(8,128)(2,1)S(1)}, u32[]{:S(2)}, u32[]{:S(2)}) %collective-permute-start.18) | collective-permute-done | bytes 114720 | tf_op jit(solution)/shard_map/ppermute | solution.py:44
  (71 shorter events, 18.9 us)
Async XLA Ops:
  0.0 20.4 %collective-permute-start.4 = (bf16[576,1024]{1,0:T(8,128)(2,1)}, bf16[576,1024]{1,0:T(8,128)(2,1)S(1)}, u32[]{:S(2)}, u32[]{:S(2)}) collective-permute-start(bf16[576,1024]{1,0:T(8,128)(2,1)} %cache_ref.1), channel_id=1, source_target_pairs={{0,8},{8,0},{16,24},{24,16},{32,40},{40,32},{48,56},{56,48},{64,72... | collective-permute-start | bytes 3538952 | tf_op jit(solution)/shard_map/ppermute | solution.py:40
  1.7 1.5 %collective-permute-start = (bf16[64,768]{1,0:T(8,128)(2,1)S(1)}, bf16[64,768]{1,0:T(8,128)(2,1)S(1)}, u32[]{:S(2)}, u32[]{:S(2)}) collective-permute-start(bf16[64,768]{1,0:T(8,128)(2,1)S(1)} %pad_maximum_fusion.3), channel_id=1, source_target_pairs={{0,8},{8,0},{16,24},{24,16},{32,40},{40,32},{48,56},{56,48},{64,72... | collective-permute-start | bytes 294920 | tf_op jit(solution)/shard_map/ppermute | solution.py:40
  3.2 14.8 %copy-start.3 = (bf16[128,768]{1,0:T(8,128)(2,1)}, bf16[128,768]{1,0:T(8,128)(2,1)S(1)}, u32[]{:S(2)}) copy-start(bf16[128,768]{1,0:T(8,128)(2,1)S(1)} %pad_maximum_fusion.2.refs_0_.refs_1_) | copy-start | bytes 589828
  3.2 14.8 %collective-permute-start.1 = (bf16[128,768]{1,0:T(8,128)(2,1)S(1)}, bf16[128,768]{1,0:T(8,128)(2,1)S(1)}, u32[]{:S(2)}, u32[]{:S(2)}) collective-permute-start(bf16[128,768]{1,0:T(8,128)(2,1)S(1)} %pad_maximum_fusion.2.refs_0_.refs_1_), channel_id=1, source_target_pairs={{0,16},{8,24},{16,0},{24,8},{32,48},{40,56},{48,32},{56,40},{64,80... | collective-permute-start | bytes 589832 | tf_op jit(solution)/shard_map/ppermute | solution.py:40
  5.3 15.1 %collective-permute-start.7 = (bf16[128,768]{1,0:T(8,128)(2,1)S(1)}, bf16[128,768]{1,0:T(8,128)(2,1)S(1)}, u32[]{:S(2)}, u32[]{:S(2)}) collective-permute-start(bf16[128,768]{1,0:T(8,128)(2,1)S(1)} %pad_maximum_fusion.2.refs_0_.refs_1_), channel_id=1, source_target_pairs={{0,64},{8,72},{16,80},{24,88},{32,96},{40,104},{48,112},{56,120},{... | collective-permute-start | bytes 589832 | tf_op jit(solution)/shard_map/ppermute | solution.py:40
  10.4 16.7 %collective-permute-start.2 = (bf16[128,768]{1,0:T(8,128)(2,1)S(1)}, bf16[128,768]{1,0:T(8,128)(2,1)S(1)}, u32[]{:S(2)}, u32[]{:S(2)}) collective-permute-start(bf16[128,768]{1,0:T(8,128)(2,1)S(1)} %pad_maximum_fusion.2.refs_0_.refs_1_), channel_id=1, source_target_pairs={{0,96},{8,104},{16,112},{24,120},{32,0},{40,8},{48,16},{56,24},{64... | collective-permute-start | bytes 589832 | tf_op jit(solution)/shard_map/ppermute | solution.py:40
  11.5 15.7 %collective-permute-start.3 = (bf16[128,768]{1,0:T(8,128)(2,1)S(1)}, bf16[128,768]{1,0:T(8,128)(2,1)S(1)}, u32[]{:S(2)}, u32[]{:S(2)}) collective-permute-start(bf16[128,768]{1,0:T(8,128)(2,1)S(1)} %pad_maximum_fusion.2.refs_0_.refs_1_), channel_id=1, source_target_pairs={{0,32},{8,40},{16,48},{24,56},{32,64},{40,72},{48,80},{56,88},{64,... | collective-permute-start | bytes 589832 | tf_op jit(solution)/shard_map/ppermute | solution.py:40
  18.1 9.1 %copy-start.11 = (bf16[128,768]{1,0:T(8,128)(2,1)}, bf16[128,768]{1,0:T(8,128)(2,1)S(1)}, u32[]{:S(2)}) copy-start(bf16[128,768]{1,0:T(8,128)(2,1)S(1)} %collective-permute-done.1.refs_2_.refs_3_) | copy-start | bytes 589828
  18.1 29.9 %collective-permute-start.5 = (bf16[128,768]{1,0:T(8,128)(2,1)S(1)}, bf16[128,768]{1,0:T(8,128)(2,1)S(1)}, u32[]{:S(2)}, u32[]{:S(2)}) collective-permute-start(bf16[128,768]{1,0:T(8,128)(2,1)S(1)} %collective-permute-done.1.refs_2_.refs_3_), channel_id=1, source_target_pairs={{0,96},{8,104},{16,112},{24,120},{32,0},{40,8},{48,16},{56,24},{64... | collective-permute-start | bytes 589832 | tf_op jit(solution)/shard_map/ppermute | solution.py:40
  20.4 27.5 %copy-start.10 = (bf16[128,768]{1,0:T(8,128)(2,1)}, bf16[128,768]{1,0:T(8,128)(2,1)S(1)}, u32[]{:S(2)}) copy-start(bf16[128,768]{1,0:T(8,128)(2,1)S(1)} %collective-permute-done.7.refs_4_.refs_5_) | copy-start | bytes 589828
  20.4 27.6 %collective-permute-start.6 = (bf16[128,768]{1,0:T(8,128)(2,1)S(1)}, bf16[128,768]{1,0:T(8,128)(2,1)S(1)}, u32[]{:S(2)}, u32[]{:S(2)}) collective-permute-start(bf16[128,768]{1,0:T(8,128)(2,1)S(1)} %collective-permute-done.1.refs_2_.refs_3_), channel_id=1, source_target_pairs={{0,32},{8,40},{16,48},{24,56},{32,64},{40,72},{48,80},{56,88},{64,... | collective-permute-start | bytes 589832 | tf_op jit(solution)/shard_map/ppermute | solution.py:40
  20.4 27.6 %collective-permute-start.8 = (bf16[128,768]{1,0:T(8,128)(2,1)S(1)}, bf16[128,768]{1,0:T(8,128)(2,1)S(1)}, u32[]{:S(2)}, u32[]{:S(2)}) collective-permute-start(bf16[128,768]{1,0:T(8,128)(2,1)S(1)} %collective-permute-done.7.refs_4_.refs_5_), channel_id=1, source_target_pairs={{0,16},{8,24},{16,0},{24,8},{32,48},{40,56},{48,32},{56,40},{64,80... | collective-permute-start | bytes 589832 | tf_op jit(solution)/shard_map/ppermute | solution.py:40
  47.9 21.7 %copy-start.8 = (bf16[144,512]{1,0:T(8,128)(2,1)S(1)}, bf16[144,512]{1,0:T(8,128)(2,1)}, u32[]{:S(2)}) copy-start(bf16[144,512]{1,0:T(8,128)(2,1)} %get-tuple-element.24) | copy-start | bytes 442372
  47.9 22.7 %copy-start.7 = (bf16[144,512]{1,0:T(8,128)(2,1)S(1)}, bf16[144,512]{1,0:T(8,128)(2,1)}, u32[]{:S(2)}) copy-start(bf16[144,512]{1,0:T(8,128)(2,1)} %get-tuple-element.22) | copy-start | bytes 442372
  70.6 11.2 %collective-permute-start.10 = (bf16[288,512]{1,0:T(8,128)(2,1)S(1)}, bf16[288,512]{1,0:T(8,128)(2,1)S(1)}, u32[]{:S(2)}, u32[]{:S(2)}) collective-permute-start(bf16[288,512]{1,0:T(8,128)(2,1)S(1)} %pad_maximum_fusion.1), channel_id=1, source_target_pairs={{0,96},{8,104},{16,112},{24,120},{32,0},{40,8},{48,16},{56,24},{64... | collective-permute-start | bytes 884744 | tf_op jit(solution)/shard_map/ppermute | solution.py:40
  71.6 10.2 %collective-permute-start.9 = (bf16[288,512]{1,0:T(8,128)(2,1)S(1)}, bf16[288,512]{1,0:T(8,128)(2,1)S(1)}, u32[]{:S(2)}, u32[]{:S(2)}) collective-permute-start(bf16[288,512]{1,0:T(8,128)(2,1)S(1)} %pad_maximum_fusion), channel_id=1, source_target_pairs={{0,32},{8,40},{16,48},{24,56},{32,64},{40,72},{48,80},{56,88},{64,... | collective-permute-start | bytes 884744 | tf_op jit(solution)/shard_map/ppermute | solution.py:40
  73.7 5.4 %collective-permute-start.11 = (bf16[144,512]{1,0:T(8,128)(2,1)}, bf16[144,512]{1,0:T(8,128)(2,1)S(1)}, u32[]{:S(2)}, u32[]{:S(2)}) collective-permute-start(bf16[144,512]{1,0:T(8,128)(2,1)} %get-tuple-element.27), channel_id=1, source_target_pairs={{0,16},{8,24},{16,0},{24,8},{32,48},{40,56},{48,32},{56,40},{64,80... | collective-permute-start | bytes 442376 | tf_op jit(solution)/shard_map/ppermute | solution.py:40
  81.8 6.9 %collective-permute-start.12 = (bf16[144,512]{1,0:T(8,128)(2,1)}, bf16[144,512]{1,0:T(8,128)(2,1)S(1)}, u32[]{:S(2)}, u32[]{:S(2)}) collective-permute-start(bf16[144,512]{1,0:T(8,128)(2,1)} %join.3), channel_id=1, source_target_pairs={{0,64},{8,72},{16,80},{24,88},{32,96},{40,104},{48,112},{56,120},{... | collective-permute-start | bytes 442376 | tf_op jit(solution)/shard_map/ppermute | solution.py:40
  84.9 5.4 %collective-permute-start.13 = (bf16[144,512]{1,0:T(8,128)(2,1)}, bf16[144,512]{1,0:T(8,128)(2,1)S(1)}, u32[]{:S(2)}, u32[]{:S(2)}) collective-permute-start(bf16[144,512]{1,0:T(8,128)(2,1)} %join.4), channel_id=1, source_target_pairs={{0,16},{8,24},{16,0},{24,8},{32,48},{40,56},{48,32},{56,40},{64,80... | collective-permute-start | bytes 442376 | tf_op jit(solution)/shard_map/ppermute | solution.py:40
  94.9 1.3 collective-permute-start.14
  100.6 17.2 %collective-permute-start.15 = (bf16[128,896]{1,0:T(8,128)(2,1)}, bf16[128,896]{1,0:T(8,128)(2,1)S(1)}, u32[]{:S(2)}, u32[]{:S(2)}) collective-permute-start(bf16[128,896]{1,0:T(8,128)(2,1)} %project.5), channel_id=1, source_target_pairs={{0,1},{1,2},{2,3},{3,0},{4,5},{5,6},{6,7},{7,4},{8,9},{9,10},{10,1... | collective-permute-start | bytes 688136 | tf_op jit(solution)/shard_map/ppermute | solution.py:44
  105.9 11.8 %collective-permute-start.16 = (bf16[128,896]{1,0:T(8,128)(2,1)}, bf16[128,896]{1,0:T(8,128)(2,1)S(1)}, u32[]{:S(2)}, u32[]{:S(2)}) collective-permute-start(bf16[128,896]{1,0:T(8,128)(2,1)} %project.6), channel_id=1, source_target_pairs={{0,2},{1,3},{2,0},{3,1},{4,6},{5,7},{6,4},{7,5},{8,10},{9,11},{10,... | collective-permute-start | bytes 688136 | tf_op jit(solution)/shard_map/ppermute | solution.py:44
  112.5 7.3 %collective-permute-start.17 = (bf16[128,896]{1,0:T(8,128)(2,1)}, bf16[128,896]{1,0:T(8,128)(2,1)S(1)}, u32[]{:S(2)}, u32[]{:S(2)}) collective-permute-start(bf16[128,896]{1,0:T(8,128)(2,1)} %project.7), channel_id=1, source_target_pairs={{0,3},{1,0},{2,1},{3,2},{4,7},{5,4},{6,5},{7,6},{8,11},{9,8},{10,9... | collective-permute-start | bytes 688136 | tf_op jit(solution)/shard_map/ppermute | solution.py:44
  120.9 6.4 %collective-permute-start.18 = (bf16[64,896]{1,0:T(8,128)(2,1)S(1)}, bf16[64,896]{1,0:T(8,128)(2,1)S(1)}, u32[]{:S(2)}, u32[]{:S(2)}) collective-permute-start(bf16[64,896]{1,0:T(8,128)(2,1)S(1)} %slice.25), channel_id=1, source_target_pairs={{0,4},{1,5},{2,6},{3,7},{4,0},{5,1},{6,2},{7,3},{8,12},{9,13},{10,... | collective-permute-start | bytes 344072 | tf_op jit(solution)/shard_map/ppermute | solution.py:44
  (12 other events, 9.8 us)

commit v2 on v0

v2 whole, which is shorter than its diff:
```python
import functools
import math

import jax
import jax.numpy as jnp
from jax import lax
from jax.experimental import pallas as pl
from jax.experimental.pallas import tpu as pltpu
from jax.sharding import PartitionSpec as P

LATENT = 512
ROPE = 64
NOPE = 128
VDIM = 128
HALF = 4
SLOTS = 1024
TOK = 64
PIECE = 2 * TOK
ROWS = PIECE + 16
STEP = 256

F32 = jnp.float32
BF16 = jnp.bfloat16
MASKED = -1e30
SCALE2 = (NOPE + ROPE) ** (-0.5) * (0.1 * math.log(32.0) + 1.0) ** 2 * math.log2(math.e)
VMEM = 20 << 20

CORE = [(i, i ^ 1) for i in range(16)]
ZLO = [(i, i ^ 2) for i in range(16)]
YP = [(i, (i + 4) % 16) for i in range(16)]
YM = [(i, (i - 4) % 16) for i in range(16)]
Y2 = [(i, (i + 8) % 16) for i in range(16)]
DIAGP = [(i, (i + 4) % 16 ^ 2) for i in range(16)]
DIAGM = [(i, (i - 4) % 16 ^ 2) for i in range(16)]
DIAG2 = [(i, (i + 8) % 16 ^ 2) for i in range(16)]
XP = [(i, (i // 4) * 4 + (i + 1) % 4) for i in range(8)]
XM = [(i, (i // 4) * 4 + (i - 1) % 4) for i in range(8)]
X2 = [(i, (i // 4) * 4 + (i + 2) % 4) for i in range(8)]
ZHI = [(i, i ^ 4) for i in range(8)]


def to_ctx(array, pairs):
    return lax.ppermute(array, "ctx", pairs)


def to_head(array, pairs):
    return lax.ppermute(array, "head", pairs)


def vmem(n):
    return [pl.BlockSpec(memory_space=pltpu.VMEM)] * n


SMEM = pl.BlockSpec(memory_space=pltpu.SMEM)
HBM = pl.BlockSpec(memory_space=pltpu.HBM)


def lanes(index, width=128):
    return pl.ds(pl.multiple_of(index * width, 128), width)


def split_kernel(nope_ref, rope_ref, keep_ref, give_ref, sems):
    core = lax.axis_index("ctx") & 1
    copies = []
    for ref, side in ((give_ref, 1 - core), (keep_ref, core)):
        for source, target in (
            (nope_ref.at[:, lanes(side, HALF * NOPE)], ref.at[:, : HALF * NOPE]),
            (rope_ref.at[:, lanes(side, HALF * ROPE)], ref.at[:, HALF * NOPE :]),
        ):
            copies.append(pltpu.make_async_copy(source, target, sems.at[len(copies)]))
    for copy in copies:
        copy.start()
    for copy in copies:
        copy.wait()


def split_queries(q_nope, q_rope):
    shape = jax.ShapeDtypeStruct((TOK, HALF * (NOPE + ROPE)), BF16)
    return pl.pallas_call(
        split_kernel,
        in_specs=[HBM] * 2,
        out_specs=vmem(2),
        out_shape=[shape, shape],
        scratch_shapes=[pltpu.SemaphoreType.DMA((4,))],
        compiler_params=pltpu.CompilerParams(vmem_limit_bytes=4 << 20),
        name="split_queries",
    )(q_nope, q_rope)


def form(cache, uk, uv, key_ref, val_ref):
    slots = cache.shape[1]
    latent = cache[:LATENT]
    rope = cache[LATENT:]
    blank = jnp.zeros((ROPE, slots), BF16)
    ones = jnp.ones((slots, VDIM), BF16)
    keys = jnp.dot(uk[...].reshape(HALF * NOPE, LATENT), latent, preferred_element_type=F32).astype(BF16)
    up = jnp.concatenate([uv[h] for h in range(HALF)], axis=1)
    vals = jnp.dot(latent.T, up, preferred_element_type=F32).astype(BF16)
    for h in range(HALF):
        key_ref[h, :NOPE] = keys[h * NOPE : (h + 1) * NOPE]
        key_ref[h, NOPE : NOPE + ROPE] = rope if h % 2 == 0 else blank
        key_ref[h, NOPE + ROPE :] = blank if h % 2 == 0 else rope
        val_ref[h, :, :VDIM] = vals[:, h * VDIM : (h + 1) * VDIM]
        val_ref[h, :, VDIM:] = ones


def near_kernel(cache_ref, other_ref, uk_ref, uv_ref, key0, val0, key1, val1, uk, uv, own, sems):
    heads = pl.ds((lax.axis_index("ctx") & 1) * HALF, HALF)
    copies = [
        pltpu.make_async_copy(source, target, sems.at[i])
        for i, (source, target) in enumerate(((uk_ref.at[heads], uk), (uv_ref.at[heads], uv), (cache_ref, own)))
    ]
    for copy in copies:
        copy.start()
    copies[0].wait()
    copies[1].wait()
    form(other_ref, uk, uv, key1, val1)
    copies[2].wait()
    form(own, uk, uv, key0, val0)


def kv_shapes(slots):
    return [jax.ShapeDtypeStruct((HALF, 256, slots), BF16), jax.ShapeDtypeStruct((HALF, slots, 256), BF16)]


def kv_cost(slots):
    return pl.CostEstimate(flops=4 * HALF * NOPE * LATENT * slots, bytes_accessed=4 << 20, transcendentals=0)


def near_keys_values(cache, other, w_uk, w_uv):
    uk = jax.ShapeDtypeStruct((HALF, NOPE, LATENT), BF16)
    uv = jax.ShapeDtypeStruct((HALF, LATENT, VDIM), BF16)
    return pl.pallas_call(
        near_kernel,
        in_specs=[HBM] + vmem(1) + [HBM] * 2,
        out_specs=vmem(6),
        out_shape=kv_shapes(SLOTS) * 2 + [uk, uv],
        scratch_shapes=[pltpu.VMEM((LATENT + ROPE, SLOTS), BF16), pltpu.SemaphoreType.DMA((3,))],
        cost_estimate=kv_cost(2 * SLOTS),
        compiler_params=pltpu.CompilerParams(vmem_limit_bytes=12 << 20),
        name="near_keys_values",
    )(cache, other, w_uk, w_uv)


def far_keys_values(cache, uk, uv):
    slots = cache.shape[1]
    return pl.pallas_call(
        form,
        in_specs=vmem(3),
        out_specs=vmem(2),
        out_shape=kv_shapes(slots),
        cost_estimate=kv_cost(slots),
        compiler_params=pltpu.CompilerParams(vmem_limit_bytes=12 << 20),
        name="far_keys_values",
    )(cache, uk, uv)


def split3(x):
    a = x.astype(BF16)
    r = x - a.astype(F32)
    b = r.astype(BF16)
    return a, b, (r - b.astype(F32)).astype(BF16)


def store_piece(o_ref, h, out, lse):
    o_ref[:PIECE, lanes(h)] = out.astype(BF16)
    row = lse.T[:1]
    a, b, c = split3(row)
    index = lax.broadcasted_iota(jnp.int32, (16, PIECE), 0)
    spread = lambda v: jnp.broadcast_to(v.astype(F32), (16, PIECE))
    pick = jnp.where(index == 0, spread(a), jnp.where(index == 1, spread(b), jnp.where(index == 2, spread(c), 0.0)))
    o_ref[PIECE:, lanes(h)] = pick.astype(BF16)


def attention_kernel(places, carried, last, bases, spot_ref, *refs):
    n = len(places)
    rows = n * PIECE
    m = n + 2 * len(bases)
    q_refs, kv_refs, refs = refs[:n], refs[n:m], refs[m:]
    carry, o_refs = (refs[:2], refs[2:]) if carried else (None, refs)
    start = spot_ref[0]
    core = spot_ref[1]
    slots = kv_refs[0].shape[2]
    blocks = [(kv_refs[2 * i], kv_refs[2 * i + 1], spot_ref[b] * SLOTS) for i, b in enumerate(bases)]
    first = functools.reduce(jnp.minimum, [b for _, _, b in blocks])
    final = functools.reduce(jnp.maximum, [b for _, _, b in blocks]) + slots - 1

    def queries(h):
        tall = lambda lane: jnp.concatenate([q[:, lane] for q in q_refs], axis=0)
        return jnp.concatenate([tall(lanes(h)), tall(lanes(HALF + h // 2))], axis=1)

    def positions():
        place = lax.broadcasted_iota(jnp.int32, (PIECE, 1), 0)
        mine = place < TOK
        inner = jnp.where(mine, place, place - TOK)
        side = jnp.where(mine, core, 1 - core)
        local = start + inner + side * TOK
        return jnp.concatenate([local + spot_ref[i] * PIECE for i in places], axis=0)

    def scores(q, k, h, c):
        return jnp.dot(q, k[h, :, c * STEP : (c + 1) * STEP], preferred_element_type=F32) * SCALE2

    def seen(pos, base, c):
        key = base + c * STEP + lax.broadcasted_iota(jnp.int32, (1, STEP), 1)
        return key <= pos

    def finish(h, acc, shift):
        if carried:
            old, old_shift = carry[0][h], carry[1][h]
            shift = jnp.where(acc[:, VDIM:] == 0.0, MASKED, shift)
            best = jnp.maximum(shift, old_shift)
            new_part, old_part = jnp.exp2(shift - best), jnp.exp2(old_shift - best)
            out = acc[:, :VDIM] * new_part + old[:, :VDIM] * old_part
            total = acc[:, VDIM:] * new_part + old[:, VDIM:] * old_part
            shift = best
        else:
            out, total = acc[:, :VDIM], acc[:, VDIM:]
            shift = jnp.where(total == 0.0, MASKED, shift)
        if not last:
            o_refs[0][h, :, :VDIM] = out
            o_refs[0][h, :, VDIM:] = total
            o_refs[1][h] = shift
            return
        none = total == 0.0
        safe = jnp.where(none, 1.0, total)
        out = out / safe
        lse = jnp.where(none, MASKED, jnp.log2(safe) + shift)
        for i in range(n):
            store_piece(o_refs[i], h, out[i * PIECE : (i + 1) * PIECE], lse[i * PIECE : (i + 1) * PIECE])

    def quick(masked):
        pos = positions() if masked else None

        def one(h, fine):
            q = queries(h)
            acc = None
            for k, v, base in blocks:
                for c in range(slots // STEP):
                    p = jnp.exp2(scores(q, k, h, c))
                    if masked:
                        p = jnp.where(seen(pos, base, c), p, 0.0)
                    term = jnp.dot(p.astype(BF16), v[h, c * STEP : (c + 1) * STEP], preferred_element_type=F32)
                    acc = term if acc is None else acc + term
            total = acc[:, VDIM:]
            good = (total > 1e-27) & (total < 1e30)
            if masked:
                good = good | (pos < first)
            finish(h, acc, 0.0)
            return jnp.minimum(fine, good.astype(F32).reshape(rows // 8, 8, VDIM).min(axis=0))

        return jnp.min(lax.fori_loop(0, HALF, one, jnp.ones((8, VDIM), F32)))

    def careful():
        pos = positions()

        def one(h, _):
            q = queries(h)
            best = jnp.full((rows, 1), MASKED, F32)
            for k, v, base in blocks:
                for c in range(slots // STEP):
                    s = jnp.where(seen(pos, base, c), scores(q, k, h, c), MASKED)
                    best = jnp.maximum(best, jnp.max(s, axis=1, keepdims=True))
            acc = jnp.zeros((rows, 2 * VDIM), F32)
            for k, v, base in blocks:
                for c in range(slots // STEP):
                    p = jnp.where(seen(pos, base, c), jnp.exp2(scores(q, k, h, c) - best), 0.0)
                    acc += jnp.dot(p.astype(BF16), v[h, c * STEP : (c + 1) * STEP], preferred_element_type=F32)
            finish(h, acc, best)
            return 0

        lax.fori_loop(0, HALF, one, 0)

    everything = final <= start
    nothing = first > start + 16 * TOK - 1

    @pl.when(nothing)
    def _():
        def one(h, _):
            finish(h, jnp.zeros((rows, 2 * VDIM), F32), MASKED)
            return 0

        lax.fori_loop(0, HALF, one, 0)

    @pl.when(everything)
    def _():
        good = quick(False)

        @pl.when(good < 0.5)
        def _():
            careful()

    @pl.when(jnp.logical_not(everything | nothing))
    def _():
        good = quick(True)

        @pl.when(good < 0.5)
        def _():
            careful()


def attention(spot, places, pieces, keys_vals, bases, carry=(), last=False):
    n = len(pieces)
    slots = keys_vals[0].shape[2]
    if last:
        shapes = [jax.ShapeDtypeStruct((ROWS, HALF * VDIM), BF16)] * n
    else:
        shapes = [
            jax.ShapeDtypeStruct((HALF, n * PIECE, 2 * VDIM), F32),
            jax.ShapeDtypeStruct((HALF, n * PIECE, VDIM), F32),
        ]
    return pl.pallas_call(
        functools.partial(attention_kernel, places, len(carry) > 0, last, bases),
        in_specs=[SMEM] + vmem(n + len(keys_vals) + len(carry)),
        out_specs=vmem(len(shapes)),
        out_shape=shapes,
        cost_estimate=pl.CostEstimate(
            flops=len(keys_vals) * HALF * n * PIECE * slots * 512,
            bytes_accessed=4 << 20,
            transcendentals=HALF * n * PIECE * 2 * slots,
        ),
        compiler_params=pltpu.CompilerParams(vmem_limit_bytes=VMEM),
        name="attention",
    )(spot, *pieces, *keys_vals, *carry)


def join_kernel(n, *refs):
    pieces, o_ref = refs[:n], refs[n]
    logs = [sum(p[PIECE + j : PIECE + j + 1].astype(F32) for j in range(3)) for p in pieces]
    best = functools.reduce(jnp.maximum, logs)
    shares = [jnp.exp2(v - best) for v in logs]
    total = sum(shares)
    stack = jnp.concatenate([s / total for s in shares] + [jnp.zeros((-n % 8, HALF * VDIM), F32)][: -n % 8], axis=0)
    for h in range(HALF):
        lane = slice(h * VDIM, (h + 1) * VDIM)
        cols = stack[:, lane].T
        out = sum(p[:PIECE, lane].astype(F32) * cols[:, i : i + 1] for i, p in enumerate(pieces))
        o_ref[:, lane] = out.astype(BF16)


def join(pieces):
    n = len(pieces)
    return pl.pallas_call(
        functools.partial(join_kernel, n),
        in_specs=vmem(n),
        out_specs=vmem(1)[0],
        out_shape=jax.ShapeDtypeStruct((PIECE, HALF * VDIM), BF16),
        cost_estimate=pl.CostEstimate(flops=1 << 20, bytes_accessed=1 << 20, transcendentals=4096),
        compiler_params=pltpu.CompilerParams(vmem_limit_bytes=8 << 20),
        name="join",
    )(*pieces)


def project_kernel(step, spot_ref, mine_ref, theirs_ref, w_ref, o_ref):
    core, x, zhi = spot_ref[1], spot_ref[3], spot_ref[4]
    wide = o_ref.shape[1]
    rows = HALF * VDIM
    top = pl.ds(pl.multiple_of(core * rows, rows), rows)
    low = pl.ds(pl.multiple_of((1 - core) * rows, rows), rows)
    for j, side in enumerate((zhi, 1 - zhi)):
        column = lanes(side * 4 + ((x + step) & 3), wide)
        acc = jnp.dot(mine_ref[:TOK], w_ref[top, column], preferred_element_type=F32)
        acc += jnp.dot(theirs_ref[...], w_ref[low, column], preferred_element_type=F32)
        o_ref[j * TOK : (j + 1) * TOK] = acc.astype(BF16)


def project(spot, mine, theirs, w_o, step):
    wide = w_o.shape[1] // 8
    return pl.pallas_call(
        functools.partial(project_kernel, step),
        in_specs=[SMEM] + vmem(3),
        out_specs=vmem(1)[0],
        out_shape=jax.ShapeDtypeStruct((2 * TOK, wide), BF16),
        cost_estimate=pl.CostEstimate(
            flops=2 * 2 * 256 * wide * 1024, bytes_accessed=4 << 20, transcendentals=0
        ),
        compiler_params=pltpu.CompilerParams(vmem_limit_bytes=12 << 20),
        name="project",
    )(spot, mine, theirs, w_o)


def on_device(q_nope, q_rope, w_uk, w_uv, w_o, latent_cache, group_start):
    ctx = lax.axis_index("ctx")
    head = lax.axis_index("head")
    chip = ctx >> 1
    place = lambda dy: (((chip >> 1) + dy) & 3) * 2 + (chip & 1)
    spot = jnp.stack(
        [group_start[0], ctx & 1, chip, head & 3, head >> 2]
        + [place(dy) for dy in range(4)]
        + [ctx ^ flip for flip in range(4)]
    ).astype(jnp.int32)
    U, PU, DU, MU = range(5, 9)
    OWN, CORES, ZNEAR, ZCORES = range(9, 13)
    z_cache = to_ctx(latent_cache, ZLO)
    cache_other = to_ctx(latent_cache, CORE)
    keep, give = split_queries(q_nope, q_rope)
    given = to_ctx(give, CORE)
    u = jnp.concatenate([keep, given], axis=0)
    d_u = to_ctx(u, Y2)
    p_u = to_ctx(u, YM)
    m_u = to_ctx(u, YP)

    places, pieces = (U, PU, DU, MU), (u, p_u, d_u, m_u)
    cache_other, u_ = lax.optimization_barrier((cache_other, u))
    *near, uk, uv = near_keys_values(latent_cache, cache_other, w_uk, w_uv)
    carry = attention(spot, places, pieces, near, (OWN, CORES))
    z_cache, carry = lax.optimization_barrier((z_cache, carry))
    zc_cache = to_ctx(z_cache, CORE)
    carry = attention(spot, places, pieces, far_keys_values(z_cache, uk, uv), (ZNEAR,), carry)
    zc_cache, carry = lax.optimization_barrier((zc_cache, carry))
    r_u, r_p, r_d, r_m = attention(
        spot, places, pieces, far_keys_values(zc_cache, uk, uv), (ZCORES,), carry, True
    )
    mine = join([r_u, to_ctx(r_d, Y2), to_ctx(r_p, YP), to_ctx(r_m, YM)])

    theirs = to_ctx(mine[TOK:], CORE)
    out2 = to_head(project(spot, mine, theirs, w_o, 2), X2)
    out1 = to_head(project(spot, mine, theirs, w_o, 1), XP)
    out3 = to_head(project(spot, mine, theirs, w_o, 3), XM)
    out0 = project(spot, mine, theirs, w_o, 0)
    total = out0.astype(F32) + out1.astype(F32) + out2.astype(F32) + out3.astype(F32)
    back = to_head(total[TOK:].astype(BF16), ZHI)
    return (total[:TOK] + back.astype(F32)).astype(BF16)


def solution(mesh):
    placed = (
        P("ctx", "head"),
        P("ctx", "head"),
        P("head", None, None),
        P("head", None, None),
        P("head", None),
        P(None, "ctx"),
        P(),
    )
    return jax.shard_map(
        on_device, mesh=mesh, in_specs=placed, out_specs=P("ctx", "head"), check_vma=False
    )
```

time: 303 us -> 91 us (0.30)
  the two profiles are of different devices: /device:TPU:0 before, /device:TPU:2 now
where the time goes in v2:
time: 91 us; the launch traced here: 89.4 us
  Pallas kernels  39 us (43%)
  waiting for transfers between devices  24.1 us (26%)
  starting transfers between devices  19.1 us (21%)
  local copies, waits for them, and re-layouts  5.61 us (6%)
    pallas_call x3, Pallas kernels, attention(): pl.pallas_call(functools.partial(attention_kernel, places, len(carry) > 0...  27.2 us
    ppermute x11, waiting for transfers between devices, to_ctx(): return lax.ppermute(array, 'ctx', pairs)  12.8 us
    ppermute x4, waiting for transfers between devices, to_head(): return lax.ppermute(array, 'head', pairs)  11.2 us
    ppermute x11, starting transfers between devices, to_ctx(): return lax.ppermute(array, 'ctx', pairs)  10.5 us
    ppermute x4, starting transfers between devices, to_head(): return lax.ppermute(array, 'head', pairs)  8.62 us
    unnamed x19, local copies, waits for them, and re-layouts  5.49 us
    pallas_call x4, Pallas kernels, project(): pl.pallas_call(functools.partial(project_kernel, step), in_specs=[SMEM] +...  5.11 us
    pallas_call x1, Pallas kernels, near_keys_values(): pl.pallas_call(near_kernel, in_specs=[HBM] + vmem(1) + [HBM] * 2, out_spe...  3.24 us
  transfers between devices with their start and end apart: 15, of which 10 were waited for; matrix products, arithmetic and copies ran while one was open for 0% of the time, Pallas kernels for 34%

profile of v2, /device:TPU:2, one launch (start us, length us, event | category | flops | bytes accessed | tf_op | source)
XLA Modules:
  0.0 89.4 jit_solution(15067752883570056340)
XLA Ops:
  0.0 1.9 %collective-permute-start.4 = (bf16[576,1024]{1,0:T(8,128)(2,1)}, bf16[576,1024]{1,0:T(8,128)(2,1)S(1)}, u32[]{:S(2)}, u32[]{:S(2)}) collective-permute-start(bf16[576,1024]{1,0:T(8,128)(2,1)} %cache_ref.1), channel_id=1, source_target_pairs={{0,16},{8,24},{16,0},{24,8},{32,48},{40,56},{48,32},{56,40},{64,80... | collective-permute-start | bytes 3538952 | tf_op jit(solution)/shard_map/ppermute | solution.py:43
  5.1 3.1 %collective-permute-start.1 = (bf16[128,768]{1,0:T(8,128)(2,1)S(1)}, bf16[128,768]{1,0:T(8,128)(2,1)S(1)}, u32[]{:S(2)}, u32[]{:S(2)}) collective-permute-start(bf16[128,768]{1,0:T(8,128)(2,1)S(1)} %constant_dynamic-update-slice_fusion.refs_0_), channel_id=1, source_target_pairs={{0,96},{8,104},{16,112},{24,120},{32,0},{40,8},{48,16},{56,24},{64... | collective-permute-start | bytes 589832 | tf_op jit(solution)/shard_map/ppermute | solution.py:43
  9.8 1.3 %copy-done.2 = bf16[576,1024]{1,0:T(8,128)(2,1)S(1)} copy-done((bf16[576,1024]{1,0:T(8,128)(2,1)S(1)}, bf16[576,1024]{1,0:T(8,128)(2,1)}, u32[]{:S(2)}) %copy-start.2) | copy-done | bytes 1179672
  13.6 3.2 %near_keys_values.1 = (bf16[4,256,1024]{2,1,0:T(8,128)(2,1)S(1)}, bf16[4,1024,256]{2,1,0:T(8,128)(2,1)S(1)}, bf16[4,256,1024]{2,1,0:T(8,128)(2,1)S(1)}, bf16[4,1...) custom-call(bf16[576,1024]{1,0:T(8,128)(2,1)S(1)} %copy-done.2, ...), custom_call_target="tpu_custom_call" | custom-call | flops 2147483648 | bytes 4194304 | tf_op jit(solution)/shard_map/near_keys_values/pallas_call | solution.py:133
  17.5 3.1 %collective-permute-done.3.refs_3_ = bf16[128,768]{1,0:T(8,128)(2,1)S(1)} collective-permute-done((bf16[128,768]{1,0:T(8,128)(2,1)S(1)}, bf16[128,768]{1,0:T(8,128)(2,1)S(1)}, u32[]{:S(2)}, u32[]{:S(2)}) %collective-permute-start.3) | collective-permute-done | bytes 196640 | tf_op jit(solution)/shard_map/ppermute | solution.py:43
  20.7 17.2 %attention.3 = (f32[4,512,256]{2,1,0:T(8,128)S(1)}, f32[4,512,128]{2,1,0:T(8,128)S(1)}) custom-call(s32[13]{0:T(128)S(1)} %stack.51.spot_ref, bf16[128,768]{1,0:T(8,128)(2,1)S(1)} %constant_dynamic-update-slice_fusion.refs_0_, bf16[128,768]{1,0:T(8,128)(2,1)S(1)} %collective-permute-done.1.refs_1_, bf16[128,768]{1,0:T(8,128)(2,1)S(1)} %collective-permute-done.2.refs_2_, ...), custom_call_target="tpu_custom_call" | custom-call | flops 4294967296 | bytes 4194304 | tf_op jit(solution)/shard_map/attention/pallas_call | solution.py:311
  38.0 1.4 %far_keys_values.2 = (bf16[4,256,1024]{2,1,0:T(8,128)(2,1)S(1)}, bf16[4,1024,256]{2,1,0:T(8,128)(2,1)S(1)}) custom-call(bf16[576,1024]{1,0:T(8,128)(2,1)S(1)} %collective-permute-done.4.cache, bf16[4,128,512]{2,1,0:T(8,128)(2,1)S(1)} %get-tuple-element.42.uk, bf16[4,512,128]{2,1,0:T(8,128)(2,1)S(1)} %get-tuple-element.43.uv), custom_call_target="tpu_custom_call" | custom-call | flops 1073741824 | bytes 4194304 | tf_op jit(solution)/shard_map/far_keys_values/pallas_call | solution.py:147
  39.4 4.7 %attention.4 = (f32[4,512,256]{2,1,0:T(8,128)S(1)}, f32[4,512,128]{2,1,0:T(8,128)S(1)}) custom-call(s32[13]{0:T(128)S(1)} %stack.51.spot_ref, bf16[128,768]{1,0:T(8,128)(2,1)S(1)} %constant_dynamic-update-slice_fusion.refs_0_, bf16[128,768]{1,0:T(8,128)(2,1)S(1)} %collective-permute-done.1.refs_1_, bf16[128,768]{1,0:T(8,128)(2,1)S(1)} %collective-permute-done.2.refs_2_, ...), custom_call_target="tpu_custom_call" | custom-call | flops 2147483648 | bytes 4194304 | tf_op jit(solution)/shard_map/attention/pallas_call | solution.py:311
  44.1 1.4 %far_keys_values.3 = (bf16[4,256,1024]{2,1,0:T(8,128)(2,1)S(1)}, bf16[4,1024,256]{2,1,0:T(8,128)(2,1)S(1)}) custom-call(bf16[576,1024]{1,0:T(8,128)(2,1)S(1)} %collective-permute-done.6.cache, bf16[4,128,512]{2,1,0:T(8,128)(2,1)S(1)} %get-tuple-element.42.uk, bf16[4,512,128]{2,1,0:T(8,128)(2,1)S(1)} %get-tuple-element.43.uv), custom_call_target="tpu_custom_call" | custom-call | flops 1073741824 | bytes 4194304 | tf_op jit(solution)/shard_map/far_keys_values/pallas_call | solution.py:147
  45.5 5.4 %attention.5 = (bf16[144,512]{1,0:T(8,128)(2,1)S(1)}, bf16[144,512]{1,0:T(8,128)(2,1)S(1)}, bf16[144,512]{1,0:T(8,128)(2,1)S(1)}, bf16[144,512]{1,0:T(8,128)(2,1)S(1)}) custom-call(s32[13]{0:T(128)S(1)} %stack.51.spot_ref, bf16[128,768]{1,0:T(8,128)(2,1)S(1)} %constant_dynamic-update-slice_fusion.refs_0_, ...), custom_call_target="tpu_custom_call" | custom-call | flops 2147483648 | bytes 4194304 | tf_op jit(solution)/shard_map/attention/pallas_call | solution.py:311
  51.1 3.2 %collective-permute-start.9 = (bf16[144,512]{1,0:T(8,128)(2,1)S(1)}, bf16[144,512]{1,0:T(8,128)(2,1)S(1)}, u32[]{:S(2)}, u32[]{:S(2)}) collective-permute-start(bf16[144,512]{1,0:T(8,128)(2,1)S(1)} %get-tuple-element.58), channel_id=1, source_target_pairs={{0,96},{8,104},{16,112},{24,120},{32,0},{40,8},{48,16},{56,24},{64... | collective-permute-start | bytes 442376 | tf_op jit(solution)/shard_map/ppermute | solution.py:43
  54.3 4.9 %collective-permute-done.7.refs_1_ = bf16[144,512]{1,0:T(8,128)(2,1)S(1)} collective-permute-done((bf16[144,512]{1,0:T(8,128)(2,1)S(1)}, bf16[144,512]{1,0:T(8,128)(2,1)S(1)}, u32[]{:S(2)}, u32[]{:S(2)}) %collective-permute-start.7) | collective-permute-done | bytes 147488 | tf_op jit(solution)/shard_map/ppermute | solution.py:43
  59.2 2.5 %collective-permute-done.8.refs_2_ = bf16[144,512]{1,0:T(8,128)(2,1)S(1)} collective-permute-done((bf16[144,512]{1,0:T(8,128)(2,1)S(1)}, bf16[144,512]{1,0:T(8,128)(2,1)S(1)}, u32[]{:S(2)}, u32[]{:S(2)}) %collective-permute-start.8) | collective-permute-done | bytes 147488 | tf_op jit(solution)/shard_map/ppermute | solution.py:43
  62.4 1.2 %collective-permute-done.10.theirs_ref = bf16[64,512]{1,0:T(8,128)(2,1)S(1)} collective-permute-done((bf16[64,512]{1,0:T(8,128)(2,1)S(1)}, bf16[64,512]{1,0:T(8,128)(2,1)S(1)}, u32[]{:S(2)}, u32[]{:S(2)}) %collective-permute-start.10) | collective-permute-done | bytes 65568 | tf_op jit(solution)/shard_map/ppermute | solution.py:43
  63.6 1.3 %project.5 = bf16[128,896]{1,0:T(8,128)(2,1)S(1)} custom-call(s32[13]{0:T(128)S(1)} %stack.51.spot_ref, bf16[128,512]{1,0:T(8,128)(2,1)S(1)} %join.1.mine_ref, bf16[64,512]{1,0:T(8,128)(2,1)S(1)} %collective-permute-done.10.theirs_ref, bf16[1024,7168]{1,0:T(8,128)(2,1)S(1)} %bitcast.13), custom_call_target="tpu_custom_call" | custom-call | flops 939524096 | bytes 4194304 | tf_op jit(solution)/shard_map/project/pallas_call | solution.py:368
  64.9 1.5 %collective-permute-start.11 = (bf16[128,896]{1,0:T(8,128)(2,1)S(1)}, bf16[128,896]{1,0:T(8,128)(2,1)S(1)}, u32[]{:S(2)}, u32[]{:S(2)}) collective-permute-start(bf16[128,896]{1,0:T(8,128)(2,1)S(1)} %project.5), channel_id=1, source_target_pairs={{0,1},{1,2},{2,3},{3,0},{4,5},{5,6},{6,7},{7,4},{8,9},{9,10},{10,1... | collective-permute-start | bytes 688136 | tf_op jit(solution)/shard_map/ppermute | solution.py:47
  66.5 1.3 %project.6 = bf16[128,896]{1,0:T(8,128)(2,1)S(1)} custom-call(s32[13]{0:T(128)S(1)} %stack.51.spot_ref, bf16[128,512]{1,0:T(8,128)(2,1)S(1)} %join.1.mine_ref, bf16[64,512]{1,0:T(8,128)(2,1)S(1)} %collective-permute-done.10.theirs_ref, bf16[1024,7168]{1,0:T(8,128)(2,1)S(1)} %bitcast.13), custom_call_target="tpu_custom_call" | custom-call | flops 939524096 | bytes 4194304 | tf_op jit(solution)/shard_map/project/pallas_call | solution.py:368
  69.0 1.3 %project.7 = bf16[128,896]{1,0:T(8,128)(2,1)S(1)} custom-call(s32[13]{0:T(128)S(1)} %stack.51.spot_ref, bf16[128,512]{1,0:T(8,128)(2,1)S(1)} %join.1.mine_ref, bf16[64,512]{1,0:T(8,128)(2,1)S(1)} %collective-permute-done.10.theirs_ref, bf16[1024,7168]{1,0:T(8,128)(2,1)S(1)} %bitcast.13), custom_call_target="tpu_custom_call" | custom-call | flops 939524096 | bytes 4194304 | tf_op jit(solution)/shard_map/project/pallas_call | solution.py:368
  70.2 2.2 %collective-permute-start.13 = (bf16[128,896]{1,0:T(8,128)(2,1)S(1)}, bf16[128,896]{1,0:T(8,128)(2,1)S(1)}, u32[]{:S(2)}, u32[]{:S(2)}) collective-permute-start(bf16[128,896]{1,0:T(8,128)(2,1)S(1)} %project.7), channel_id=1, source_target_pairs={{0,3},{1,0},{2,1},{3,2},{4,7},{5,4},{6,5},{7,6},{8,11},{9,8},{10,9... | collective-permute-start | bytes 688136 | tf_op jit(solution)/shard_map/ppermute | solution.py:47
  72.4 1.3 %project.4 = bf16[128,896]{1,0:T(8,128)(2,1)S(1)} custom-call(s32[13]{0:T(128)S(1)} %stack.51.spot_ref, bf16[128,512]{1,0:T(8,128)(2,1)S(1)} %join.1.mine_ref, bf16[64,512]{1,0:T(8,128)(2,1)S(1)} %collective-permute-done.10.theirs_ref, bf16[1024,7168]{1,0:T(8,128)(2,1)S(1)} %bitcast.13), custom_call_target="tpu_custom_call" | custom-call | flops 939524096 | bytes 4194304 | tf_op jit(solution)/shard_map/project/pallas_call | solution.py:368
  73.7 4.1 %collective-permute-done.12 = bf16[128,896]{1,0:T(8,128)(2,1)S(1)} collective-permute-done((bf16[128,896]{1,0:T(8,128)(2,1)S(1)}, bf16[128,896]{1,0:T(8,128)(2,1)S(1)}, u32[]{:S(2)}, u32[]{:S(2)}) %collective-permute-start.12) | collective-permute-done | bytes 229408 | tf_op jit(solution)/shard_map/ppermute | solution.py:47
  77.9 3.8 %collective-permute-done.13 = bf16[128,896]{1,0:T(8,128)(2,1)S(1)} collective-permute-done((bf16[128,896]{1,0:T(8,128)(2,1)S(1)}, bf16[128,896]{1,0:T(8,128)(2,1)S(1)}, u32[]{:S(2)}, u32[]{:S(2)}) %collective-permute-start.13) | collective-permute-done | bytes 229408 | tf_op jit(solution)/shard_map/ppermute | solution.py:47
  81.8 3.7 %collective-permute-start.14 = (bf16[64,896]{1,0:T(8,128)(2,1)S(1)}, bf16[64,896]{1,0:T(8,128)(2,1)S(1)}, u32[]{:S(2)}, u32[]{:S(2)}) collective-permute-start(bf16[64,896]{1,0:T(8,128)(2,1)S(1)} %slice.20), channel_id=1, source_target_pairs={{0,4},{1,5},{2,6},{3,7},{4,0},{5,1},{6,2},{7,3},{8,12},{9,13},{10,... | collective-permute-start | bytes 344072 | tf_op jit(solution)/shard_map/ppermute | solution.py:47
  85.4 3.3 %collective-permute-done.14 = bf16[64,896]{1,0:T(8,128)(2,1)S(1)} collective-permute-done((bf16[64,896]{1,0:T(8,128)(2,1)S(1)}, bf16[64,896]{1,0:T(8,128)(2,1)S(1)}, u32[]{:S(2)}, u32[]{:S(2)}) %collective-permute-start.14) | collective-permute-done | bytes 114720 | tf_op jit(solution)/shard_map/ppermute | solution.py:47
  (44 shorter events, 10.3 us)
Async XLA Ops:
  0.0 9.8 %collective-permute-start.5 = (bf16[576,1024]{1,0:T(8,128)(2,1)}, bf16[576,1024]{1,0:T(8,128)(2,1)S(1)}, u32[]{:S(2)}, u32[]{:S(2)}) collective-permute-start(bf16[576,1024]{1,0:T(8,128)(2,1)} %cache_ref.1), channel_id=1, source_target_pairs={{0,8},{8,0},{16,24},{24,16},{32,40},{40,32},{48,56},{56,48},{64,72... | collective-permute-start | bytes 3538952 | tf_op jit(solution)/shard_map/ppermute | solution.py:43
  0.0 37.9 %collective-permute-start.4 = (bf16[576,1024]{1,0:T(8,128)(2,1)}, bf16[576,1024]{1,0:T(8,128)(2,1)S(1)}, u32[]{:S(2)}, u32[]{:S(2)}) collective-permute-start(bf16[576,1024]{1,0:T(8,128)(2,1)} %cache_ref.1), channel_id=1, source_target_pairs={{0,16},{8,24},{16,0},{24,8},{32,48},{40,56},{48,32},{56,40},{64,80... | collective-permute-start | bytes 3538952 | tf_op jit(solution)/shard_map/ppermute | solution.py:43
  1.9 0.9 %copy-start = (bf16[64,1024]{1,0:T(8,128)(2,1)S(1)}, bf16[64,1024]{1,0:T(8,128)(2,1)}, u32[]{:S(2)}) copy-start(bf16[64,1024]{1,0:T(8,128)(2,1)} %nope_ref.1) | copy-start | bytes 393220
  2.8 0.8 copy-start.1
  3.7 1.4 %collective-permute-start = (bf16[64,768]{1,0:T(8,128)(2,1)S(1)}, bf16[64,768]{1,0:T(8,128)(2,1)S(1)}, u32[]{:S(2)}, u32[]{:S(2)}) collective-permute-start(bf16[64,768]{1,0:T(8,128)(2,1)S(1)} %get-tuple-element.33), channel_id=1, source_target_pairs={{0,8},{8,0},{16,24},{24,16},{32,40},{40,32},{48,56},{56,48},{64,72... | collective-permute-start | bytes 294920 | tf_op jit(solution)/shard_map/ppermute | solution.py:43
  5.1 11.8 %collective-permute-start.1 = (bf16[128,768]{1,0:T(8,128)(2,1)S(1)}, bf16[128,768]{1,0:T(8,128)(2,1)S(1)}, u32[]{:S(2)}, u32[]{:S(2)}) collective-permute-start(bf16[128,768]{1,0:T(8,128)(2,1)S(1)} %constant_dynamic-update-slice_fusion.refs_0_), channel_id=1, source_target_pairs={{0,96},{8,104},{16,112},{24,120},{32,0},{40,8},{48,16},{56,24},{64... | collective-permute-start | bytes 589832 | tf_op jit(solution)/shard_map/ppermute | solution.py:43
  8.2 9.3 %collective-permute-start.2 = (bf16[128,768]{1,0:T(8,128)(2,1)S(1)}, bf16[128,768]{1,0:T(8,128)(2,1)S(1)}, u32[]{:S(2)}, u32[]{:S(2)}) collective-permute-start(bf16[128,768]{1,0:T(8,128)(2,1)S(1)} %constant_dynamic-update-slice_fusion.refs_0_), channel_id=1, source_target_pairs={{0,64},{8,72},{16,80},{24,88},{32,96},{40,104},{48,112},{56,120},{... | collective-permute-start | bytes 589832 | tf_op jit(solution)/shard_map/ppermute | solution.py:43
  8.9 11.8 %collective-permute-start.3 = (bf16[128,768]{1,0:T(8,128)(2,1)S(1)}, bf16[128,768]{1,0:T(8,128)(2,1)S(1)}, u32[]{:S(2)}, u32[]{:S(2)}) collective-permute-start(bf16[128,768]{1,0:T(8,128)(2,1)S(1)} %constant_dynamic-update-slice_fusion.refs_0_), channel_id=1, source_target_pairs={{0,32},{8,40},{16,48},{24,56},{32,64},{40,72},{48,80},{56,88},{64,... | collective-permute-start | bytes 589832 | tf_op jit(solution)/shard_map/ppermute | solution.py:43
  9.8 1.3 %copy-start.2 = (bf16[576,1024]{1,0:T(8,128)(2,1)S(1)}, bf16[576,1024]{1,0:T(8,128)(2,1)}, u32[]{:S(2)}) copy-start(bf16[576,1024]{1,0:T(8,128)(2,1)} %cache_ref.1) | copy-start | bytes 3538948
  11.1 1.2 %copy-start.3 = (bf16[8,128,512]{2,1,0:T(8,128)(2,1)S(1)}, bf16[8,128,512]{2,1,0:T(8,128)(2,1)}, u32[]{:S(2)}) copy-start(bf16[8,128,512]{2,1,0:T(8,128)(2,1)} %uk_ref.1) | copy-start | bytes 3145732
  12.3 1.2 %copy-start.4 = (bf16[8,512,128]{2,1,0:T(8,128)(2,1)S(1)}, bf16[8,512,128]{2,1,0:T(8,128)(2,1)}, u32[]{:S(2)}) copy-start(bf16[8,512,128]{2,1,0:T(8,128)(2,1)} %uv_ref.1) | copy-start | bytes 3145732
  20.7 42.9 %slice-start = ((s8[14680064]{0:T(1024)(128)(4,1)}), s8[2097152]{0:T(1024)(128)(4,1)S(1)}, s32[]{:S(2)}) async-start(s8[14680064]{0:T(1024)(128)(4,1)} %bitcast.12), calls=%async_computation | async-start | bytes 4194304
  20.7 42.9 %slice-start.1 = ((s8[14680064]{0:T(1024)(128)(4,1)}), s8[4194304]{0:T(1024)(128)(4,1)S(1)}, s32[]{:S(2)}) async-start(s8[14680064]{0:T(1024)(128)(4,1)} %bitcast.12), calls=%async_computation.1 | async-start | bytes 8388608
  37.9 6.2 %collective-permute-start.6 = (bf16[576,1024]{1,0:T(8,128)(2,1)S(1)}, bf16[576,1024]{1,0:T(8,128)(2,1)S(1)}, u32[]{:S(2)}, u32[]{:S(2)}) collective-permute-start(bf16[576,1024]{1,0:T(8,128)(2,1)S(1)} %collective-permute-done.4.cache), channel_id=1, source_target_pairs={{0,8},{8,0},{16,24},{24,16},{32,40},{40,32},{48,56},{56,48},{64,72... | collective-permute-start | bytes 3538952 | tf_op jit(solution)/shard_map/ppermute | solution.py:43
  39.4 24.2 %slice-start.2 = ((s8[14680064]{0:T(1024)(128)(4,1)}), s8[4194304]{0:T(1024)(128)(4,1)S(1)}, s32[]{:S(2)}) async-start(s8[14680064]{0:T(1024)(128)(4,1)} %bitcast.12), calls=%async_computation.2 | async-start | bytes 8388608
  44.1 19.5 %slice-start.3 = ((s8[14680064]{0:T(1024)(128)(4,1)}), s8[4194304]{0:T(1024)(128)(4,1)S(1)}, s32[]{:S(2)}) async-start(s8[14680064]{0:T(1024)(128)(4,1)} %bitcast.12), calls=%async_computation.3 | async-start | bytes 8388608
  50.9 8.3 %collective-permute-start.7 = (bf16[144,512]{1,0:T(8,128)(2,1)S(1)}, bf16[144,512]{1,0:T(8,128)(2,1)S(1)}, u32[]{:S(2)}, u32[]{:S(2)}) collective-permute-start(bf16[144,512]{1,0:T(8,128)(2,1)S(1)} %get-tuple-element.56), channel_id=1, source_target_pairs={{0,64},{8,72},{16,80},{24,88},{32,96},{40,104},{48,112},{56,120},{... | collective-permute-start | bytes 442376 | tf_op jit(solution)/shard_map/ppermute | solution.py:43
  51.0 10.7 %collective-permute-start.8 = (bf16[144,512]{1,0:T(8,128)(2,1)S(1)}, bf16[144,512]{1,0:T(8,128)(2,1)S(1)}, u32[]{:S(2)}, u32[]{:S(2)}) collective-permute-start(bf16[144,512]{1,0:T(8,128)(2,1)S(1)} %get-tuple-element.57), channel_id=1, source_target_pairs={{0,32},{8,40},{16,48},{24,56},{32,64},{40,72},{48,80},{56,88},{64,... | collective-permute-start | bytes 442376 | tf_op jit(solution)/shard_map/ppermute | solution.py:43
  51.1 10.6 %collective-permute-start.9 = (bf16[144,512]{1,0:T(8,128)(2,1)S(1)}, bf16[144,512]{1,0:T(8,128)(2,1)S(1)}, u32[]{:S(2)}, u32[]{:S(2)}) collective-permute-start(bf16[144,512]{1,0:T(8,128)(2,1)S(1)} %get-tuple-element.58), channel_id=1, source_target_pairs={{0,96},{8,104},{16,112},{24,120},{32,0},{40,8},{48,16},{56,24},{64... | collective-permute-start | bytes 442376 | tf_op jit(solution)/shard_map/ppermute | solution.py:43
  62.3 1.3 %collective-permute-start.10 = (bf16[64,512]{1,0:T(8,128)(2,1)S(1)}, bf16[64,512]{1,0:T(8,128)(2,1)S(1)}, u32[]{:S(2)}, u32[]{:S(2)}) collective-permute-start(bf16[64,512]{1,0:T(8,128)(2,1)S(1)} %slice.13), channel_id=1, source_target_pairs={{0,8},{8,0},{16,24},{24,16},{32,40},{40,32},{48,56},{56,48},{64,72... | collective-permute-start | bytes 196616 | tf_op jit(solution)/shard_map/ppermute | solution.py:43
  64.9 8.8 %collective-permute-start.11 = (bf16[128,896]{1,0:T(8,128)(2,1)S(1)}, bf16[128,896]{1,0:T(8,128)(2,1)S(1)}, u32[]{:S(2)}, u32[]{:S(2)}) collective-permute-start(bf16[128,896]{1,0:T(8,128)(2,1)S(1)} %project.5), channel_id=1, source_target_pairs={{0,1},{1,2},{2,3},{3,0},{4,5},{5,6},{6,7},{7,4},{8,9},{9,10},{10,1... | collective-permute-start | bytes 688136 | tf_op jit(solution)/shard_map/ppermute | solution.py:47
  67.8 10.1 %collective-permute-start.12 = (bf16[128,896]{1,0:T(8,128)(2,1)S(1)}, bf16[128,896]{1,0:T(8,128)(2,1)S(1)}, u32[]{:S(2)}, u32[]{:S(2)}) collective-permute-start(bf16[128,896]{1,0:T(8,128)(2,1)S(1)} %project.6), channel_id=1, source_target_pairs={{0,2},{1,3},{2,0},{3,1},{4,6},{5,7},{6,4},{7,5},{8,10},{9,11},{10,... | collective-permute-start | bytes 688136 | tf_op jit(solution)/shard_map/ppermute | solution.py:47
  70.2 11.4 %collective-permute-start.13 = (bf16[128,896]{1,0:T(8,128)(2,1)S(1)}, bf16[128,896]{1,0:T(8,128)(2,1)S(1)}, u32[]{:S(2)}, u32[]{:S(2)}) collective-permute-start(bf16[128,896]{1,0:T(8,128)(2,1)S(1)} %project.7), channel_id=1, source_target_pairs={{0,3},{1,0},{2,1},{3,2},{4,7},{5,4},{6,5},{7,6},{8,11},{9,8},{10,9... | collective-permute-start | bytes 688136 | tf_op jit(solution)/shard_map/ppermute | solution.py:47
  81.8 7.0 %collective-permute-start.14 = (bf16[64,896]{1,0:T(8,128)(2,1)S(1)}, bf16[64,896]{1,0:T(8,128)(2,1)S(1)}, u32[]{:S(2)}, u32[]{:S(2)}) collective-permute-start(bf16[64,896]{1,0:T(8,128)(2,1)S(1)} %slice.20), channel_id=1, source_target_pairs={{0,4},{1,5},{2,6},{3,7},{4,0},{5,1},{6,2},{7,3},{8,12},{9,13},{10,... | collective-permute-start | bytes 344072 | tf_op jit(solution)/shard_map/ppermute | solution.py:47

commit v3 on v2

--- a/solution.py
+++ b/solution.py
@@ -18,6 +18,8 @@
 PIECE = 2 * TOK
 ROWS = PIECE + 16
 STEP = 256
+PART = SLOTS // 2
+SHARE = (SLOTS - PART) // 4
 
 F32 = jnp.float32
 BF16 = jnp.bfloat16
@@ -55,12 +57,17 @@
 HBM = pl.BlockSpec(memory_space=pltpu.HBM)
 
 
+def hbm(x):
+    return pltpu.with_memory_space_constraint(x, pltpu.HBM)
+
+
 def lanes(index, width=128):
     return pl.ds(pl.multiple_of(index * width, 128), width)
 
 
-def split_kernel(nope_ref, rope_ref, keep_ref, give_ref, sems):
+def split_kernel(nope_ref, rope_ref, cache_ref, keep_ref, give_ref, half_ref, share_ref, sems):
     core = lax.axis_index("ctx") & 1
+    x = lax.axis_index("head") & 3
     copies = []
     for ref, side in ((give_ref, 1 - core), (keep_ref, core)):
         for source, target in (
@@ -68,23 +75,26 @@
             (rope_ref.at[:, lanes(side, HALF * ROPE)], ref.at[:, HALF * NOPE :]),
         ):
             copies.append(pltpu.make_async_copy(source, target, sems.at[len(copies)]))
+    mine = pl.ds(pl.multiple_of(PART + x * SHARE, SHARE), SHARE)
+    for source, target in ((cache_ref.at[:, mine], share_ref), (cache_ref.at[:, :PART], half_ref)):
+        copies.append(pltpu.make_async_copy(source, target, sems.at[len(copies)]))
     for copy in copies:
         copy.start()
     for copy in copies:
         copy.wait()
 
 
-def split_queries(q_nope, q_rope):
+def split_queries(q_nope, q_rope, cache):
     shape = jax.ShapeDtypeStruct((TOK, HALF * (NOPE + ROPE)), BF16)
     return pl.pallas_call(
         split_kernel,
-        in_specs=[HBM] * 2,
-        out_specs=vmem(2),
-        out_shape=[shape, shape],
-        scratch_shapes=[pltpu.SemaphoreType.DMA((4,))],
+        in_specs=[HBM] * 3,
+        out_specs=vmem(4),
+        out_shape=[shape, shape] + [jax.ShapeDtypeStruct((LATENT + ROPE, n), BF16) for n in (PART, SHARE)],
+        scratch_shapes=[pltpu.SemaphoreType.DMA((6,))],
         compiler_params=pltpu.CompilerParams(vmem_limit_bytes=4 << 20),
         name="split_queries",
-    )(q_nope, q_rope)
+    )(hbm(q_nope), hbm(q_rope), hbm(cache))
 
 
 def form(cache, uk, uv, key_ref, val_ref):
@@ -139,7 +149,7 @@
         cost_estimate=kv_cost(2 * SLOTS),
         compiler_params=pltpu.CompilerParams(vmem_limit_bytes=12 << 20),
         name="near_keys_values",
-    )(cache, other, w_uk, w_uv)
+    )(hbm(cache), other, hbm(w_uk), hbm(w_uv))
 
 
 def far_keys_values(cache, uk, uv):
@@ -172,7 +182,7 @@
     o_ref[PIECE:, lanes(h)] = pick.astype(BF16)
 
 
-def attention_kernel(places, carried, last, bases, spot_ref, *refs):
+def attention_kernel(places, carried, last, bases, mixed, spot_ref, *refs):
     n = len(places)
     rows = n * PIECE
     m = n + 2 * len(bases)
@@ -201,7 +211,12 @@
         return jnp.dot(q, k[h, :, c * STEP : (c + 1) * STEP], preferred_element_type=F32) * SCALE2
 
     def seen(pos, base, c):
-        key = base + c * STEP + lax.broadcasted_iota(jnp.int32, (1, STEP), 1)
+        if mixed and c * STEP >= PART:
+            place = lax.broadcasted_iota(jnp.int32, (1, SHARE), 1)
+            two = [spot_ref[13 + (c * STEP - PART) // SHARE + i] * SHARE for i in range(STEP // SHARE)]
+            key = jnp.concatenate([base + PART + at + place for at in two], axis=1)
+        else:
+            key = base + c * STEP + lax.broadcasted_iota(jnp.int32, (1, STEP), 1)
         return key <= pos
 
     def finish(h, acc, shift):
@@ -235,12 +250,19 @@
             q = queries(h)
             acc = None
             for k, v, base in blocks:
+                wide = slots // STEP if len(blocks) == 1 else 1
+                weights = []
                 for c in range(slots // STEP):
                     p = jnp.exp2(scores(q, k, h, c))
                     if masked:
                         p = jnp.where(seen(pos, base, c), p, 0.0)
-                    term = jnp.dot(p.astype(BF16), v[h, c * STEP : (c + 1) * STEP], preferred_element_type=F32)
+                    weights.append(p.astype(BF16))
+                    if len(weights) < wide:
+                        continue
+                    rows_of_v = v[h, (c + 1 - wide) * STEP : (c + 1) * STEP]
+                    term = jnp.dot(jnp.concatenate(weights, axis=1), rows_of_v, preferred_element_type=F32)
                     acc = term if acc is None else acc + term
+                    weights = []
             total = acc[:, VDIM:]
             good = (total > 1e-27) & (total < 1e30)
             if masked:
@@ -298,7 +320,7 @@
             careful()
 
 
-def attention(spot, places, pieces, keys_vals, bases, carry=(), last=False):
+def attention(spot, places, pieces, keys_vals, bases, mixed, carry=(), last=False):
     n = len(pieces)
     slots = keys_vals[0].shape[2]
     if last:
@@ -309,7 +331,7 @@
             jax.ShapeDtypeStruct((HALF, n * PIECE, VDIM), F32),
         ]
     return pl.pallas_call(
-        functools.partial(attention_kernel, places, len(carry) > 0, last, bases),
+        functools.partial(attention_kernel, places, len(carry) > 0, last, bases, mixed),
         in_specs=[SMEM] + vmem(n + len(keys_vals) + len(carry)),
         out_specs=vmem(len(shapes)),
         out_shape=shapes,
@@ -387,28 +409,34 @@
         [group_start[0], ctx & 1, chip, head & 3, head >> 2]
         + [place(dy) for dy in range(4)]
         + [ctx ^ flip for flip in range(4)]
+        + [(head + step) & 3 for step in (0, 3, 1, 2)]
     ).astype(jnp.int32)
     U, PU, DU, MU = range(5, 9)
     OWN, CORES, ZNEAR, ZCORES = range(9, 13)
-    z_cache = to_ctx(latent_cache, ZLO)
     cache_other = to_ctx(latent_cache, CORE)
-    keep, give = split_queries(q_nope, q_rope)
+    keep, give, half, share = split_queries(q_nope, q_rope, latent_cache)
+    z_share = to_ctx(share, ZLO)
     given = to_ctx(give, CORE)
     u = jnp.concatenate([keep, given], axis=0)
     d_u = to_ctx(u, Y2)
     p_u = to_ctx(u, YM)
     m_u = to_ctx(u, YP)
-
-    places, pieces = (U, PU, DU, MU), (u, p_u, d_u, m_u)
-    cache_other, u_ = lax.optimization_barrier((cache_other, u))
-    *near, uk, uv = near_keys_values(latent_cache, cache_other, w_uk, w_uv)
-    carry = attention(spot, places, pieces, near, (OWN, CORES))
-    z_cache, carry = lax.optimization_barrier((z_cache, carry))
+    z_share, half = lax.optimization_barrier((z_share, half))
+    z_half = to_ctx(half, ZLO)
+    near = near_keys_values(latent_cache, cache_other, w_uk, w_uv)
+    z_share, near = lax.optimization_barrier((z_share, near))
+    *near, uk, uv = near
+    shares = [z_share, to_head(z_share, XP), to_head(z_share, XM), to_head(z_share, X2)]
+
+    places, pieces = (U, DU, PU, MU), (u, d_u, p_u, m_u)
+    carry = attention(spot, places, pieces, near, (OWN, CORES), False)
+    shares, z_half, carry = lax.optimization_barrier((shares, z_half, carry))
+    z_cache = jnp.concatenate([z_half] + shares, axis=1)
     zc_cache = to_ctx(z_cache, CORE)
-    carry = attention(spot, places, pieces, far_keys_values(z_cache, uk, uv), (ZNEAR,), carry)
+    carry = attention(spot, places, pieces, far_keys_values(z_cache, uk, uv), (ZNEAR,), True, carry)
     zc_cache, carry = lax.optimization_barrier((zc_cache, carry))
-    r_u, r_p, r_d, r_m = attention(
-        spot, places, pieces, far_keys_values(zc_cache, uk, uv), (ZCORES,), carry, True
+    r_u, r_d, r_p, r_m = attention(
+        spot, places, pieces, far_keys_values(zc_cache, uk, uv), (ZCORES,), True, carry, True
     )
     mine = join([r_u, to_ctx(r_d, Y2), to_ctx(r_p, YP), to_ctx(r_m, YM)])
 

time: 91 us -> 87.5 us (0.962)
  the two profiles are of different devices: /device:TPU:2 before, /device:TPU:0 now
where the time goes in v3:
time: 87.5 us; the launch traced here: 86.2 us
  Pallas kernels  40 us (46%)
  starting transfers between devices  25 us (29%)
  waiting for transfers between devices  19.1 us (22%)
  between operations  0.94 us (1%)
    pallas_call x3, Pallas kernels, attention(): pl.pallas_call(functools.partial(attention_kernel, places, len(carry) > 0...  26.1 us
    ppermute x7, starting transfers between devices, to_head(): return lax.ppermute(array, 'head', pairs)  13.2 us
    ppermute x12, starting transfers between devices, to_ctx(): return lax.ppermute(array, 'ctx', pairs)  11.7 us
    ppermute x7, waiting for transfers between devices, to_head(): return lax.ppermute(array, 'head', pairs)  10.4 us
    ppermute x12, waiting for transfers between devices, to_ctx(): return lax.ppermute(array, 'ctx', pairs)  8.64 us
    pallas_call x4, Pallas kernels, project(): pl.pallas_call(functools.partial(project_kernel, step), in_specs=[SMEM] +...  5.1 us
    pallas_call x1, Pallas kernels, near_keys_values(): pl.pallas_call(near_kernel, in_specs=[HBM] + vmem(1) + [HBM] * 2, out_spe...  4.13 us
    pallas_call x2, Pallas kernels, far_keys_values(): pl.pallas_call(form, in_specs=vmem(3), out_specs=vmem(2), out_shape=kv_sh...  2.78 us
  transfers between devices with their start and end apart: 19, of which 7 were waited for; matrix products, arithmetic and copies ran while one was open for 0% of the time, Pallas kernels for 37%

profile of v3, /device:TPU:0, one launch (start us, length us, event | category | flops | bytes accessed | tf_op | source)
XLA Modules:
  0.0 86.2 jit_solution(15545696923407167269)
XLA Ops:
  0.0 1.3 %split_queries.1 = (bf16[64,768]{1,0:T(8,128)(2,1)S(1)}, bf16[64,768]{1,0:T(8,128)(2,1)S(1)}, bf16[576,512]{1,0:T(8,128)(2,1)S(1)}, bf16[576,128]{1,0:T(8,128)(2,1)S(1)}) custom-call(bf16[64,1024]{1,0:T(8,128)(2,1)} %nope_ref.1, bf16[64,512]{1,0:T(8,128)(2,1)} %rope_ref.1, bf16[576,1024]{1,0:T(8,128)(2,1)} %cache_ref.3), custom_call_target="tpu_custom_call" | custom-call | tf_op jit(solution)/shard_map/split_queries/pallas_call | solution.py:89
  1.9 2.0 %collective-permute-start.4 = (bf16[576,128]{1,0:T(8,128)(2,1)S(1)}, bf16[576,128]{1,0:T(8,128)(2,1)S(1)}, u32[]{:S(2)}, u32[]{:S(2)}) collective-permute-start(bf16[576,128]{1,0:T(8,128)(2,1)S(1)} %get-tuple-element.48), channel_id=1, source_target_pairs={{0,16},{8,24},{16,0},{24,8},{32,48},{40,56},{48,32},{56,40},{64,80... | collective-permute-start | bytes 442376 | tf_op jit(solution)/shard_map/ppermute | solution.py:45
  4.7 1.6 %collective-permute-start.3 = (bf16[128,768]{1,0:T(8,128)(2,1)S(1)}, bf16[128,768]{1,0:T(8,128)(2,1)S(1)}, u32[]{:S(2)}, u32[]{:S(2)}) collective-permute-start(bf16[128,768]{1,0:T(8,128)(2,1)S(1)} %constant_dynamic-update-slice_fusion.refs_0_), channel_id=1, source_target_pairs={{0,32},{8,40},{16,48},{24,56},{32,64},{40,72},{48,80},{56,88},{64,... | collective-permute-start | bytes 589832 | tf_op jit(solution)/shard_map/ppermute | solution.py:45
  6.3 1.7 %collective-permute-start.2 = (bf16[128,768]{1,0:T(8,128)(2,1)S(1)}, bf16[128,768]{1,0:T(8,128)(2,1)S(1)}, u32[]{:S(2)}, u32[]{:S(2)}) collective-permute-start(bf16[128,768]{1,0:T(8,128)(2,1)S(1)} %constant_dynamic-update-slice_fusion.refs_0_), channel_id=1, source_target_pairs={{0,96},{8,104},{16,112},{24,120},{32,0},{40,8},{48,16},{56,24},{64... | collective-permute-start | bytes 589832 | tf_op jit(solution)/shard_map/ppermute | solution.py:45
  8.0 2.0 %collective-permute-start.1 = (bf16[128,768]{1,0:T(8,128)(2,1)S(1)}, bf16[128,768]{1,0:T(8,128)(2,1)S(1)}, u32[]{:S(2)}, u32[]{:S(2)}) collective-permute-start(bf16[128,768]{1,0:T(8,128)(2,1)S(1)} %constant_dynamic-update-slice_fusion.refs_0_), channel_id=1, source_target_pairs={{0,64},{8,72},{16,80},{24,88},{32,96},{40,104},{48,112},{56,120},{... | collective-permute-start | bytes 589832 | tf_op jit(solution)/shard_map/ppermute | solution.py:45
  10.3 4.1 %near_keys_values.1 = (bf16[4,256,1024]{2,1,0:T(8,128)(2,1)S(1)}, bf16[4,1024,256]{2,1,0:T(8,128)(2,1)S(1)}, bf16[4,256,1024]{2,1,0:T(8,128)(2,1)S(1)}, bf16[4,1...) custom-call(bf16[576,1024]{1,0:T(8,128)(2,1)} %cache_ref.3, ...), custom_call_target="tpu_custom_call" | custom-call | flops 2147483648 | bytes 4194304 | tf_op jit(solution)/shard_map/near_keys_values/pallas_call | solution.py:143
  14.4 3.1 %collective-permute-start.8 = (bf16[576,128]{1,0:T(8,128)(2,1)S(1)}, bf16[576,128]{1,0:T(8,128)(2,1)S(1)}, u32[]{:S(2)}, u32[]{:S(2)}) collective-permute-start(bf16[576,128]{1,0:T(8,128)(2,1)S(1)} %collective-permute-done.4), channel_id=1, source_target_pairs={{0,2},{1,3},{2,0},{3,1},{4,6},{5,7},{6,4},{7,5},{8,10},{9,11},{10,... | collective-permute-start | bytes 442376 | tf_op jit(solution)/shard_map/ppermute | solution.py:49
  19.6 17.2 %attention.3 = (f32[4,512,256]{2,1,0:T(8,128)S(1)}, f32[4,512,128]{2,1,0:T(8,128)S(1)}) custom-call(s32[17]{0:T(128)S(1)} %stack.64.spot_ref, bf16[128,768]{1,0:T(8,128)(2,1)S(1)} %constant_dynamic-update-slice_fusion.refs_0_, bf16[128,768]{1,0:T(8,128)(2,1)S(1)} %collective-permute-done.1.refs_1_, bf16[128,768]{1,0:T(8,128)(2,1)S(1)} %collective-permute-done.2.refs_2_, ...), custom_call_target="tpu_custom_call" | custom-call | flops 4294967296 | bytes 4194304 | tf_op jit(solution)/shard_map/attention/pallas_call | solution.py:333
  37.2 1.4 %far_keys_values.2 = (bf16[4,256,1024]{2,1,0:T(8,128)(2,1)S(1)}, bf16[4,1024,256]{2,1,0:T(8,128)(2,1)S(1)}) custom-call(bf16[576,1024]{1,0:T(8,128)(2,1)S(1)} %constant_dynamic-update-slice_fusion.2.cache, bf16[4,128,512]{2,1,0:T(8,128)(2,1)S(1)} %get-tuple-element.70.uk, bf16[4,512,128]{2,1,0:T(8,128)(2,1)S(1)} %get-tuple-element.71.uv), custom_call_target="tpu_custom_call" | custom-call | flops 1073741824 | bytes 4194304 | tf_op jit(solution)/shard_map/far_keys_values/pallas_call | solution.py:157
  38.6 4.1 %attention.4 = (f32[4,512,256]{2,1,0:T(8,128)S(1)}, f32[4,512,128]{2,1,0:T(8,128)S(1)}) custom-call(s32[17]{0:T(128)S(1)} %stack.64.spot_ref, bf16[128,768]{1,0:T(8,128)(2,1)S(1)} %constant_dynamic-update-slice_fusion.refs_0_, bf16[128,768]{1,0:T(8,128)(2,1)S(1)} %collective-permute-done.1.refs_1_, bf16[128,768]{1,0:T(8,128)(2,1)S(1)} %collective-permute-done.2.refs_2_, ...), custom_call_target="tpu_custom_call" | custom-call | flops 2147483648 | bytes 4194304 | tf_op jit(solution)/shard_map/attention/pallas_call | solution.py:333
  42.8 1.4 %far_keys_values.3 = (bf16[4,256,1024]{2,1,0:T(8,128)(2,1)S(1)}, bf16[4,1024,256]{2,1,0:T(8,128)(2,1)S(1)}) custom-call(bf16[576,1024]{1,0:T(8,128)(2,1)S(1)} %collective-permute-done.10.cache, bf16[4,128,512]{2,1,0:T(8,128)(2,1)S(1)} %get-tuple-element.70.uk, bf16[4,512,128]{2,1,0:T(8,128)(2,1)S(1)} %get-tuple-element.71.uv), custom_call_target="tpu_custom_call" | custom-call | flops 1073741824 | bytes 4194304 | tf_op jit(solution)/shard_map/far_keys_values/pallas_call | solution.py:157
  44.2 4.8 %attention.5 = (bf16[144,512]{1,0:T(8,128)(2,1)S(1)}, bf16[144,512]{1,0:T(8,128)(2,1)S(1)}, bf16[144,512]{1,0:T(8,128)(2,1)S(1)}, bf16[144,512]{1,0:T(8,128)(2,1)S(1)}) custom-call(s32[17]{0:T(128)S(1)} %stack.64.spot_ref, bf16[128,768]{1,0:T(8,128)(2,1)S(1)} %constant_dynamic-update-slice_fusion.refs_0_, ...), custom_call_target="tpu_custom_call" | custom-call | flops 2147483648 | bytes 4194304 | tf_op jit(solution)/shard_map/attention/pallas_call | solution.py:333
  49.2 3.2 %collective-permute-start.13 = (bf16[144,512]{1,0:T(8,128)(2,1)S(1)}, bf16[144,512]{1,0:T(8,128)(2,1)S(1)}, u32[]{:S(2)}, u32[]{:S(2)}) collective-permute-start(bf16[144,512]{1,0:T(8,128)(2,1)S(1)} %get-tuple-element.86), channel_id=1, source_target_pairs={{0,96},{8,104},{16,112},{24,120},{32,0},{40,8},{48,16},{56,24},{64... | collective-permute-start | bytes 442376 | tf_op jit(solution)/shard_map/ppermute | solution.py:45
  52.4 4.9 %collective-permute-done.11.refs_1_ = bf16[144,512]{1,0:T(8,128)(2,1)S(1)} collective-permute-done((bf16[144,512]{1,0:T(8,128)(2,1)S(1)}, bf16[144,512]{1,0:T(8,128)(2,1)S(1)}, u32[]{:S(2)}, u32[]{:S(2)}) %collective-permute-start.11) | collective-permute-done | bytes 147488 | tf_op jit(solution)/shard_map/ppermute | solution.py:45
  57.3 2.5 %collective-permute-done.12.refs_2_ = bf16[144,512]{1,0:T(8,128)(2,1)S(1)} collective-permute-done((bf16[144,512]{1,0:T(8,128)(2,1)S(1)}, bf16[144,512]{1,0:T(8,128)(2,1)S(1)}, u32[]{:S(2)}, u32[]{:S(2)}) %collective-permute-start.12) | collective-permute-done | bytes 147488 | tf_op jit(solution)/shard_map/ppermute | solution.py:45
  61.7 1.3 %project.5 = bf16[128,896]{1,0:T(8,128)(2,1)S(1)} custom-call(s32[17]{0:T(128)S(1)} %stack.64.spot_ref, bf16[128,512]{1,0:T(8,128)(2,1)S(1)} %join.1.mine_ref, bf16[64,512]{1,0:T(8,128)(2,1)S(1)} %collective-permute-done.14.theirs_ref, bf16[1024,7168]{1,0:T(8,128)(2,1)S(1)} %bitcast.16), custom_call_target="tpu_custom_call" | custom-call | flops 939524096 | bytes 4194304 | tf_op jit(solution)/shard_map/project/pallas_call | solution.py:390
  63.7 1.3 %project.6 = bf16[128,896]{1,0:T(8,128)(2,1)S(1)} custom-call(s32[17]{0:T(128)S(1)} %stack.64.spot_ref, bf16[128,512]{1,0:T(8,128)(2,1)S(1)} %join.1.mine_ref, bf16[64,512]{1,0:T(8,128)(2,1)S(1)} %collective-permute-done.14.theirs_ref, bf16[1024,7168]{1,0:T(8,128)(2,1)S(1)} %bitcast.16), custom_call_target="tpu_custom_call" | custom-call | flops 939524096 | bytes 4194304 | tf_op jit(solution)/shard_map/project/pallas_call | solution.py:390
  65.0 3.2 %collective-permute-start.16 = (bf16[128,896]{1,0:T(8,128)(2,1)S(1)}, bf16[128,896]{1,0:T(8,128)(2,1)S(1)}, u32[]{:S(2)}, u32[]{:S(2)}) collective-permute-start(bf16[128,896]{1,0:T(8,128)(2,1)S(1)} %project.6), channel_id=1, source_target_pairs={{0,2},{1,3},{2,0},{3,1},{4,6},{5,7},{6,4},{7,5},{8,10},{9,11},{10,... | collective-permute-start | bytes 688136 | tf_op jit(solution)/shard_map/ppermute | solution.py:49
  68.2 1.3 %project.7 = bf16[128,896]{1,0:T(8,128)(2,1)S(1)} custom-call(s32[17]{0:T(128)S(1)} %stack.64.spot_ref, bf16[128,512]{1,0:T(8,128)(2,1)S(1)} %join.1.mine_ref, bf16[64,512]{1,0:T(8,128)(2,1)S(1)} %collective-permute-done.14.theirs_ref, bf16[1024,7168]{1,0:T(8,128)(2,1)S(1)} %bitcast.16), custom_call_target="tpu_custom_call" | custom-call | flops 939524096 | bytes 4194304 | tf_op jit(solution)/shard_map/project/pallas_call | solution.py:390
  69.9 1.3 %project.4 = bf16[128,896]{1,0:T(8,128)(2,1)S(1)} custom-call(s32[17]{0:T(128)S(1)} %stack.64.spot_ref, bf16[128,512]{1,0:T(8,128)(2,1)S(1)} %join.1.mine_ref, bf16[64,512]{1,0:T(8,128)(2,1)S(1)} %collective-permute-done.14.theirs_ref, bf16[1024,7168]{1,0:T(8,128)(2,1)S(1)} %bitcast.16), custom_call_target="tpu_custom_call" | custom-call | flops 939524096 | bytes 4194304 | tf_op jit(solution)/shard_map/project/pallas_call | solution.py:390
  72.2 5.3 %collective-permute-done.16 = bf16[128,896]{1,0:T(8,128)(2,1)S(1)} collective-permute-done((bf16[128,896]{1,0:T(8,128)(2,1)S(1)}, bf16[128,896]{1,0:T(8,128)(2,1)S(1)}, u32[]{:S(2)}, u32[]{:S(2)}) %collective-permute-start.16) | collective-permute-done | bytes 229408 | tf_op jit(solution)/shard_map/ppermute | solution.py:49
  77.4 1.4 %collective-permute-done.17 = bf16[128,896]{1,0:T(8,128)(2,1)S(1)} collective-permute-done((bf16[128,896]{1,0:T(8,128)(2,1)S(1)}, bf16[128,896]{1,0:T(8,128)(2,1)S(1)}, u32[]{:S(2)}, u32[]{:S(2)}) %collective-permute-start.17) | collective-permute-done | bytes 229408 | tf_op jit(solution)/shard_map/ppermute | solution.py:49
  79.0 3.8 %collective-permute-start.18 = (bf16[64,896]{1,0:T(8,128)(2,1)S(1)}, bf16[64,896]{1,0:T(8,128)(2,1)S(1)}, u32[]{:S(2)}, u32[]{:S(2)}) collective-permute-start(bf16[64,896]{1,0:T(8,128)(2,1)S(1)} %slice.20), channel_id=1, source_target_pairs={{0,4},{1,5},{2,6},{3,7},{4,0},{5,1},{6,2},{7,3},{8,12},{9,13},{10,... | collective-permute-start | bytes 344072 | tf_op jit(solution)/shard_map/ppermute | solution.py:49
  82.8 2.8 %collective-permute-done.18 = bf16[64,896]{1,0:T(8,128)(2,1)S(1)} collective-permute-done((bf16[64,896]{1,0:T(8,128)(2,1)S(1)}, bf16[64,896]{1,0:T(8,128)(2,1)S(1)}, u32[]{:S(2)}, u32[]{:S(2)}) %collective-permute-start.18) | collective-permute-done | bytes 114720 | tf_op jit(solution)/shard_map/ppermute | solution.py:49
  (47 shorter events, 8.4 us)
Async XLA Ops:
  0.0 10.3 %collective-permute-start.5 = (bf16[576,1024]{1,0:T(8,128)(2,1)}, bf16[576,1024]{1,0:T(8,128)(2,1)S(1)}, u32[]{:S(2)}, u32[]{:S(2)}) collective-permute-start(bf16[576,1024]{1,0:T(8,128)(2,1)} %cache_ref.3), channel_id=1, source_target_pairs={{0,8},{8,0},{16,24},{24,16},{32,40},{40,32},{48,56},{56,48},{64,72... | collective-permute-start | bytes 3538952 | tf_op jit(solution)/shard_map/ppermute | solution.py:45
  1.3 3.3 %collective-permute-start = (bf16[64,768]{1,0:T(8,128)(2,1)S(1)}, bf16[64,768]{1,0:T(8,128)(2,1)S(1)}, u32[]{:S(2)}, u32[]{:S(2)}) collective-permute-start(bf16[64,768]{1,0:T(8,128)(2,1)S(1)} %get-tuple-element.47), channel_id=1, source_target_pairs={{0,8},{8,0},{16,24},{24,16},{32,40},{40,32},{48,56},{56,48},{64,72... | collective-permute-start | bytes 294920 | tf_op jit(solution)/shard_map/ppermute | solution.py:45
  1.9 8.1 %collective-permute-start.4 = (bf16[576,128]{1,0:T(8,128)(2,1)S(1)}, bf16[576,128]{1,0:T(8,128)(2,1)S(1)}, u32[]{:S(2)}, u32[]{:S(2)}) collective-permute-start(bf16[576,128]{1,0:T(8,128)(2,1)S(1)} %get-tuple-element.48), channel_id=1, source_target_pairs={{0,16},{8,24},{16,0},{24,8},{32,48},{40,56},{48,32},{56,40},{64,80... | collective-permute-start | bytes 442376 | tf_op jit(solution)/shard_map/ppermute | solution.py:45
  4.7 12.8 %collective-permute-start.3 = (bf16[128,768]{1,0:T(8,128)(2,1)S(1)}, bf16[128,768]{1,0:T(8,128)(2,1)S(1)}, u32[]{:S(2)}, u32[]{:S(2)}) collective-permute-start(bf16[128,768]{1,0:T(8,128)(2,1)S(1)} %constant_dynamic-update-slice_fusion.refs_0_), channel_id=1, source_target_pairs={{0,32},{8,40},{16,48},{24,56},{32,64},{40,72},{48,80},{56,88},{64,... | collective-permute-start | bytes 589832 | tf_op jit(solution)/shard_map/ppermute | solution.py:45
  6.3 12.3 %collective-permute-start.2 = (bf16[128,768]{1,0:T(8,128)(2,1)S(1)}, bf16[128,768]{1,0:T(8,128)(2,1)S(1)}, u32[]{:S(2)}, u32[]{:S(2)}) collective-permute-start(bf16[128,768]{1,0:T(8,128)(2,1)S(1)} %constant_dynamic-update-slice_fusion.refs_0_), channel_id=1, source_target_pairs={{0,96},{8,104},{16,112},{24,120},{32,0},{40,8},{48,16},{56,24},{64... | collective-permute-start | bytes 589832 | tf_op jit(solution)/shard_map/ppermute | solution.py:45
  8.0 11.6 %collective-permute-start.1 = (bf16[128,768]{1,0:T(8,128)(2,1)S(1)}, bf16[128,768]{1,0:T(8,128)(2,1)S(1)}, u32[]{:S(2)}, u32[]{:S(2)}) collective-permute-start(bf16[128,768]{1,0:T(8,128)(2,1)S(1)} %constant_dynamic-update-slice_fusion.refs_0_), channel_id=1, source_target_pairs={{0,64},{8,72},{16,80},{24,88},{32,96},{40,104},{48,112},{56,120},{... | collective-permute-start | bytes 589832 | tf_op jit(solution)/shard_map/ppermute | solution.py:45
  10.0 26.8 %collective-permute-start.9 = (bf16[576,512]{1,0:T(8,128)(2,1)S(1)}, bf16[576,512]{1,0:T(8,128)(2,1)S(1)}, u32[]{:S(2)}, u32[]{:S(2)}) collective-permute-start(bf16[576,512]{1,0:T(8,128)(2,1)S(1)} %get-tuple-element.58), channel_id=1, source_target_pairs={{0,16},{8,24},{16,0},{24,8},{32,48},{40,56},{48,32},{56,40},{64,80... | collective-permute-start | bytes 1769480 | tf_op jit(solution)/shard_map/ppermute | solution.py:45
  14.4 22.3 %collective-permute-start.8 = (bf16[576,128]{1,0:T(8,128)(2,1)S(1)}, bf16[576,128]{1,0:T(8,128)(2,1)S(1)}, u32[]{:S(2)}, u32[]{:S(2)}) collective-permute-start(bf16[576,128]{1,0:T(8,128)(2,1)S(1)} %collective-permute-done.4), channel_id=1, source_target_pairs={{0,2},{1,3},{2,0},{3,1},{4,6},{5,7},{6,4},{7,5},{8,10},{9,11},{10,... | collective-permute-start | bytes 442376 | tf_op jit(solution)/shard_map/ppermute | solution.py:49
  17.5 19.2 %collective-permute-start.7 = (bf16[576,128]{1,0:T(8,128)(2,1)S(1)}, bf16[576,128]{1,0:T(8,128)(2,1)S(1)}, u32[]{:S(2)}, u32[]{:S(2)}) collective-permute-start(bf16[576,128]{1,0:T(8,128)(2,1)S(1)} %collective-permute-done.4), channel_id=1, source_target_pairs={{0,3},{1,0},{2,1},{3,2},{4,7},{5,4},{6,5},{7,6},{8,11},{9,8},{10,9... | collective-permute-start | bytes 442376 | tf_op jit(solution)/shard_map/ppermute | solution.py:49
  18.7 18.1 %collective-permute-start.6 = (bf16[576,128]{1,0:T(8,128)(2,1)S(1)}, bf16[576,128]{1,0:T(8,128)(2,1)S(1)}, u32[]{:S(2)}, u32[]{:S(2)}) collective-permute-start(bf16[576,128]{1,0:T(8,128)(2,1)S(1)} %collective-permute-done.4), channel_id=1, source_target_pairs={{0,1},{1,2},{2,3},{3,0},{4,5},{5,6},{6,7},{7,4},{8,9},{9,10},{10,1... | collective-permute-start | bytes 442376 | tf_op jit(solution)/shard_map/ppermute | solution.py:49
  19.6 42.1 %slice-start = ((s8[14680064]{0:T(1024)(128)(4,1)}), s8[2097152]{0:T(1024)(128)(4,1)S(1)}, s32[]{:S(2)}) async-start(s8[14680064]{0:T(1024)(128)(4,1)} %bitcast.15), calls=%async_computation | async-start | bytes 4194304
  19.6 42.1 %slice-start.1 = ((s8[14680064]{0:T(1024)(128)(4,1)}), s8[4194304]{0:T(1024)(128)(4,1)S(1)}, s32[]{:S(2)}) async-start(s8[14680064]{0:T(1024)(128)(4,1)} %bitcast.15), calls=%async_computation.1 | async-start | bytes 8388608
  37.1 24.6 %slice-start.2 = ((s8[14680064]{0:T(1024)(128)(4,1)}), s8[4194304]{0:T(1024)(128)(4,1)S(1)}, s32[]{:S(2)}) async-start(s8[14680064]{0:T(1024)(128)(4,1)} %bitcast.15), calls=%async_computation.2 | async-start | bytes 8388608
  37.1 5.6 %collective-permute-start.10 = (bf16[576,1024]{1,0:T(8,128)(2,1)S(1)}, bf16[576,1024]{1,0:T(8,128)(2,1)S(1)}, u32[]{:S(2)}, u32[]{:S(2)}) collective-permute-start(bf16[576,1024]{1,0:T(8,128)(2,1)S(1)} %constant_dynamic-update-slice_fusion.2.cache), channel_id=1, source_target_pairs={{0,8},{8,0},{16,24},{24,16},{32,40},{40,32},{48,56},{56,48},{64,72... | collective-permute-start | bytes 3538952 | tf_op jit(solution)/shard_map/ppermute | solution.py:45
  42.7 19.0 %slice-start.3 = ((s8[14680064]{0:T(1024)(128)(4,1)}), s8[4194304]{0:T(1024)(128)(4,1)S(1)}, s32[]{:S(2)}) async-start(s8[14680064]{0:T(1024)(128)(4,1)} %bitcast.15), calls=%async_computation.3 | async-start | bytes 8388608
  49.0 8.3 %collective-permute-start.11 = (bf16[144,512]{1,0:T(8,128)(2,1)S(1)}, bf16[144,512]{1,0:T(8,128)(2,1)S(1)}, u32[]{:S(2)}, u32[]{:S(2)}) collective-permute-start(bf16[144,512]{1,0:T(8,128)(2,1)S(1)} %get-tuple-element.84), channel_id=1, source_target_pairs={{0,64},{8,72},{16,80},{24,88},{32,96},{40,104},{48,112},{56,120},{... | collective-permute-start | bytes 442376 | tf_op jit(solution)/shard_map/ppermute | solution.py:45
  49.1 10.7 %collective-permute-start.12 = (bf16[144,512]{1,0:T(8,128)(2,1)S(1)}, bf16[144,512]{1,0:T(8,128)(2,1)S(1)}, u32[]{:S(2)}, u32[]{:S(2)}) collective-permute-start(bf16[144,512]{1,0:T(8,128)(2,1)S(1)} %get-tuple-element.85), channel_id=1, source_target_pairs={{0,32},{8,40},{16,48},{24,56},{32,64},{40,72},{48,80},{56,88},{64,... | collective-permute-start | bytes 442376 | tf_op jit(solution)/shard_map/ppermute | solution.py:45
  49.2 10.6 %collective-permute-start.13 = (bf16[144,512]{1,0:T(8,128)(2,1)S(1)}, bf16[144,512]{1,0:T(8,128)(2,1)S(1)}, u32[]{:S(2)}, u32[]{:S(2)}) collective-permute-start(bf16[144,512]{1,0:T(8,128)(2,1)S(1)} %get-tuple-element.86), channel_id=1, source_target_pairs={{0,96},{8,104},{16,112},{24,120},{32,0},{40,8},{48,16},{56,24},{64... | collective-permute-start | bytes 442376 | tf_op jit(solution)/shard_map/ppermute | solution.py:45
  60.4 1.3 %collective-permute-start.14 = (bf16[64,512]{1,0:T(8,128)(2,1)S(1)}, bf16[64,512]{1,0:T(8,128)(2,1)S(1)}, u32[]{:S(2)}, u32[]{:S(2)}) collective-permute-start(bf16[64,512]{1,0:T(8,128)(2,1)S(1)} %slice.13), channel_id=1, source_target_pairs={{0,8},{8,0},{16,24},{24,16},{32,40},{40,32},{48,56},{56,48},{64,72... | collective-permute-start | bytes 196616 | tf_op jit(solution)/shard_map/ppermute | solution.py:45
  63.0 9.2 %collective-permute-start.15 = (bf16[128,896]{1,0:T(8,128)(2,1)S(1)}, bf16[128,896]{1,0:T(8,128)(2,1)S(1)}, u32[]{:S(2)}, u32[]{:S(2)}) collective-permute-start(bf16[128,896]{1,0:T(8,128)(2,1)S(1)} %project.5), channel_id=1, source_target_pairs={{0,1},{1,2},{2,3},{3,0},{4,5},{5,6},{6,7},{7,4},{8,9},{9,10},{10,1... | collective-permute-start | bytes 688136 | tf_op jit(solution)/shard_map/ppermute | solution.py:49
  65.0 12.4 %collective-permute-start.16 = (bf16[128,896]{1,0:T(8,128)(2,1)S(1)}, bf16[128,896]{1,0:T(8,128)(2,1)S(1)}, u32[]{:S(2)}, u32[]{:S(2)}) collective-permute-start(bf16[128,896]{1,0:T(8,128)(2,1)S(1)} %project.6), channel_id=1, source_target_pairs={{0,2},{1,3},{2,0},{3,1},{4,6},{5,7},{6,4},{7,5},{8,10},{9,11},{10,... | collective-permute-start | bytes 688136 | tf_op jit(solution)/shard_map/ppermute | solution.py:49
  69.5 9.3 %collective-permute-start.17 = (bf16[128,896]{1,0:T(8,128)(2,1)S(1)}, bf16[128,896]{1,0:T(8,128)(2,1)S(1)}, u32[]{:S(2)}, u32[]{:S(2)}) collective-permute-start(bf16[128,896]{1,0:T(8,128)(2,1)S(1)} %project.7), channel_id=1, source_target_pairs={{0,3},{1,0},{2,1},{3,2},{4,7},{5,4},{6,5},{7,6},{8,11},{9,8},{10,9... | collective-permute-start | bytes 688136 | tf_op jit(solution)/shard_map/ppermute | solution.py:49
  79.0 6.5 %collective-permute-start.18 = (bf16[64,896]{1,0:T(8,128)(2,1)S(1)}, bf16[64,896]{1,0:T(8,128)(2,1)S(1)}, u32[]{:S(2)}, u32[]{:S(2)}) collective-permute-start(bf16[64,896]{1,0:T(8,128)(2,1)S(1)} %slice.20), channel_id=1, source_target_pairs={{0,4},{1,5},{2,6},{3,7},{4,0},{5,1},{6,2},{7,3},{8,12},{9,13},{10,... | collective-permute-start | bytes 344072 | tf_op jit(solution)/shard_map/ppermute | solution.py:49

commit v4 on v3

--- a/solution.py
+++ b/solution.py
@@ -19,7 +19,7 @@
 ROWS = PIECE + 16
 STEP = 256
 PART = SLOTS // 2
-SHARE = (SLOTS - PART) // 4
+SHARE = (SLOTS - PART) // 2
 
 F32 = jnp.float32
 BF16 = jnp.bfloat16
@@ -39,6 +39,7 @@
 XM = [(i, (i // 4) * 4 + (i - 1) % 4) for i in range(8)]
 X2 = [(i, (i // 4) * 4 + (i + 2) % 4) for i in range(8)]
 ZHI = [(i, i ^ 4) for i in range(8)]
+XSIDE = [(i, i ^ 1) for i in range(8)]
 
 
 def to_ctx(array, pairs):
@@ -67,7 +68,7 @@
 
 def split_kernel(nope_ref, rope_ref, cache_ref, keep_ref, give_ref, half_ref, share_ref, sems):
     core = lax.axis_index("ctx") & 1
-    x = lax.axis_index("head") & 3
+    odd = lax.axis_index("head") & 1
     copies = []
     for ref, side in ((give_ref, 1 - core), (keep_ref, core)):
         for source, target in (
@@ -75,7 +76,7 @@
             (rope_ref.at[:, lanes(side, HALF * ROPE)], ref.at[:, HALF * NOPE :]),
         ):
             copies.append(pltpu.make_async_copy(source, target, sems.at[len(copies)]))
-    mine = pl.ds(pl.multiple_of(PART + x * SHARE, SHARE), SHARE)
+    mine = pl.ds(pl.multiple_of(PART + odd * SHARE, SHARE), SHARE)
     for source, target in ((cache_ref.at[:, mine], share_ref), (cache_ref.at[:, :PART], half_ref)):
         copies.append(pltpu.make_async_copy(source, target, sems.at[len(copies)]))
     for copy in copies:
@@ -211,12 +212,10 @@
         return jnp.dot(q, k[h, :, c * STEP : (c + 1) * STEP], preferred_element_type=F32) * SCALE2
 
     def seen(pos, base, c):
-        if mixed and c * STEP >= PART:
-            place = lax.broadcasted_iota(jnp.int32, (1, SHARE), 1)
-            two = [spot_ref[13 + (c * STEP - PART) // SHARE + i] * SHARE for i in range(STEP // SHARE)]
-            key = jnp.concatenate([base + PART + at + place for at in two], axis=1)
-        else:
-            key = base + c * STEP + lax.broadcasted_iota(jnp.int32, (1, STEP), 1)
+        at = c * STEP
+        if mixed and at >= PART:
+            at = PART + spot_ref[13 + (at - PART) // SHARE] * SHARE
+        key = base + at + lax.broadcasted_iota(jnp.int32, (1, STEP), 1)
         return key <= pos
 
     def finish(h, acc, shift):
@@ -372,28 +371,27 @@
     )(*pieces)
 
 
-def project_kernel(step, spot_ref, mine_ref, theirs_ref, w_ref, o_ref):
+def project_kernel(step, flip, spot_ref, mine_ref, theirs_ref, w_ref, o_ref):
     core, x, zhi = spot_ref[1], spot_ref[3], spot_ref[4]
     wide = o_ref.shape[1]
     rows = HALF * VDIM
     top = pl.ds(pl.multiple_of(core * rows, rows), rows)
     low = pl.ds(pl.multiple_of((1 - core) * rows, rows), rows)
-    for j, side in enumerate((zhi, 1 - zhi)):
-        column = lanes(side * 4 + ((x + step) & 3), wide)
-        acc = jnp.dot(mine_ref[:TOK], w_ref[top, column], preferred_element_type=F32)
-        acc += jnp.dot(theirs_ref[...], w_ref[low, column], preferred_element_type=F32)
-        o_ref[j * TOK : (j + 1) * TOK] = acc.astype(BF16)
-
-
-def project(spot, mine, theirs, w_o, step):
+    column = lanes((zhi ^ flip) * 4 + ((x + step) & 3), wide)
+    acc = jnp.dot(mine_ref[:TOK], w_ref[top, column], preferred_element_type=F32)
+    acc += jnp.dot(theirs_ref[...], w_ref[low, column], preferred_element_type=F32)
+    o_ref[...] = acc.astype(BF16)
+
+
+def project(spot, mine, theirs, w_o, step, flip):
     wide = w_o.shape[1] // 8
     return pl.pallas_call(
-        functools.partial(project_kernel, step),
+        functools.partial(project_kernel, step, flip),
         in_specs=[SMEM] + vmem(3),
         out_specs=vmem(1)[0],
-        out_shape=jax.ShapeDtypeStruct((2 * TOK, wide), BF16),
+        out_shape=jax.ShapeDtypeStruct((TOK, wide), BF16),
         cost_estimate=pl.CostEstimate(
-            flops=2 * 2 * 256 * wide * 1024, bytes_accessed=4 << 20, transcendentals=0
+            flops=2 * 256 * wide * 1024, bytes_accessed=2 << 20, transcendentals=0
         ),
         compiler_params=pltpu.CompilerParams(vmem_limit_bytes=12 << 20),
         name="project",
@@ -409,7 +407,7 @@
         [group_start[0], ctx & 1, chip, head & 3, head >> 2]
         + [place(dy) for dy in range(4)]
         + [ctx ^ flip for flip in range(4)]
-        + [(head + step) & 3 for step in (0, 3, 1, 2)]
+        + [(head + step) & 1 for step in range(2)]
     ).astype(jnp.int32)
     U, PU, DU, MU = range(5, 9)
     OWN, CORES, ZNEAR, ZCORES = range(9, 13)
@@ -421,12 +419,12 @@
     d_u = to_ctx(u, Y2)
     p_u = to_ctx(u, YM)
     m_u = to_ctx(u, YP)
-    z_share, half = lax.optimization_barrier((z_share, half))
+    cache_other, half = lax.optimization_barrier((cache_other, half))
     z_half = to_ctx(half, ZLO)
     near = near_keys_values(latent_cache, cache_other, w_uk, w_uv)
     z_share, near = lax.optimization_barrier((z_share, near))
     *near, uk, uv = near
-    shares = [z_share, to_head(z_share, XP), to_head(z_share, XM), to_head(z_share, X2)]
+    shares = [z_share, to_head(z_share, XSIDE)]
 
     places, pieces = (U, DU, PU, MU), (u, d_u, p_u, m_u)
     carry = attention(spot, places, pieces, near, (OWN, CORES), False)
@@ -441,13 +439,24 @@
     mine = join([r_u, to_ctx(r_d, Y2), to_ctx(r_p, YP), to_ctx(r_m, YM)])
 
     theirs = to_ctx(mine[TOK:], CORE)
-    out2 = to_head(project(spot, mine, theirs, w_o, 2), X2)
-    out1 = to_head(project(spot, mine, theirs, w_o, 1), XP)
-    out3 = to_head(project(spot, mine, theirs, w_o, 3), XM)
-    out0 = project(spot, mine, theirs, w_o, 0)
-    total = out0.astype(F32) + out1.astype(F32) + out2.astype(F32) + out3.astype(F32)
-    back = to_head(total[TOK:].astype(BF16), ZHI)
-    return (total[:TOK] + back.astype(F32)).astype(BF16)
+
+    def columns(mine, flip):
+        across = to_head(project(spot, mine, theirs, w_o, 2, flip), X2)
+        right = to_head(project(spot, mine, theirs, w_o, 1, flip), XP)
+        third = project(spot, mine, theirs, w_o, 3, flip)
+        left = to_head(third, XM)
+        after, _ = lax.optimization_barrier((mine, third))
+        own = project(spot, after, theirs, w_o, 0, flip)
+        return own, (right, across, left)
+
+    def added(own, others):
+        return own.astype(F32) + sum(part.astype(F32) for part in others)
+
+    own, others = columns(mine, 1)
+    after, own = lax.optimization_barrier((mine, own))
+    last = columns(after, 0)
+    back = to_head(added(own, others).astype(BF16), ZHI)
+    return (added(*last) + back.astype(F32)).astype(BF16)
 
 
 def solution(mesh):

time: 87.5 us -> 84.8 us (0.969)
  waiting for transfers between devices: 19.1 us -> 12.6 us
  Pallas kernels: 40 us -> 42.8 us
  starting transfers between devices: 25 us -> 26.9 us
    ppermute x7 -> x8, waiting for transfers between devices: 10.4 us -> 1.87 us  [to_head(): return lax.ppermute(array, 'head', pairs)]
    pallas_call x4 -> x8, Pallas kernels: 5.1 us -> 7.85 us  [project(): pl.pallas_call(functools.partial(project_kernel, step, flip), in_specs=[S...]
    ppermute x12, waiting for transfers between devices: 8.64 us -> 10.7 us  [to_ctx(): return lax.ppermute(array, 'ctx', pairs)]
    ppermute x7 -> x8, starting transfers between devices: 13.2 us -> 15.1 us  [to_head(): return lax.ppermute(array, 'head', pairs)]
  transfers between devices with their start and end apart: 19 -> 20, of which waited for: 7 -> 7; matrix products, arithmetic and copies ran while one was open for 0% -> 0% of each run, Pallas kernels for 37% -> 42%
where the time goes in v4:
time: 84.8 us; the launch traced here: 84.2 us
  Pallas kernels  42.8 us (50%)
  starting transfers between devices  26.9 us (32%)
  waiting for transfers between devices  12.6 us (15%)
  between operations  0.97 us (1%)
    pallas_call x3, Pallas kernels, attention(): pl.pallas_call(functools.partial(attention_kernel, places, len(carry) > 0...  26.1 us
    ppermute x8, starting transfers between devices, to_head(): return lax.ppermute(array, 'head', pairs)  15.1 us
    ppermute x12, starting transfers between devices, to_ctx(): return lax.ppermute(array, 'ctx', pairs)  11.7 us
    ppermute x12, waiting for transfers between devices, to_ctx(): return lax.ppermute(array, 'ctx', pairs)  10.7 us
    pallas_call x8, Pallas kernels, project(): pl.pallas_call(functools.partial(project_kernel, step, flip), in_specs=[S...  7.85 us
    pallas_call x1, Pallas kernels, near_keys_values(): pl.pallas_call(near_kernel, in_specs=[HBM] + vmem(1) + [HBM] * 2, out_spe...  4.13 us
    pallas_call x2, Pallas kernels, far_keys_values(): pl.pallas_call(form, in_specs=vmem(3), out_specs=vmem(2), out_shape=kv_sh...  2.77 us
    ppermute x8, waiting for transfers between devices, to_head(): return lax.ppermute(array, 'head', pairs)  1.87 us
  transfers between devices with their start and end apart: 20, of which 7 were waited for; matrix products, arithmetic and copies ran while one was open for 0% of the time, Pallas kernels for 42%

profile of v4, /device:TPU:0, one launch (start us, length us, event | category | flops | bytes accessed | tf_op | source)
XLA Modules:
  0.0 84.2 jit_solution(13155891532580327489)
XLA Ops:
  0.0 1.3 %split_queries.1 = (bf16[64,768]{1,0:T(8,128)(2,1)S(1)}, bf16[64,768]{1,0:T(8,128)(2,1)S(1)}, bf16[576,512]{1,0:T(8,128)(2,1)S(1)}, bf16[576,256]{1,0:T(8,128)(2,1)S(1)}) custom-call(bf16[64,1024]{1,0:T(8,128)(2,1)} %nope_ref.1, bf16[64,512]{1,0:T(8,128)(2,1)} %rope_ref.1, bf16[576,1024]{1,0:T(8,128)(2,1)} %cache_ref.3), custom_call_target="tpu_custom_call" | custom-call | tf_op jit(solution)/shard_map/split_queries/pallas_call | solution.py:90
  1.9 2.0 %collective-permute-start.4 = (bf16[576,256]{1,0:T(8,128)(2,1)S(1)}, bf16[576,256]{1,0:T(8,128)(2,1)S(1)}, u32[]{:S(2)}, u32[]{:S(2)}) collective-permute-start(bf16[576,256]{1,0:T(8,128)(2,1)S(1)} %get-tuple-element.50), channel_id=1, source_target_pairs={{0,16},{8,24},{16,0},{24,8},{32,48},{40,56},{48,32},{56,40},{64,80... | collective-permute-start | bytes 884744 | tf_op jit(solution)/shard_map/ppermute | solution.py:46
  4.7 1.6 %collective-permute-start.3 = (bf16[128,768]{1,0:T(8,128)(2,1)S(1)}, bf16[128,768]{1,0:T(8,128)(2,1)S(1)}, u32[]{:S(2)}, u32[]{:S(2)}) collective-permute-start(bf16[128,768]{1,0:T(8,128)(2,1)S(1)} %constant_dynamic-update-slice_fusion.refs_0_), channel_id=1, source_target_pairs={{0,32},{8,40},{16,48},{24,56},{32,64},{40,72},{48,80},{56,88},{64,... | collective-permute-start | bytes 589832 | tf_op jit(solution)/shard_map/ppermute | solution.py:46
  6.4 1.7 %collective-permute-start.2 = (bf16[128,768]{1,0:T(8,128)(2,1)S(1)}, bf16[128,768]{1,0:T(8,128)(2,1)S(1)}, u32[]{:S(2)}, u32[]{:S(2)}) collective-permute-start(bf16[128,768]{1,0:T(8,128)(2,1)S(1)} %constant_dynamic-update-slice_fusion.refs_0_), channel_id=1, source_target_pairs={{0,96},{8,104},{16,112},{24,120},{32,0},{40,8},{48,16},{56,24},{64... | collective-permute-start | bytes 589832 | tf_op jit(solution)/shard_map/ppermute | solution.py:46
  8.0 2.0 %collective-permute-start.1 = (bf16[128,768]{1,0:T(8,128)(2,1)S(1)}, bf16[128,768]{1,0:T(8,128)(2,1)S(1)}, u32[]{:S(2)}, u32[]{:S(2)}) collective-permute-start(bf16[128,768]{1,0:T(8,128)(2,1)S(1)} %constant_dynamic-update-slice_fusion.refs_0_), channel_id=1, source_target_pairs={{0,64},{8,72},{16,80},{24,88},{32,96},{40,104},{48,112},{56,120},{... | collective-permute-start | bytes 589832 | tf_op jit(solution)/shard_map/ppermute | solution.py:46
  10.3 4.1 %near_keys_values.1 = (bf16[4,256,1024]{2,1,0:T(8,128)(2,1)S(1)}, bf16[4,1024,256]{2,1,0:T(8,128)(2,1)S(1)}, bf16[4,256,1024]{2,1,0:T(8,128)(2,1)S(1)}, bf16[4,1...) custom-call(bf16[576,1024]{1,0:T(8,128)(2,1)} %cache_ref.3, ...), custom_call_target="tpu_custom_call" | custom-call | flops 2147483648 | bytes 4194304 | tf_op jit(solution)/shard_map/near_keys_values/pallas_call | solution.py:144
  14.4 1.6 %collective-permute-start.6 = (bf16[576,256]{1,0:T(8,128)(2,1)S(1)}, bf16[576,256]{1,0:T(8,128)(2,1)S(1)}, u32[]{:S(2)}, u32[]{:S(2)}) collective-permute-start(bf16[576,256]{1,0:T(8,128)(2,1)S(1)} %collective-permute-done.4), channel_id=1, source_target_pairs={{0,1},{1,0},{2,3},{3,2},{4,5},{5,4},{6,7},{7,6},{8,9},{9,8},{10,11... | collective-permute-start | bytes 884744 | tf_op jit(solution)/shard_map/ppermute | solution.py:50
  16.3 1.8 %collective-permute-done.1.refs_1_ = bf16[128,768]{1,0:T(8,128)(2,1)S(1)} collective-permute-done((bf16[128,768]{1,0:T(8,128)(2,1)S(1)}, bf16[128,768]{1,0:T(8,128)(2,1)S(1)}, u32[]{:S(2)}, u32[]{:S(2)}) %collective-permute-start.1) | collective-permute-done | bytes 196640 | tf_op jit(solution)/shard_map/ppermute | solution.py:46
  18.1 17.2 %attention.3 = (f32[4,512,256]{2,1,0:T(8,128)S(1)}, f32[4,512,128]{2,1,0:T(8,128)S(1)}) custom-call(s32[15]{0:T(128)S(1)} %stack.59.spot_ref, bf16[128,768]{1,0:T(8,128)(2,1)S(1)} %constant_dynamic-update-slice_fusion.refs_0_, bf16[128,768]{1,0:T(8,128)(2,1)S(1)} %collective-permute-done.1.refs_1_, bf16[128,768]{1,0:T(8,128)(2,1)S(1)} %collective-permute-done.2.refs_2_, ...), custom_call_target="tpu_custom_call" | custom-call | flops 4294967296 | bytes 4194304 | tf_op jit(solution)/shard_map/attention/pallas_call | solution.py:332
  35.6 1.4 %far_keys_values.2 = (bf16[4,256,1024]{2,1,0:T(8,128)(2,1)S(1)}, bf16[4,1024,256]{2,1,0:T(8,128)(2,1)S(1)}) custom-call(bf16[576,1024]{1,0:T(8,128)(2,1)S(1)} %constant_dynamic-update-slice_fusion.2.cache, bf16[4,128,512]{2,1,0:T(8,128)(2,1)S(1)} %get-tuple-element.70.uk, bf16[4,512,128]{2,1,0:T(8,128)(2,1)S(1)} %get-tuple-element.71.uv), custom_call_target="tpu_custom_call" | custom-call | flops 1073741824 | bytes 4194304 | tf_op jit(solution)/shard_map/far_keys_values/pallas_call | solution.py:158
  36.9 4.1 %attention.4 = (f32[4,512,256]{2,1,0:T(8,128)S(1)}, f32[4,512,128]{2,1,0:T(8,128)S(1)}) custom-call(s32[15]{0:T(128)S(1)} %stack.59.spot_ref, bf16[128,768]{1,0:T(8,128)(2,1)S(1)} %constant_dynamic-update-slice_fusion.refs_0_, bf16[128,768]{1,0:T(8,128)(2,1)S(1)} %collective-permute-done.1.refs_1_, bf16[128,768]{1,0:T(8,128)(2,1)S(1)} %collective-permute-done.2.refs_2_, ...), custom_call_target="tpu_custom_call" | custom-call | flops 2147483648 | bytes 4194304 | tf_op jit(solution)/shard_map/attention/pallas_call | solution.py:332
  41.1 1.4 %far_keys_values.3 = (bf16[4,256,1024]{2,1,0:T(8,128)(2,1)S(1)}, bf16[4,1024,256]{2,1,0:T(8,128)(2,1)S(1)}) custom-call(bf16[576,1024]{1,0:T(8,128)(2,1)S(1)} %collective-permute-done.8.cache, bf16[4,128,512]{2,1,0:T(8,128)(2,1)S(1)} %get-tuple-element.70.uk, bf16[4,512,128]{2,1,0:T(8,128)(2,1)S(1)} %get-tuple-element.71.uv), custom_call_target="tpu_custom_call" | custom-call | flops 1073741824 | bytes 4194304 | tf_op jit(solution)/shard_map/far_keys_values/pallas_call | solution.py:158
  42.5 4.8 %attention.5 = (bf16[144,512]{1,0:T(8,128)(2,1)S(1)}, bf16[144,512]{1,0:T(8,128)(2,1)S(1)}, bf16[144,512]{1,0:T(8,128)(2,1)S(1)}, bf16[144,512]{1,0:T(8,128)(2,1)S(1)}) custom-call(s32[15]{0:T(128)S(1)} %stack.59.spot_ref, bf16[128,768]{1,0:T(8,128)(2,1)S(1)} %constant_dynamic-update-slice_fusion.refs_0_, ...), custom_call_target="tpu_custom_call" | custom-call | flops 2147483648 | bytes 4194304 | tf_op jit(solution)/shard_map/attention/pallas_call | solution.py:332
  47.5 3.2 %collective-permute-start.11 = (bf16[144,512]{1,0:T(8,128)(2,1)S(1)}, bf16[144,512]{1,0:T(8,128)(2,1)S(1)}, u32[]{:S(2)}, u32[]{:S(2)}) collective-permute-start(bf16[144,512]{1,0:T(8,128)(2,1)S(1)} %get-tuple-element.86), channel_id=1, source_target_pairs={{0,96},{8,104},{16,112},{24,120},{32,0},{40,8},{48,16},{56,24},{64... | collective-permute-start | bytes 442376 | tf_op jit(solution)/shard_map/ppermute | solution.py:46
  50.7 4.9 %collective-permute-done.9.refs_1_ = bf16[144,512]{1,0:T(8,128)(2,1)S(1)} collective-permute-done((bf16[144,512]{1,0:T(8,128)(2,1)S(1)}, bf16[144,512]{1,0:T(8,128)(2,1)S(1)}, u32[]{:S(2)}, u32[]{:S(2)}) %collective-permute-start.9) | collective-permute-done | bytes 147488 | tf_op jit(solution)/shard_map/ppermute | solution.py:46
  55.6 2.5 %collective-permute-done.10.refs_2_ = bf16[144,512]{1,0:T(8,128)(2,1)S(1)} collective-permute-done((bf16[144,512]{1,0:T(8,128)(2,1)S(1)}, bf16[144,512]{1,0:T(8,128)(2,1)S(1)}, u32[]{:S(2)}, u32[]{:S(2)}) %collective-permute-start.10) | collective-permute-done | bytes 147488 | tf_op jit(solution)/shard_map/ppermute | solution.py:46
  58.8 1.2 %collective-permute-done.12.theirs_ref = bf16[64,512]{1,0:T(8,128)(2,1)S(1)} collective-permute-done((bf16[64,512]{1,0:T(8,128)(2,1)S(1)}, bf16[64,512]{1,0:T(8,128)(2,1)S(1)}, u32[]{:S(2)}, u32[]{:S(2)}) %collective-permute-start.12) | collective-permute-done | bytes 65568 | tf_op jit(solution)/shard_map/ppermute | solution.py:46
  61.1 2.8 %collective-permute-start.18 = (bf16[64,896]{1,0:T(8,128)(2,1)S(1)}, bf16[64,896]{1,0:T(8,128)(2,1)S(1)}, u32[]{:S(2)}, u32[]{:S(2)}) collective-permute-start(bf16[64,896]{1,0:T(8,128)(2,1)S(1)} %project.8), channel_id=1, source_target_pairs={{0,3},{1,0},{2,1},{3,2},{4,7},{5,4},{6,5},{7,6},{8,11},{9,8},{10,9... | collective-permute-start | bytes 344072 | tf_op jit(solution)/shard_map/ppermute | solution.py:50
  66.0 1.0 %project.15 = bf16[64,896]{1,0:T(8,128)(2,1)S(1)} custom-call(s32[15]{0:T(128)S(1)} %stack.59.spot_ref, bf16[128,512]{1,0:T(8,128)(2,1)S(1)} %join.1.mine_ref, bf16[64,512]{1,0:T(8,128)(2,1)S(1)} %collective-permute-done.12.theirs_ref, bf16[1024,7168]{1,0:T(8,128)(2,1)S(1)} %bitcast.15), custom_call_target="tpu_custom_call" | custom-call | flops 469762048 | bytes 2097152 | tf_op jit(solution)/shard_map/project/pallas_call | solution.py:388
  66.9 2.3 %collective-permute-start.17 = (bf16[64,896]{1,0:T(8,128)(2,1)S(1)}, bf16[64,896]{1,0:T(8,128)(2,1)S(1)}, u32[]{:S(2)}, u32[]{:S(2)}) collective-permute-start(bf16[64,896]{1,0:T(8,128)(2,1)S(1)} %project.15), channel_id=1, source_target_pairs={{0,2},{1,3},{2,0},{3,1},{4,6},{5,7},{6,4},{7,5},{8,10},{9,11},{10,... | collective-permute-start | bytes 344072 | tf_op jit(solution)/shard_map/ppermute | solution.py:50
  70.3 1.9 %collective-permute-start.13 = (bf16[64,896]{1,0:T(8,128)(2,1)S(1)}, bf16[64,896]{1,0:T(8,128)(2,1)S(1)}, u32[]{:S(2)}, u32[]{:S(2)}) collective-permute-start(bf16[64,896]{1,0:T(8,128)(2,1)S(1)} %project.12), channel_id=1, source_target_pairs={{0,1},{1,2},{2,3},{3,0},{4,5},{5,6},{6,7},{7,4},{8,9},{9,10},{10,1... | collective-permute-start | bytes 344072 | tf_op jit(solution)/shard_map/ppermute | solution.py:50
  75.1 1.9 %collective-permute-start.15 = (bf16[64,896]{1,0:T(8,128)(2,1)S(1)}, bf16[64,896]{1,0:T(8,128)(2,1)S(1)}, u32[]{:S(2)}, u32[]{:S(2)}) collective-permute-start(bf16[64,896]{1,0:T(8,128)(2,1)S(1)} %project.10), channel_id=1, source_target_pairs={{0,3},{1,0},{2,1},{3,2},{4,7},{5,4},{6,5},{7,6},{8,11},{9,8},{10,9... | collective-permute-start | bytes 344072 | tf_op jit(solution)/shard_map/ppermute | solution.py:50
  77.1 3.7 %collective-permute-start.19 = (bf16[64,896]{1,0:T(8,128)(2,1)S(1)}, bf16[64,896]{1,0:T(8,128)(2,1)S(1)}, u32[]{:S(2)}, u32[]{:S(2)}) collective-permute-start(bf16[64,896]{1,0:T(8,128)(2,1)S(1)} %add_convert_fusion.1), channel_id=1, source_target_pairs={{0,4},{1,5},{2,6},{3,7},{4,0},{5,1},{6,2},{7,3},{8,12},{9,13},{10,... | collective-permute-start | bytes 344072 | tf_op jit(solution)/shard_map/ppermute | solution.py:50
  81.8 1.8 %collective-permute-done.19 = bf16[64,896]{1,0:T(8,128)(2,1)S(1)} collective-permute-done((bf16[64,896]{1,0:T(8,128)(2,1)S(1)}, bf16[64,896]{1,0:T(8,128)(2,1)S(1)}, u32[]{:S(2)}, u32[]{:S(2)}) %collective-permute-start.19) | collective-permute-done | bytes 114720 | tf_op jit(solution)/shard_map/ppermute | solution.py:50
  (50 shorter events, 11.0 us)
Async XLA Ops:
  0.0 10.0 %collective-permute-start.5 = (bf16[576,1024]{1,0:T(8,128)(2,1)}, bf16[576,1024]{1,0:T(8,128)(2,1)S(1)}, u32[]{:S(2)}, u32[]{:S(2)}) collective-permute-start(bf16[576,1024]{1,0:T(8,128)(2,1)} %cache_ref.3), channel_id=1, source_target_pairs={{0,8},{8,0},{16,24},{24,16},{32,40},{40,32},{48,56},{56,48},{64,72... | collective-permute-start | bytes 3538952 | tf_op jit(solution)/shard_map/ppermute | solution.py:46
  1.3 3.4 %collective-permute-start = (bf16[64,768]{1,0:T(8,128)(2,1)S(1)}, bf16[64,768]{1,0:T(8,128)(2,1)S(1)}, u32[]{:S(2)}, u32[]{:S(2)}) collective-permute-start(bf16[64,768]{1,0:T(8,128)(2,1)S(1)} %get-tuple-element.49), channel_id=1, source_target_pairs={{0,8},{8,0},{16,24},{24,16},{32,40},{40,32},{48,56},{56,48},{64,72... | collective-permute-start | bytes 294920 | tf_op jit(solution)/shard_map/ppermute | solution.py:46
  1.9 12.5 %collective-permute-start.4 = (bf16[576,256]{1,0:T(8,128)(2,1)S(1)}, bf16[576,256]{1,0:T(8,128)(2,1)S(1)}, u32[]{:S(2)}, u32[]{:S(2)}) collective-permute-start(bf16[576,256]{1,0:T(8,128)(2,1)S(1)} %get-tuple-element.50), channel_id=1, source_target_pairs={{0,16},{8,24},{16,0},{24,8},{32,48},{40,56},{48,32},{56,40},{64,80... | collective-permute-start | bytes 884744 | tf_op jit(solution)/shard_map/ppermute | solution.py:46
  4.7 11.3 %collective-permute-start.3 = (bf16[128,768]{1,0:T(8,128)(2,1)S(1)}, bf16[128,768]{1,0:T(8,128)(2,1)S(1)}, u32[]{:S(2)}, u32[]{:S(2)}) collective-permute-start(bf16[128,768]{1,0:T(8,128)(2,1)S(1)} %constant_dynamic-update-slice_fusion.refs_0_), channel_id=1, source_target_pairs={{0,32},{8,40},{16,48},{24,56},{32,64},{40,72},{48,80},{56,88},{64,... | collective-permute-start | bytes 589832 | tf_op jit(solution)/shard_map/ppermute | solution.py:46
  6.4 9.9 %collective-permute-start.2 = (bf16[128,768]{1,0:T(8,128)(2,1)S(1)}, bf16[128,768]{1,0:T(8,128)(2,1)S(1)}, u32[]{:S(2)}, u32[]{:S(2)}) collective-permute-start(bf16[128,768]{1,0:T(8,128)(2,1)S(1)} %constant_dynamic-update-slice_fusion.refs_0_), channel_id=1, source_target_pairs={{0,96},{8,104},{16,112},{24,120},{32,0},{40,8},{48,16},{56,24},{64... | collective-permute-start | bytes 589832 | tf_op jit(solution)/shard_map/ppermute | solution.py:46
  8.0 10.0 %collective-permute-start.1 = (bf16[128,768]{1,0:T(8,128)(2,1)S(1)}, bf16[128,768]{1,0:T(8,128)(2,1)S(1)}, u32[]{:S(2)}, u32[]{:S(2)}) collective-permute-start(bf16[128,768]{1,0:T(8,128)(2,1)S(1)} %constant_dynamic-update-slice_fusion.refs_0_), channel_id=1, source_target_pairs={{0,64},{8,72},{16,80},{24,88},{32,96},{40,104},{48,112},{56,120},{... | collective-permute-start | bytes 589832 | tf_op jit(solution)/shard_map/ppermute | solution.py:46
  10.0 25.3 %collective-permute-start.7 = (bf16[576,512]{1,0:T(8,128)(2,1)S(1)}, bf16[576,512]{1,0:T(8,128)(2,1)S(1)}, u32[]{:S(2)}, u32[]{:S(2)}) collective-permute-start(bf16[576,512]{1,0:T(8,128)(2,1)S(1)} %get-tuple-element.60), channel_id=1, source_target_pairs={{0,16},{8,24},{16,0},{24,8},{32,48},{40,56},{48,32},{56,40},{64,80... | collective-permute-start | bytes 1769480 | tf_op jit(solution)/shard_map/ppermute | solution.py:46
  14.4 20.8 %collective-permute-start.6 = (bf16[576,256]{1,0:T(8,128)(2,1)S(1)}, bf16[576,256]{1,0:T(8,128)(2,1)S(1)}, u32[]{:S(2)}, u32[]{:S(2)}) collective-permute-start(bf16[576,256]{1,0:T(8,128)(2,1)S(1)} %collective-permute-done.4), channel_id=1, source_target_pairs={{0,1},{1,0},{2,3},{3,2},{4,5},{5,4},{6,7},{7,6},{8,9},{9,8},{10,11... | collective-permute-start | bytes 884744 | tf_op jit(solution)/shard_map/ppermute | solution.py:50
  18.1 42.0 %slice-start = ((s8[14680064]{0:T(1024)(128)(4,1)}), s8[2097152]{0:T(1024)(128)(4,1)S(1)}, s32[]{:S(2)}) async-start(s8[14680064]{0:T(1024)(128)(4,1)} %bitcast.14), calls=%async_computation | async-start | bytes 4194304
  18.1 42.0 %slice-start.1 = ((s8[14680064]{0:T(1024)(128)(4,1)}), s8[4194304]{0:T(1024)(128)(4,1)S(1)}, s32[]{:S(2)}) async-start(s8[14680064]{0:T(1024)(128)(4,1)} %bitcast.14), calls=%async_computation.1 | async-start | bytes 8388608
  35.4 24.6 %slice-start.2 = ((s8[14680064]{0:T(1024)(128)(4,1)}), s8[4194304]{0:T(1024)(128)(4,1)S(1)}, s32[]{:S(2)}) async-start(s8[14680064]{0:T(1024)(128)(4,1)} %bitcast.14), calls=%async_computation.2 | async-start | bytes 8388608
  35.5 5.6 %collective-permute-start.8 = (bf16[576,1024]{1,0:T(8,128)(2,1)S(1)}, bf16[576,1024]{1,0:T(8,128)(2,1)S(1)}, u32[]{:S(2)}, u32[]{:S(2)}) collective-permute-start(bf16[576,1024]{1,0:T(8,128)(2,1)S(1)} %constant_dynamic-update-slice_fusion.2.cache), channel_id=1, source_target_pairs={{0,8},{8,0},{16,24},{24,16},{32,40},{40,32},{48,56},{56,48},{64,72... | collective-permute-start | bytes 3538952 | tf_op jit(solution)/shard_map/ppermute | solution.py:46
  41.1 19.0 %slice-start.3 = ((s8[14680064]{0:T(1024)(128)(4,1)}), s8[4194304]{0:T(1024)(128)(4,1)S(1)}, s32[]{:S(2)}) async-start(s8[14680064]{0:T(1024)(128)(4,1)} %bitcast.14), calls=%async_computation.3 | async-start | bytes 8388608
  47.3 8.3 %collective-permute-start.9 = (bf16[144,512]{1,0:T(8,128)(2,1)S(1)}, bf16[144,512]{1,0:T(8,128)(2,1)S(1)}, u32[]{:S(2)}, u32[]{:S(2)}) collective-permute-start(bf16[144,512]{1,0:T(8,128)(2,1)S(1)} %get-tuple-element.84), channel_id=1, source_target_pairs={{0,64},{8,72},{16,80},{24,88},{32,96},{40,104},{48,112},{56,120},{... | collective-permute-start | bytes 442376 | tf_op jit(solution)/shard_map/ppermute | solution.py:46
  47.4 10.7 %collective-permute-start.10 = (bf16[144,512]{1,0:T(8,128)(2,1)S(1)}, bf16[144,512]{1,0:T(8,128)(2,1)S(1)}, u32[]{:S(2)}, u32[]{:S(2)}) collective-permute-start(bf16[144,512]{1,0:T(8,128)(2,1)S(1)} %get-tuple-element.85), channel_id=1, source_target_pairs={{0,32},{8,40},{16,48},{24,56},{32,64},{40,72},{48,80},{56,88},{64,... | collective-permute-start | bytes 442376 | tf_op jit(solution)/shard_map/ppermute | solution.py:46
  47.5 10.6 %collective-permute-start.11 = (bf16[144,512]{1,0:T(8,128)(2,1)S(1)}, bf16[144,512]{1,0:T(8,128)(2,1)S(1)}, u32[]{:S(2)}, u32[]{:S(2)}) collective-permute-start(bf16[144,512]{1,0:T(8,128)(2,1)S(1)} %get-tuple-element.86), channel_id=1, source_target_pairs={{0,96},{8,104},{16,112},{24,120},{32,0},{40,8},{48,16},{56,24},{64... | collective-permute-start | bytes 442376 | tf_op jit(solution)/shard_map/ppermute | solution.py:46
  58.7 1.3 %collective-permute-start.12 = (bf16[64,512]{1,0:T(8,128)(2,1)S(1)}, bf16[64,512]{1,0:T(8,128)(2,1)S(1)}, u32[]{:S(2)}, u32[]{:S(2)}) collective-permute-start(bf16[64,512]{1,0:T(8,128)(2,1)S(1)} %slice.4), channel_id=1, source_target_pairs={{0,8},{8,0},{16,24},{24,16},{32,40},{40,32},{48,56},{56,48},{64,72... | collective-permute-start | bytes 196616 | tf_op jit(solution)/shard_map/ppermute | solution.py:46
  61.1 15.9 %collective-permute-start.18 = (bf16[64,896]{1,0:T(8,128)(2,1)S(1)}, bf16[64,896]{1,0:T(8,128)(2,1)S(1)}, u32[]{:S(2)}, u32[]{:S(2)}) collective-permute-start(bf16[64,896]{1,0:T(8,128)(2,1)S(1)} %project.8), channel_id=1, source_target_pairs={{0,3},{1,0},{2,1},{3,2},{4,7},{5,4},{6,5},{7,6},{8,11},{9,8},{10,9... | collective-permute-start | bytes 344072 | tf_op jit(solution)/shard_map/ppermute | solution.py:50
  65.9 9.2 %collective-permute-start.16 = (bf16[64,896]{1,0:T(8,128)(2,1)S(1)}, bf16[64,896]{1,0:T(8,128)(2,1)S(1)}, u32[]{:S(2)}, u32[]{:S(2)}) collective-permute-start(bf16[64,896]{1,0:T(8,128)(2,1)S(1)} %project.14), channel_id=1, source_target_pairs={{0,1},{1,2},{2,3},{3,0},{4,5},{5,6},{6,7},{7,4},{8,9},{9,10},{10,1... | collective-permute-start | bytes 344072 | tf_op jit(solution)/shard_map/ppermute | solution.py:50
  66.9 10.1 %collective-permute-start.17 = (bf16[64,896]{1,0:T(8,128)(2,1)S(1)}, bf16[64,896]{1,0:T(8,128)(2,1)S(1)}, u32[]{:S(2)}, u32[]{:S(2)}) collective-permute-start(bf16[64,896]{1,0:T(8,128)(2,1)S(1)} %project.15), channel_id=1, source_target_pairs={{0,2},{1,3},{2,0},{3,1},{4,6},{5,7},{6,4},{7,5},{8,10},{9,11},{10,... | collective-permute-start | bytes 344072 | tf_op jit(solution)/shard_map/ppermute | solution.py:50
  70.3 11.5 %collective-permute-start.13 = (bf16[64,896]{1,0:T(8,128)(2,1)S(1)}, bf16[64,896]{1,0:T(8,128)(2,1)S(1)}, u32[]{:S(2)}, u32[]{:S(2)}) collective-permute-start(bf16[64,896]{1,0:T(8,128)(2,1)S(1)} %project.12), channel_id=1, source_target_pairs={{0,1},{1,2},{2,3},{3,0},{4,5},{5,6},{6,7},{7,4},{8,9},{9,10},{10,1... | collective-permute-start | bytes 344072 | tf_op jit(solution)/shard_map/ppermute | solution.py:50
  73.2 8.6 %collective-permute-start.14 = (bf16[64,896]{1,0:T(8,128)(2,1)S(1)}, bf16[64,896]{1,0:T(8,128)(2,1)S(1)}, u32[]{:S(2)}, u32[]{:S(2)}) collective-permute-start(bf16[64,896]{1,0:T(8,128)(2,1)S(1)} %project.13), channel_id=1, source_target_pairs={{0,2},{1,3},{2,0},{3,1},{4,6},{5,7},{6,4},{7,5},{8,10},{9,11},{10,... | collective-permute-start | bytes 344072 | tf_op jit(solution)/shard_map/ppermute | solution.py:50
  75.1 6.7 %collective-permute-start.15 = (bf16[64,896]{1,0:T(8,128)(2,1)S(1)}, bf16[64,896]{1,0:T(8,128)(2,1)S(1)}, u32[]{:S(2)}, u32[]{:S(2)}) collective-permute-start(bf16[64,896]{1,0:T(8,128)(2,1)S(1)} %project.10), channel_id=1, source_target_pairs={{0,3},{1,0},{2,1},{3,2},{4,7},{5,4},{6,5},{7,6},{8,11},{9,8},{10,9... | collective-permute-start | bytes 344072 | tf_op jit(solution)/shard_map/ppermute | solution.py:50
  77.1 6.4 %collective-permute-start.19 = (bf16[64,896]{1,0:T(8,128)(2,1)S(1)}, bf16[64,896]{1,0:T(8,128)(2,1)S(1)}, u32[]{:S(2)}, u32[]{:S(2)}) collective-permute-start(bf16[64,896]{1,0:T(8,128)(2,1)S(1)} %add_convert_fusion.1), channel_id=1, source_target_pairs={{0,4},{1,5},{2,6},{3,7},{4,0},{5,1},{6,2},{7,3},{8,12},{9,13},{10,... | collective-permute-start | bytes 344072 | tf_op jit(solution)/shard_map/ppermute | solution.py:50

commit v5 on v4

--- a/solution.py
+++ b/solution.py
@@ -371,27 +371,27 @@
     )(*pieces)
 
 
-def project_kernel(step, flip, spot_ref, mine_ref, theirs_ref, w_ref, o_ref):
+def project_kernel(blocks, spot_ref, mine_ref, theirs_ref, w_ref, *o_refs):
     core, x, zhi = spot_ref[1], spot_ref[3], spot_ref[4]
-    wide = o_ref.shape[1]
     rows = HALF * VDIM
     top = pl.ds(pl.multiple_of(core * rows, rows), rows)
     low = pl.ds(pl.multiple_of((1 - core) * rows, rows), rows)
-    column = lanes((zhi ^ flip) * 4 + ((x + step) & 3), wide)
-    acc = jnp.dot(mine_ref[:TOK], w_ref[top, column], preferred_element_type=F32)
-    acc += jnp.dot(theirs_ref[...], w_ref[low, column], preferred_element_type=F32)
-    o_ref[...] = acc.astype(BF16)
-
-
-def project(spot, mine, theirs, w_o, step, flip):
-    wide = w_o.shape[1] // 8
-    return pl.pallas_call(
-        functools.partial(project_kernel, step, flip),
+    for (step, flip), o_ref in zip(blocks, o_refs):
+        column = lanes((zhi ^ flip) * 4 + ((x + step) & 3), o_ref.shape[1])
+        acc = jnp.dot(mine_ref[:TOK], w_ref[top, column], preferred_element_type=F32)
+        acc += jnp.dot(theirs_ref[...], w_ref[low, column], preferred_element_type=F32)
+        o_ref[...] = acc.astype(BF16)
+
+
+def project(spot, mine, theirs, w_o, blocks):
+    n, wide = len(blocks), w_o.shape[1] // 8
+    return pl.pallas_call(
+        functools.partial(project_kernel, blocks),
         in_specs=[SMEM] + vmem(3),
-        out_specs=vmem(1)[0],
-        out_shape=jax.ShapeDtypeStruct((TOK, wide), BF16),
+        out_specs=vmem(n),
+        out_shape=[jax.ShapeDtypeStruct((TOK, wide), BF16)] * n,
         cost_estimate=pl.CostEstimate(
-            flops=2 * 256 * wide * 1024, bytes_accessed=2 << 20, transcendentals=0
+            flops=2 * n * 256 * wide * 1024, bytes_accessed=n << 21, transcendentals=0
         ),
         compiler_params=pltpu.CompilerParams(vmem_limit_bytes=12 << 20),
         name="project",
@@ -440,23 +440,20 @@
 
     theirs = to_ctx(mine[TOK:], CORE)
 
-    def columns(mine, flip):
-        across = to_head(project(spot, mine, theirs, w_o, 2, flip), X2)
-        right = to_head(project(spot, mine, theirs, w_o, 1, flip), XP)
-        third = project(spot, mine, theirs, w_o, 3, flip)
-        left = to_head(third, XM)
-        after, _ = lax.optimization_barrier((mine, third))
-        own = project(spot, after, theirs, w_o, 0, flip)
-        return own, (right, across, left)
-
-    def added(own, others):
-        return own.astype(F32) + sum(part.astype(F32) for part in others)
-
-    own, others = columns(mine, 1)
-    after, own = lax.optimization_barrier((mine, own))
-    last = columns(after, 0)
-    back = to_head(added(own, others).astype(BF16), ZHI)
-    return (added(*last) + back.astype(F32)).astype(BF16)
+    def after(*earlier):
+        return lax.optimization_barrier((mine, *earlier))[0]
+
+    (far2,) = project(spot, mine, theirs, w_o, ((2, 1),))
+    far1, far3 = project(spot, after(far2), theirs, w_o, ((1, 1), (3, 1)))
+    own1, own3 = project(spot, after(far1), theirs, w_o, ((1, 0), (3, 0)))
+    own2, far0, own0 = project(spot, after(own1), theirs, w_o, ((2, 0), (0, 1), (0, 0)))
+
+    def summed(own, right, across, left):
+        parts = (to_head(across, X2), to_head(right, XP), to_head(left, XM))
+        return own.astype(F32) + sum(part.astype(F32) for part in parts)
+
+    back = to_head(summed(far0, far1, far2, far3).astype(BF16), ZHI)
+    return (summed(own0, own1, own2, own3) + back.astype(F32)).astype(BF16)
 
 
 def solution(mesh):

time: 84.8 us -> 83 us (0.979); the launches traced: 84.2 us -> 81.4 us
  Pallas kernels: 42.8 us -> 40.1 us
  starting transfers between devices: 26.9 us -> 25.5 us
  waiting for transfers between devices: 12.6 us -> 13.8 us
    pallas_call x8 -> x4, Pallas kernels: 7.85 us -> 5.13 us  [project(): pl.pallas_call(functools.partial(project_kernel, blocks), in_specs=[SMEM]...]
    ppermute x8, starting transfers between devices: 15.1 us -> 13.8 us  [to_head(): return lax.ppermute(array, 'head', pairs)]
    ppermute x8, waiting for transfers between devices: 1.87 us -> 3.09 us  [to_head(): return lax.ppermute(array, 'head', pairs)]
  transfers between devices with their start and end apart: 20 -> 20, of which waited for: 7 -> 8; matrix products, arithmetic and copies ran while one was open for 0% -> 0% of each run, Pallas kernels for 42% -> 40%
where the time goes in v5:
time: 83 us; the launch traced here: 81.4 us
  Pallas kernels  40.1 us (48%)
  starting transfers between devices  25.5 us (31%)
  waiting for transfers between devices  13.8 us (17%)
  between operations  0.93 us (1%)
    pallas_call x3, Pallas kernels, attention(): pl.pallas_call(functools.partial(attention_kernel, places, len(carry) > 0...  26.1 us
    ppermute x8, starting transfers between devices, to_head(): return lax.ppermute(array, 'head', pairs)  13.8 us
    ppermute x12, starting transfers between devices, to_ctx(): return lax.ppermute(array, 'ctx', pairs)  11.7 us
    ppermute x12, waiting for transfers between devices, to_ctx(): return lax.ppermute(array, 'ctx', pairs)  10.7 us
    pallas_call x4, Pallas kernels, project(): pl.pallas_call(functools.partial(project_kernel, blocks), in_specs=[SMEM]...  5.13 us
    pallas_call x1, Pallas kernels, near_keys_values(): pl.pallas_call(near_kernel, in_specs=[HBM] + vmem(1) + [HBM] * 2, out_spe...  4.13 us
    ppermute x8, waiting for transfers between devices, to_head(): return lax.ppermute(array, 'head', pairs)  3.09 us
    pallas_call x2, Pallas kernels, far_keys_values(): pl.pallas_call(form, in_specs=vmem(3), out_specs=vmem(2), out_shape=kv_sh...  2.77 us
  transfers between devices with their start and end apart: 20, of which 8 were waited for; matrix products, arithmetic and copies ran while one was open for 0% of the time, Pallas kernels for 40%

profile of v5, /device:TPU:0, one launch (start us, length us, event | category | flops | bytes accessed | tf_op | source)
XLA Modules:
  0.0 81.4 jit_solution(6554700063777810546)
XLA Ops:
  0.0 1.3 %split_queries.1 = (bf16[64,768]{1,0:T(8,128)(2,1)S(1)}, bf16[64,768]{1,0:T(8,128)(2,1)S(1)}, bf16[576,512]{1,0:T(8,128)(2,1)S(1)}, bf16[576,256]{1,0:T(8,128)(2,1)S(1)}) custom-call(bf16[64,1024]{1,0:T(8,128)(2,1)} %nope_ref.1, bf16[64,512]{1,0:T(8,128)(2,1)} %rope_ref.1, bf16[576,1024]{1,0:T(8,128)(2,1)} %cache_ref.3), custom_call_target="tpu_custom_call" | custom-call | tf_op jit(solution)/shard_map/split_queries/pallas_call | solution.py:90
  1.9 2.0 %collective-permute-start.4 = (bf16[576,256]{1,0:T(8,128)(2,1)S(1)}, bf16[576,256]{1,0:T(8,128)(2,1)S(1)}, u32[]{:S(2)}, u32[]{:S(2)}) collective-permute-start(bf16[576,256]{1,0:T(8,128)(2,1)S(1)} %get-tuple-element.56), channel_id=1, source_target_pairs={{0,16},{8,24},{16,0},{24,8},{32,48},{40,56},{48,32},{56,40},{64,80... | collective-permute-start | bytes 884744 | tf_op jit(solution)/shard_map/ppermute | solution.py:46
  4.7 1.6 %collective-permute-start.3 = (bf16[128,768]{1,0:T(8,128)(2,1)S(1)}, bf16[128,768]{1,0:T(8,128)(2,1)S(1)}, u32[]{:S(2)}, u32[]{:S(2)}) collective-permute-start(bf16[128,768]{1,0:T(8,128)(2,1)S(1)} %constant_dynamic-update-slice_fusion.refs_0_), channel_id=1, source_target_pairs={{0,32},{8,40},{16,48},{24,56},{32,64},{40,72},{48,80},{56,88},{64,... | collective-permute-start | bytes 589832 | tf_op jit(solution)/shard_map/ppermute | solution.py:46
  6.4 1.7 %collective-permute-start.2 = (bf16[128,768]{1,0:T(8,128)(2,1)S(1)}, bf16[128,768]{1,0:T(8,128)(2,1)S(1)}, u32[]{:S(2)}, u32[]{:S(2)}) collective-permute-start(bf16[128,768]{1,0:T(8,128)(2,1)S(1)} %constant_dynamic-update-slice_fusion.refs_0_), channel_id=1, source_target_pairs={{0,96},{8,104},{16,112},{24,120},{32,0},{40,8},{48,16},{56,24},{64... | collective-permute-start | bytes 589832 | tf_op jit(solution)/shard_map/ppermute | solution.py:46
  8.0 2.0 %collective-permute-start.1 = (bf16[128,768]{1,0:T(8,128)(2,1)S(1)}, bf16[128,768]{1,0:T(8,128)(2,1)S(1)}, u32[]{:S(2)}, u32[]{:S(2)}) collective-permute-start(bf16[128,768]{1,0:T(8,128)(2,1)S(1)} %constant_dynamic-update-slice_fusion.refs_0_), channel_id=1, source_target_pairs={{0,64},{8,72},{16,80},{24,88},{32,96},{40,104},{48,112},{56,120},{... | collective-permute-start | bytes 589832 | tf_op jit(solution)/shard_map/ppermute | solution.py:46
  10.3 4.1 %near_keys_values.1 = (bf16[4,256,1024]{2,1,0:T(8,128)(2,1)S(1)}, bf16[4,1024,256]{2,1,0:T(8,128)(2,1)S(1)}, bf16[4,256,1024]{2,1,0:T(8,128)(2,1)S(1)}, bf16[4,1...) custom-call(bf16[576,1024]{1,0:T(8,128)(2,1)} %cache_ref.3, ...), custom_call_target="tpu_custom_call" | custom-call | flops 2147483648 | bytes 4194304 | tf_op jit(solution)/shard_map/near_keys_values/pallas_call | solution.py:144
  14.4 1.6 %collective-permute-start.6 = (bf16[576,256]{1,0:T(8,128)(2,1)S(1)}, bf16[576,256]{1,0:T(8,128)(2,1)S(1)}, u32[]{:S(2)}, u32[]{:S(2)}) collective-permute-start(bf16[576,256]{1,0:T(8,128)(2,1)S(1)} %collective-permute-done.4), channel_id=1, source_target_pairs={{0,1},{1,0},{2,3},{3,2},{4,5},{5,4},{6,7},{7,6},{8,9},{9,8},{10,11... | collective-permute-start | bytes 884744 | tf_op jit(solution)/shard_map/ppermute | solution.py:50
  16.3 1.8 %collective-permute-done.1.refs_1_ = bf16[128,768]{1,0:T(8,128)(2,1)S(1)} collective-permute-done((bf16[128,768]{1,0:T(8,128)(2,1)S(1)}, bf16[128,768]{1,0:T(8,128)(2,1)S(1)}, u32[]{:S(2)}, u32[]{:S(2)}) %collective-permute-start.1) | collective-permute-done | bytes 196640 | tf_op jit(solution)/shard_map/ppermute | solution.py:46
  18.1 17.2 %attention.3 = (f32[4,512,256]{2,1,0:T(8,128)S(1)}, f32[4,512,128]{2,1,0:T(8,128)S(1)}) custom-call(s32[15]{0:T(128)S(1)} %stack.59.spot_ref, bf16[128,768]{1,0:T(8,128)(2,1)S(1)} %constant_dynamic-update-slice_fusion.refs_0_, bf16[128,768]{1,0:T(8,128)(2,1)S(1)} %collective-permute-done.1.refs_1_, bf16[128,768]{1,0:T(8,128)(2,1)S(1)} %collective-permute-done.2.refs_2_, ...), custom_call_target="tpu_custom_call" | custom-call | flops 4294967296 | bytes 4194304 | tf_op jit(solution)/shard_map/attention/pallas_call | solution.py:332
  35.6 1.4 %far_keys_values.2 = (bf16[4,256,1024]{2,1,0:T(8,128)(2,1)S(1)}, bf16[4,1024,256]{2,1,0:T(8,128)(2,1)S(1)}) custom-call(bf16[576,1024]{1,0:T(8,128)(2,1)S(1)} %constant_dynamic-update-slice_fusion.2.cache, bf16[4,128,512]{2,1,0:T(8,128)(2,1)S(1)} %get-tuple-element.76.uk, bf16[4,512,128]{2,1,0:T(8,128)(2,1)S(1)} %get-tuple-element.77.uv), custom_call_target="tpu_custom_call" | custom-call | flops 1073741824 | bytes 4194304 | tf_op jit(solution)/shard_map/far_keys_values/pallas_call | solution.py:158
  36.9 4.1 %attention.4 = (f32[4,512,256]{2,1,0:T(8,128)S(1)}, f32[4,512,128]{2,1,0:T(8,128)S(1)}) custom-call(s32[15]{0:T(128)S(1)} %stack.59.spot_ref, bf16[128,768]{1,0:T(8,128)(2,1)S(1)} %constant_dynamic-update-slice_fusion.refs_0_, bf16[128,768]{1,0:T(8,128)(2,1)S(1)} %collective-permute-done.1.refs_1_, bf16[128,768]{1,0:T(8,128)(2,1)S(1)} %collective-permute-done.2.refs_2_, ...), custom_call_target="tpu_custom_call" | custom-call | flops 2147483648 | bytes 4194304 | tf_op jit(solution)/shard_map/attention/pallas_call | solution.py:332
  41.1 1.4 %far_keys_values.3 = (bf16[4,256,1024]{2,1,0:T(8,128)(2,1)S(1)}, bf16[4,1024,256]{2,1,0:T(8,128)(2,1)S(1)}) custom-call(bf16[576,1024]{1,0:T(8,128)(2,1)S(1)} %collective-permute-done.8.cache, bf16[4,128,512]{2,1,0:T(8,128)(2,1)S(1)} %get-tuple-element.76.uk, bf16[4,512,128]{2,1,0:T(8,128)(2,1)S(1)} %get-tuple-element.77.uv), custom_call_target="tpu_custom_call" | custom-call | flops 1073741824 | bytes 4194304 | tf_op jit(solution)/shard_map/far_keys_values/pallas_call | solution.py:158
  42.5 4.8 %attention.5 = (bf16[144,512]{1,0:T(8,128)(2,1)S(1)}, bf16[144,512]{1,0:T(8,128)(2,1)S(1)}, bf16[144,512]{1,0:T(8,128)(2,1)S(1)}, bf16[144,512]{1,0:T(8,128)(2,1)S(1)}) custom-call(s32[15]{0:T(128)S(1)} %stack.59.spot_ref, bf16[128,768]{1,0:T(8,128)(2,1)S(1)} %constant_dynamic-update-slice_fusion.refs_0_, ...), custom_call_target="tpu_custom_call" | custom-call | flops 2147483648 | bytes 4194304 | tf_op jit(solution)/shard_map/attention/pallas_call | solution.py:332
  47.5 3.2 %collective-permute-start.11 = (bf16[144,512]{1,0:T(8,128)(2,1)S(1)}, bf16[144,512]{1,0:T(8,128)(2,1)S(1)}, u32[]{:S(2)}, u32[]{:S(2)}) collective-permute-start(bf16[144,512]{1,0:T(8,128)(2,1)S(1)} %get-tuple-element.92), channel_id=1, source_target_pairs={{0,96},{8,104},{16,112},{24,120},{32,0},{40,8},{48,16},{56,24},{64... | collective-permute-start | bytes 442376 | tf_op jit(solution)/shard_map/ppermute | solution.py:46
  50.7 4.9 %collective-permute-done.9.refs_1_ = bf16[144,512]{1,0:T(8,128)(2,1)S(1)} collective-permute-done((bf16[144,512]{1,0:T(8,128)(2,1)S(1)}, bf16[144,512]{1,0:T(8,128)(2,1)S(1)}, u32[]{:S(2)}, u32[]{:S(2)}) %collective-permute-start.9) | collective-permute-done | bytes 147488 | tf_op jit(solution)/shard_map/ppermute | solution.py:46
  55.6 2.5 %collective-permute-done.10.refs_2_ = bf16[144,512]{1,0:T(8,128)(2,1)S(1)} collective-permute-done((bf16[144,512]{1,0:T(8,128)(2,1)S(1)}, bf16[144,512]{1,0:T(8,128)(2,1)S(1)}, u32[]{:S(2)}, u32[]{:S(2)}) %collective-permute-start.10) | collective-permute-done | bytes 147488 | tf_op jit(solution)/shard_map/ppermute | solution.py:46
  61.1 3.1 %collective-permute-start.16 = (bf16[64,896]{1,0:T(8,128)(2,1)S(1)}, bf16[64,896]{1,0:T(8,128)(2,1)S(1)}, u32[]{:S(2)}, u32[]{:S(2)}) collective-permute-start(bf16[64,896]{1,0:T(8,128)(2,1)S(1)} %project.4), channel_id=1, source_target_pairs={{0,2},{1,3},{2,0},{3,1},{4,6},{5,7},{6,4},{7,5},{8,10},{9,11},{10,... | collective-permute-start | bytes 344072 | tf_op jit(solution)/shard_map/ppermute | solution.py:50
  64.2 1.3 %project.5 = (bf16[64,896]{1,0:T(8,128)(2,1)S(1)}, bf16[64,896]{1,0:T(8,128)(2,1)S(1)}) custom-call(s32[15]{0:T(128)S(1)} %stack.59.spot_ref, bf16[128,512]{1,0:T(8,128)(2,1)S(1)} %join.1.mine_ref, bf16[64,512]{1,0:T(8,128)(2,1)S(1)} %collective-permute-done.12.theirs_ref, bf16[1024,7168]{1,0:T(8,128)(2,1)S(1)} %bitcast.15), custom_call_target="tpu_custom_call" | custom-call | flops 939524096 | bytes 4194304 | tf_op jit(solution)/shard_map/project/pallas_call | solution.py:388
  66.1 1.3 %project.6 = (bf16[64,896]{1,0:T(8,128)(2,1)S(1)}, bf16[64,896]{1,0:T(8,128)(2,1)S(1)}) custom-call(s32[15]{0:T(128)S(1)} %stack.59.spot_ref, bf16[128,512]{1,0:T(8,128)(2,1)S(1)} %join.1.mine_ref, bf16[64,512]{1,0:T(8,128)(2,1)S(1)} %collective-permute-done.12.theirs_ref, bf16[1024,7168]{1,0:T(8,128)(2,1)S(1)} %bitcast.15), custom_call_target="tpu_custom_call" | custom-call | flops 939524096 | bytes 4194304 | tf_op jit(solution)/shard_map/project/pallas_call | solution.py:388
  67.5 3.2 %collective-permute-start.18 = (bf16[64,896]{1,0:T(8,128)(2,1)S(1)}, bf16[64,896]{1,0:T(8,128)(2,1)S(1)}, u32[]{:S(2)}, u32[]{:S(2)}) collective-permute-start(bf16[64,896]{1,0:T(8,128)(2,1)S(1)} %get-tuple-element.102), channel_id=1, source_target_pairs={{0,3},{1,0},{2,1},{3,2},{4,7},{5,4},{6,5},{7,6},{8,11},{9,8},{10,9... | collective-permute-start | bytes 344072 | tf_op jit(solution)/shard_map/ppermute | solution.py:50
  70.7 1.4 %collective-permute-start.15 = (bf16[64,896]{1,0:T(8,128)(2,1)S(1)}, bf16[64,896]{1,0:T(8,128)(2,1)S(1)}, u32[]{:S(2)}, u32[]{:S(2)}) collective-permute-start(bf16[64,896]{1,0:T(8,128)(2,1)S(1)} %get-tuple-element.100), channel_id=1, source_target_pairs={{0,3},{1,0},{2,1},{3,2},{4,7},{5,4},{6,5},{7,6},{8,11},{9,8},{10,9... | collective-permute-start | bytes 344072 | tf_op jit(solution)/shard_map/ppermute | solution.py:50
  72.1 1.6 %project.7 = (bf16[64,896]{1,0:T(8,128)(2,1)S(1)}, bf16[64,896]{1,0:T(8,128)(2,1)S(1)}, bf16[64,896]{1,0:T(8,128)(2,1)S(1)}) custom-call(s32[15]{0:T(128)S(1)} %stack.59.spot_ref, bf16[128,512]{1,0:T(8,128)(2,1)S(1)} %join.1.mine_ref, bf16[64,512]{1,0:T(8,128)(2,1)S(1)} %collective-permute-done.12.theirs_ref, bf16[1024,7168]{1,0:T(8,128)(2,1)S(1)} %bitcast.15), custom_call_target="tpu_custom_call" | custom-call | flops 1409286144 | bytes 6291456 | tf_op jit(solution)/shard_map/project/pallas_call | solution.py:388
  74.2 3.7 %collective-permute-start.19 = (bf16[64,896]{1,0:T(8,128)(2,1)S(1)}, bf16[64,896]{1,0:T(8,128)(2,1)S(1)}, u32[]{:S(2)}, u32[]{:S(2)}) collective-permute-start(bf16[64,896]{1,0:T(8,128)(2,1)S(1)} %add_convert_fusion.1), channel_id=1, source_target_pairs={{0,4},{1,5},{2,6},{3,7},{4,0},{5,1},{6,2},{7,3},{8,12},{9,13},{10,... | collective-permute-start | bytes 344072 | tf_op jit(solution)/shard_map/ppermute | solution.py:50
  77.9 2.2 %collective-permute-done.13 = bf16[64,896]{1,0:T(8,128)(2,1)S(1)} collective-permute-done((bf16[64,896]{1,0:T(8,128)(2,1)S(1)}, bf16[64,896]{1,0:T(8,128)(2,1)S(1)}, u32[]{:S(2)}, u32[]{:S(2)}) %collective-permute-start.13) | collective-permute-done | bytes 114720 | tf_op jit(solution)/shard_map/ppermute | solution.py:50
  (46 shorter events, 7.1 us)
Async XLA Ops:
  0.0 10.0 %collective-permute-start.5 = (bf16[576,1024]{1,0:T(8,128)(2,1)}, bf16[576,1024]{1,0:T(8,128)(2,1)S(1)}, u32[]{:S(2)}, u32[]{:S(2)}) collective-permute-start(bf16[576,1024]{1,0:T(8,128)(2,1)} %cache_ref.3), channel_id=1, source_target_pairs={{0,8},{8,0},{16,24},{24,16},{32,40},{40,32},{48,56},{56,48},{64,72... | collective-permute-start | bytes 3538952 | tf_op jit(solution)/shard_map/ppermute | solution.py:46
  1.3 3.4 %collective-permute-start = (bf16[64,768]{1,0:T(8,128)(2,1)S(1)}, bf16[64,768]{1,0:T(8,128)(2,1)S(1)}, u32[]{:S(2)}, u32[]{:S(2)}) collective-permute-start(bf16[64,768]{1,0:T(8,128)(2,1)S(1)} %get-tuple-element.55), channel_id=1, source_target_pairs={{0,8},{8,0},{16,24},{24,16},{32,40},{40,32},{48,56},{56,48},{64,72... | collective-permute-start | bytes 294920 | tf_op jit(solution)/shard_map/ppermute | solution.py:46
  1.9 12.5 %collective-permute-start.4 = (bf16[576,256]{1,0:T(8,128)(2,1)S(1)}, bf16[576,256]{1,0:T(8,128)(2,1)S(1)}, u32[]{:S(2)}, u32[]{:S(2)}) collective-permute-start(bf16[576,256]{1,0:T(8,128)(2,1)S(1)} %get-tuple-element.56), channel_id=1, source_target_pairs={{0,16},{8,24},{16,0},{24,8},{32,48},{40,56},{48,32},{56,40},{64,80... | collective-permute-start | bytes 884744 | tf_op jit(solution)/shard_map/ppermute | solution.py:46
  4.7 11.3 %collective-permute-start.3 = (bf16[128,768]{1,0:T(8,128)(2,1)S(1)}, bf16[128,768]{1,0:T(8,128)(2,1)S(1)}, u32[]{:S(2)}, u32[]{:S(2)}) collective-permute-start(bf16[128,768]{1,0:T(8,128)(2,1)S(1)} %constant_dynamic-update-slice_fusion.refs_0_), channel_id=1, source_target_pairs={{0,32},{8,40},{16,48},{24,56},{32,64},{40,72},{48,80},{56,88},{64,... | collective-permute-start | bytes 589832 | tf_op jit(solution)/shard_map/ppermute | solution.py:46
  6.4 9.9 %collective-permute-start.2 = (bf16[128,768]{1,0:T(8,128)(2,1)S(1)}, bf16[128,768]{1,0:T(8,128)(2,1)S(1)}, u32[]{:S(2)}, u32[]{:S(2)}) collective-permute-start(bf16[128,768]{1,0:T(8,128)(2,1)S(1)} %constant_dynamic-update-slice_fusion.refs_0_), channel_id=1, source_target_pairs={{0,96},{8,104},{16,112},{24,120},{32,0},{40,8},{48,16},{56,24},{64... | collective-permute-start | bytes 589832 | tf_op jit(solution)/shard_map/ppermute | solution.py:46
  8.0 10.0 %collective-permute-start.1 = (bf16[128,768]{1,0:T(8,128)(2,1)S(1)}, bf16[128,768]{1,0:T(8,128)(2,1)S(1)}, u32[]{:S(2)}, u32[]{:S(2)}) collective-permute-start(bf16[128,768]{1,0:T(8,128)(2,1)S(1)} %constant_dynamic-update-slice_fusion.refs_0_), channel_id=1, source_target_pairs={{0,64},{8,72},{16,80},{24,88},{32,96},{40,104},{48,112},{56,120},{... | collective-permute-start | bytes 589832 | tf_op jit(solution)/shard_map/ppermute | solution.py:46
  10.0 25.3 %collective-permute-start.7 = (bf16[576,512]{1,0:T(8,128)(2,1)S(1)}, bf16[576,512]{1,0:T(8,128)(2,1)S(1)}, u32[]{:S(2)}, u32[]{:S(2)}) collective-permute-start(bf16[576,512]{1,0:T(8,128)(2,1)S(1)} %get-tuple-element.66), channel_id=1, source_target_pairs={{0,16},{8,24},{16,0},{24,8},{32,48},{40,56},{48,32},{56,40},{64,80... | collective-permute-start | bytes 1769480 | tf_op jit(solution)/shard_map/ppermute | solution.py:46
  14.4 20.8 %collective-permute-start.6 = (bf16[576,256]{1,0:T(8,128)(2,1)S(1)}, bf16[576,256]{1,0:T(8,128)(2,1)S(1)}, u32[]{:S(2)}, u32[]{:S(2)}) collective-permute-start(bf16[576,256]{1,0:T(8,128)(2,1)S(1)} %collective-permute-done.4), channel_id=1, source_target_pairs={{0,1},{1,0},{2,3},{3,2},{4,5},{5,4},{6,7},{7,6},{8,9},{9,8},{10,11... | collective-permute-start | bytes 884744 | tf_op jit(solution)/shard_map/ppermute | solution.py:50
  18.1 42.0 %slice-start = ((s8[14680064]{0:T(1024)(128)(4,1)}), s8[2097152]{0:T(1024)(128)(4,1)S(1)}, s32[]{:S(2)}) async-start(s8[14680064]{0:T(1024)(128)(4,1)} %bitcast.14), calls=%async_computation | async-start | bytes 4194304
  18.1 42.0 %slice-start.1 = ((s8[14680064]{0:T(1024)(128)(4,1)}), s8[4194304]{0:T(1024)(128)(4,1)S(1)}, s32[]{:S(2)}) async-start(s8[14680064]{0:T(1024)(128)(4,1)} %bitcast.14), calls=%async_computation.1 | async-start | bytes 8388608
  35.4 24.6 %slice-start.2 = ((s8[14680064]{0:T(1024)(128)(4,1)}), s8[4194304]{0:T(1024)(128)(4,1)S(1)}, s32[]{:S(2)}) async-start(s8[14680064]{0:T(1024)(128)(4,1)} %bitcast.14), calls=%async_computation.2 | async-start | bytes 8388608
  35.5 5.6 %collective-permute-start.8 = (bf16[576,1024]{1,0:T(8,128)(2,1)S(1)}, bf16[576,1024]{1,0:T(8,128)(2,1)S(1)}, u32[]{:S(2)}, u32[]{:S(2)}) collective-permute-start(bf16[576,1024]{1,0:T(8,128)(2,1)S(1)} %constant_dynamic-update-slice_fusion.2.cache), channel_id=1, source_target_pairs={{0,8},{8,0},{16,24},{24,16},{32,40},{40,32},{48,56},{56,48},{64,72... | collective-permute-start | bytes 3538952 | tf_op jit(solution)/shard_map/ppermute | solution.py:46
  41.1 19.0 %slice-start.3 = ((s8[14680064]{0:T(1024)(128)(4,1)}), s8[4194304]{0:T(1024)(128)(4,1)S(1)}, s32[]{:S(2)}) async-start(s8[14680064]{0:T(1024)(128)(4,1)} %bitcast.14), calls=%async_computation.3 | async-start | bytes 8388608
  47.3 8.3 %collective-permute-start.9 = (bf16[144,512]{1,0:T(8,128)(2,1)S(1)}, bf16[144,512]{1,0:T(8,128)(2,1)S(1)}, u32[]{:S(2)}, u32[]{:S(2)}) collective-permute-start(bf16[144,512]{1,0:T(8,128)(2,1)S(1)} %get-tuple-element.90), channel_id=1, source_target_pairs={{0,64},{8,72},{16,80},{24,88},{32,96},{40,104},{48,112},{56,120},{... | collective-permute-start | bytes 442376 | tf_op jit(solution)/shard_map/ppermute | solution.py:46
  47.4 10.7 %collective-permute-start.10 = (bf16[144,512]{1,0:T(8,128)(2,1)S(1)}, bf16[144,512]{1,0:T(8,128)(2,1)S(1)}, u32[]{:S(2)}, u32[]{:S(2)}) collective-permute-start(bf16[144,512]{1,0:T(8,128)(2,1)S(1)} %get-tuple-element.91), channel_id=1, source_target_pairs={{0,32},{8,40},{16,48},{24,56},{32,64},{40,72},{48,80},{56,88},{64,... | collective-permute-start | bytes 442376 | tf_op jit(solution)/shard_map/ppermute | solution.py:46
  47.5 10.6 %collective-permute-start.11 = (bf16[144,512]{1,0:T(8,128)(2,1)S(1)}, bf16[144,512]{1,0:T(8,128)(2,1)S(1)}, u32[]{:S(2)}, u32[]{:S(2)}) collective-permute-start(bf16[144,512]{1,0:T(8,128)(2,1)S(1)} %get-tuple-element.92), channel_id=1, source_target_pairs={{0,96},{8,104},{16,112},{24,120},{32,0},{40,8},{48,16},{56,24},{64... | collective-permute-start | bytes 442376 | tf_op jit(solution)/shard_map/ppermute | solution.py:46
  58.7 1.3 %collective-permute-start.12 = (bf16[64,512]{1,0:T(8,128)(2,1)S(1)}, bf16[64,512]{1,0:T(8,128)(2,1)S(1)}, u32[]{:S(2)}, u32[]{:S(2)}) collective-permute-start(bf16[64,512]{1,0:T(8,128)(2,1)S(1)} %slice.4), channel_id=1, source_target_pairs={{0,8},{8,0},{16,24},{24,16},{32,40},{40,32},{48,56},{56,48},{64,72... | collective-permute-start | bytes 196616 | tf_op jit(solution)/shard_map/ppermute | solution.py:46
  61.1 12.7 %collective-permute-start.16 = (bf16[64,896]{1,0:T(8,128)(2,1)S(1)}, bf16[64,896]{1,0:T(8,128)(2,1)S(1)}, u32[]{:S(2)}, u32[]{:S(2)}) collective-permute-start(bf16[64,896]{1,0:T(8,128)(2,1)S(1)} %project.4), channel_id=1, source_target_pairs={{0,2},{1,3},{2,0},{3,1},{4,6},{5,7},{6,4},{7,5},{8,10},{9,11},{10,... | collective-permute-start | bytes 344072 | tf_op jit(solution)/shard_map/ppermute | solution.py:50
  65.4 8.7 %collective-permute-start.17 = (bf16[64,896]{1,0:T(8,128)(2,1)S(1)}, bf16[64,896]{1,0:T(8,128)(2,1)S(1)}, u32[]{:S(2)}, u32[]{:S(2)}) collective-permute-start(bf16[64,896]{1,0:T(8,128)(2,1)S(1)} %get-tuple-element.94), channel_id=1, source_target_pairs={{0,1},{1,2},{2,3},{3,0},{4,5},{5,6},{6,7},{7,4},{8,9},{9,10},{10,1... | collective-permute-start | bytes 344072 | tf_op jit(solution)/shard_map/ppermute | solution.py:50
  67.4 10.5 %collective-permute-start.14 = (bf16[64,896]{1,0:T(8,128)(2,1)S(1)}, bf16[64,896]{1,0:T(8,128)(2,1)S(1)}, u32[]{:S(2)}, u32[]{:S(2)}) collective-permute-start(bf16[64,896]{1,0:T(8,128)(2,1)S(1)} %get-tuple-element.96), channel_id=1, source_target_pairs={{0,1},{1,2},{2,3},{3,0},{4,5},{5,6},{6,7},{7,4},{8,9},{9,10},{10,1... | collective-permute-start | bytes 344072 | tf_op jit(solution)/shard_map/ppermute | solution.py:50
  67.5 6.7 %collective-permute-start.18 = (bf16[64,896]{1,0:T(8,128)(2,1)S(1)}, bf16[64,896]{1,0:T(8,128)(2,1)S(1)}, u32[]{:S(2)}, u32[]{:S(2)}) collective-permute-start(bf16[64,896]{1,0:T(8,128)(2,1)S(1)} %get-tuple-element.102), channel_id=1, source_target_pairs={{0,3},{1,0},{2,1},{3,2},{4,7},{5,4},{6,5},{7,6},{8,11},{9,8},{10,9... | collective-permute-start | bytes 344072 | tf_op jit(solution)/shard_map/ppermute | solution.py:50
  70.7 7.2 %collective-permute-start.15 = (bf16[64,896]{1,0:T(8,128)(2,1)S(1)}, bf16[64,896]{1,0:T(8,128)(2,1)S(1)}, u32[]{:S(2)}, u32[]{:S(2)}) collective-permute-start(bf16[64,896]{1,0:T(8,128)(2,1)S(1)} %get-tuple-element.100), channel_id=1, source_target_pairs={{0,3},{1,0},{2,1},{3,2},{4,7},{5,4},{6,5},{7,6},{8,11},{9,8},{10,9... | collective-permute-start | bytes 344072 | tf_op jit(solution)/shard_map/ppermute | solution.py:50
  73.7 6.4 %collective-permute-start.13 = (bf16[64,896]{1,0:T(8,128)(2,1)S(1)}, bf16[64,896]{1,0:T(8,128)(2,1)S(1)}, u32[]{:S(2)}, u32[]{:S(2)}) collective-permute-start(bf16[64,896]{1,0:T(8,128)(2,1)S(1)} %get-tuple-element.99), channel_id=1, source_target_pairs={{0,2},{1,3},{2,0},{3,1},{4,6},{5,7},{6,4},{7,5},{8,10},{9,11},{10,... | collective-permute-start | bytes 344072 | tf_op jit(solution)/shard_map/ppermute | solution.py:50
  74.2 6.4 %collective-permute-start.19 = (bf16[64,896]{1,0:T(8,128)(2,1)S(1)}, bf16[64,896]{1,0:T(8,128)(2,1)S(1)}, u32[]{:S(2)}, u32[]{:S(2)}) collective-permute-start(bf16[64,896]{1,0:T(8,128)(2,1)S(1)} %add_convert_fusion.1), channel_id=1, source_target_pairs={{0,4},{1,5},{2,6},{3,7},{4,0},{5,1},{6,2},{7,3},{8,12},{9,13},{10,... | collective-permute-start | bytes 344072 | tf_op jit(solution)/shard_map/ppermute | solution.py:50

commit v6 on v5

--- a/solution.py
+++ b/solution.py
@@ -346,7 +346,8 @@
 
 def join_kernel(n, *refs):
     pieces, o_ref = refs[:n], refs[n]
-    logs = [sum(p[PIECE + j : PIECE + j + 1].astype(F32) for j in range(3)) for p in pieces]
+    tails = [p[PIECE:].astype(F32) for p in pieces]
+    logs = [tail[0:1] + tail[1:2] + tail[2:3] for tail in tails]
     best = functools.reduce(jnp.maximum, logs)
     shares = [jnp.exp2(v - best) for v in logs]
     total = sum(shares)

time: 83 us -> 83.5 us (level)
  the two profiles are of different devices: /device:TPU:0 before, /device:TPU:102 now
where the time goes in v6:
time: 83.5 us; the launch traced here: 83.3 us
  Pallas kernels  42.3 us (51%)
  starting transfers between devices  22.1 us (26%)
  waiting for transfers between devices  17 us (20%)
  between operations  0.92 us (1%)
    pallas_call x3, Pallas kernels, attention(): pl.pallas_call(functools.partial(attention_kernel, places, len(carry) > 0...  28.3 us
    ppermute x12, starting transfers between devices, to_ctx(): return lax.ppermute(array, 'ctx', pairs)  11.5 us
    ppermute x8, starting transfers between devices, to_head(): return lax.ppermute(array, 'head', pairs)  10.6 us
    ppermute x12, waiting for transfers between devices, to_ctx(): return lax.ppermute(array, 'ctx', pairs)  10.3 us
    ppermute x8, waiting for transfers between devices, to_head(): return lax.ppermute(array, 'head', pairs)  6.65 us
    pallas_call x4, Pallas kernels, project(): pl.pallas_call(functools.partial(project_kernel, blocks), in_specs=[SMEM]...  5.14 us
    pallas_call x1, Pallas kernels, near_keys_values(): pl.pallas_call(near_kernel, in_specs=[HBM] + vmem(1) + [HBM] * 2, out_spe...  4.13 us
    pallas_call x2, Pallas kernels, far_keys_values(): pl.pallas_call(form, in_specs=vmem(3), out_specs=vmem(2), out_shape=kv_sh...  2.78 us
  transfers between devices with their start and end apart: 20, of which 7 were waited for; matrix products, arithmetic and copies ran while one was open for 0% of the time, Pallas kernels for 34%

profile of v6, /device:TPU:102, one launch (start us, length us, event | category | flops | bytes accessed | tf_op | source)
XLA Modules:
  0.0 83.3 jit_solution(1600150344171356077)
XLA Ops:
  0.0 1.3 %split_queries.1 = (bf16[64,768]{1,0:T(8,128)(2,1)S(1)}, bf16[64,768]{1,0:T(8,128)(2,1)S(1)}, bf16[576,512]{1,0:T(8,128)(2,1)S(1)}, bf16[576,256]{1,0:T(8,128)(2,1)S(1)}) custom-call(bf16[64,1024]{1,0:T(8,128)(2,1)} %nope_ref.1, bf16[64,512]{1,0:T(8,128)(2,1)} %rope_ref.1, bf16[576,1024]{1,0:T(8,128)(2,1)} %cache_ref.3), custom_call_target="tpu_custom_call" | custom-call | tf_op jit(solution)/shard_map/split_queries/pallas_call | solution.py:90
  3.1 1.6 %collective-permute-start.3 = (bf16[128,768]{1,0:T(8,128)(2,1)S(1)}, bf16[128,768]{1,0:T(8,128)(2,1)S(1)}, u32[]{:S(2)}, u32[]{:S(2)}) collective-permute-start(bf16[128,768]{1,0:T(8,128)(2,1)S(1)} %constant_dynamic-update-slice_fusion.refs_0_), channel_id=1, source_target_pairs={{0,32},{8,40},{16,48},{24,56},{32,64},{40,72},{48,80},{56,88},{64,... | collective-permute-start | bytes 589832 | tf_op jit(solution)/shard_map/ppermute | solution.py:46
  4.8 1.7 %collective-permute-start.2 = (bf16[128,768]{1,0:T(8,128)(2,1)S(1)}, bf16[128,768]{1,0:T(8,128)(2,1)S(1)}, u32[]{:S(2)}, u32[]{:S(2)}) collective-permute-start(bf16[128,768]{1,0:T(8,128)(2,1)S(1)} %constant_dynamic-update-slice_fusion.refs_0_), channel_id=1, source_target_pairs={{0,96},{8,104},{16,112},{24,120},{32,0},{40,8},{48,16},{56,24},{64... | collective-permute-start | bytes 589832 | tf_op jit(solution)/shard_map/ppermute | solution.py:46
  6.4 2.0 %collective-permute-start.1 = (bf16[128,768]{1,0:T(8,128)(2,1)S(1)}, bf16[128,768]{1,0:T(8,128)(2,1)S(1)}, u32[]{:S(2)}, u32[]{:S(2)}) collective-permute-start(bf16[128,768]{1,0:T(8,128)(2,1)S(1)} %constant_dynamic-update-slice_fusion.refs_0_), channel_id=1, source_target_pairs={{0,64},{8,72},{16,80},{24,88},{32,96},{40,104},{48,112},{56,120},{... | collective-permute-start | bytes 589832 | tf_op jit(solution)/shard_map/ppermute | solution.py:46
  8.4 1.6 %collective-permute-start.7 = (bf16[576,512]{1,0:T(8,128)(2,1)S(1)}, bf16[576,512]{1,0:T(8,128)(2,1)S(1)}, u32[]{:S(2)}, u32[]{:S(2)}) collective-permute-start(bf16[576,512]{1,0:T(8,128)(2,1)S(1)} %get-tuple-element.66), channel_id=1, source_target_pairs={{0,16},{8,24},{16,0},{24,8},{32,48},{40,56},{48,32},{56,40},{64,80... | collective-permute-start | bytes 1769480 | tf_op jit(solution)/shard_map/ppermute | solution.py:46
  10.0 4.1 %near_keys_values.1 = (bf16[4,256,1024]{2,1,0:T(8,128)(2,1)S(1)}, bf16[4,1024,256]{2,1,0:T(8,128)(2,1)S(1)}, bf16[4,256,1024]{2,1,0:T(8,128)(2,1)S(1)}, bf16[4,1...) custom-call(bf16[576,1024]{1,0:T(8,128)(2,1)} %cache_ref.3, ...), custom_call_target="tpu_custom_call" | custom-call | flops 2147483648 | bytes 4194304 | tf_op jit(solution)/shard_map/near_keys_values/pallas_call | solution.py:144
  15.1 1.7 %collective-permute-done.1.refs_1_ = bf16[128,768]{1,0:T(8,128)(2,1)S(1)} collective-permute-done((bf16[128,768]{1,0:T(8,128)(2,1)S(1)}, bf16[128,768]{1,0:T(8,128)(2,1)S(1)}, u32[]{:S(2)}, u32[]{:S(2)}) %collective-permute-start.1) | collective-permute-done | bytes 196640 | tf_op jit(solution)/shard_map/ppermute | solution.py:46
  16.8 7.0 %attention.3 = (f32[4,512,256]{2,1,0:T(8,128)S(1)}, f32[4,512,128]{2,1,0:T(8,128)S(1)}) custom-call(s32[15]{0:T(128)S(1)} %stack.59.spot_ref, bf16[128,768]{1,0:T(8,128)(2,1)S(1)} %constant_dynamic-update-slice_fusion.refs_0_, bf16[128,768]{1,0:T(8,128)(2,1)S(1)} %collective-permute-done.1.refs_1_, bf16[128,768]{1,0:T(8,128)(2,1)S(1)} %collective-permute-done.2.refs_2_, ...), custom_call_target="tpu_custom_call" | custom-call | flops 4294967296 | bytes 4194304 | tf_op jit(solution)/shard_map/attention/pallas_call | solution.py:332
  24.1 1.4 %far_keys_values.2 = (bf16[4,256,1024]{2,1,0:T(8,128)(2,1)S(1)}, bf16[4,1024,256]{2,1,0:T(8,128)(2,1)S(1)}) custom-call(bf16[576,1024]{1,0:T(8,128)(2,1)S(1)} %constant_dynamic-update-slice_fusion.2.cache, bf16[4,128,512]{2,1,0:T(8,128)(2,1)S(1)} %get-tuple-element.76.uk, bf16[4,512,128]{2,1,0:T(8,128)(2,1)S(1)} %get-tuple-element.77.uv), custom_call_target="tpu_custom_call" | custom-call | flops 1073741824 | bytes 4194304 | tf_op jit(solution)/shard_map/far_keys_values/pallas_call | solution.py:158
  25.5 10.1 %attention.4 = (f32[4,512,256]{2,1,0:T(8,128)S(1)}, f32[4,512,128]{2,1,0:T(8,128)S(1)}) custom-call(s32[15]{0:T(128)S(1)} %stack.59.spot_ref, bf16[128,768]{1,0:T(8,128)(2,1)S(1)} %constant_dynamic-update-slice_fusion.refs_0_, bf16[128,768]{1,0:T(8,128)(2,1)S(1)} %collective-permute-done.1.refs_1_, bf16[128,768]{1,0:T(8,128)(2,1)S(1)} %collective-permute-done.2.refs_2_, ...), custom_call_target="tpu_custom_call" | custom-call | flops 2147483648 | bytes 4194304 | tf_op jit(solution)/shard_map/attention/pallas_call | solution.py:332
  35.6 1.4 %far_keys_values.3 = (bf16[4,256,1024]{2,1,0:T(8,128)(2,1)S(1)}, bf16[4,1024,256]{2,1,0:T(8,128)(2,1)S(1)}) custom-call(bf16[576,1024]{1,0:T(8,128)(2,1)S(1)} %collective-permute-done.8.cache, bf16[4,128,512]{2,1,0:T(8,128)(2,1)S(1)} %get-tuple-element.76.uk, bf16[4,512,128]{2,1,0:T(8,128)(2,1)S(1)} %get-tuple-element.77.uv), custom_call_target="tpu_custom_call" | custom-call | flops 1073741824 | bytes 4194304 | tf_op jit(solution)/shard_map/far_keys_values/pallas_call | solution.py:158
  37.0 11.2 %attention.5 = (bf16[144,512]{1,0:T(8,128)(2,1)S(1)}, bf16[144,512]{1,0:T(8,128)(2,1)S(1)}, bf16[144,512]{1,0:T(8,128)(2,1)S(1)}, bf16[144,512]{1,0:T(8,128)(2,1)S(1)}) custom-call(s32[15]{0:T(128)S(1)} %stack.59.spot_ref, bf16[128,768]{1,0:T(8,128)(2,1)S(1)} %constant_dynamic-update-slice_fusion.refs_0_, ...), custom_call_target="tpu_custom_call" | custom-call | flops 2147483648 | bytes 4194304 | tf_op jit(solution)/shard_map/attention/pallas_call | solution.py:332
  48.4 3.2 %collective-permute-start.11 = (bf16[144,512]{1,0:T(8,128)(2,1)S(1)}, bf16[144,512]{1,0:T(8,128)(2,1)S(1)}, u32[]{:S(2)}, u32[]{:S(2)}) collective-permute-start(bf16[144,512]{1,0:T(8,128)(2,1)S(1)} %get-tuple-element.92), channel_id=1, source_target_pairs={{0,96},{8,104},{16,112},{24,120},{32,0},{40,8},{48,16},{56,24},{64... | collective-permute-start | bytes 442376 | tf_op jit(solution)/shard_map/ppermute | solution.py:46
  51.7 4.9 %collective-permute-done.9.refs_1_ = bf16[144,512]{1,0:T(8,128)(2,1)S(1)} collective-permute-done((bf16[144,512]{1,0:T(8,128)(2,1)S(1)}, bf16[144,512]{1,0:T(8,128)(2,1)S(1)}, u32[]{:S(2)}, u32[]{:S(2)}) %collective-permute-start.9) | collective-permute-done | bytes 147488 | tf_op jit(solution)/shard_map/ppermute | solution.py:46
  56.5 2.5 %collective-permute-done.10.refs_2_ = bf16[144,512]{1,0:T(8,128)(2,1)S(1)} collective-permute-done((bf16[144,512]{1,0:T(8,128)(2,1)S(1)}, bf16[144,512]{1,0:T(8,128)(2,1)S(1)}, u32[]{:S(2)}, u32[]{:S(2)}) %collective-permute-start.10) | collective-permute-done | bytes 147488 | tf_op jit(solution)/shard_map/ppermute | solution.py:46
  62.0 1.5 %collective-permute-start.16 = (bf16[64,896]{1,0:T(8,128)(2,1)S(1)}, bf16[64,896]{1,0:T(8,128)(2,1)S(1)}, u32[]{:S(2)}, u32[]{:S(2)}) collective-permute-start(bf16[64,896]{1,0:T(8,128)(2,1)S(1)} %project.4), channel_id=1, source_target_pairs={{0,2},{1,3},{2,0},{3,1},{4,6},{5,7},{6,4},{7,5},{8,10},{9,11},{10,... | collective-permute-start | bytes 344072 | tf_op jit(solution)/shard_map/ppermute | solution.py:50
  63.5 1.3 %project.5 = (bf16[64,896]{1,0:T(8,128)(2,1)S(1)}, bf16[64,896]{1,0:T(8,128)(2,1)S(1)}) custom-call(s32[15]{0:T(128)S(1)} %stack.59.spot_ref, bf16[128,512]{1,0:T(8,128)(2,1)S(1)} %join.1.mine_ref, bf16[64,512]{1,0:T(8,128)(2,1)S(1)} %collective-permute-done.12.theirs_ref, bf16[1024,7168]{1,0:T(8,128)(2,1)S(1)} %bitcast.15), custom_call_target="tpu_custom_call" | custom-call | flops 939524096 | bytes 4194304 | tf_op jit(solution)/shard_map/project/pallas_call | solution.py:389
  64.8 2.1 %collective-permute-start.17 = (bf16[64,896]{1,0:T(8,128)(2,1)S(1)}, bf16[64,896]{1,0:T(8,128)(2,1)S(1)}, u32[]{:S(2)}, u32[]{:S(2)}) collective-permute-start(bf16[64,896]{1,0:T(8,128)(2,1)S(1)} %get-tuple-element.94), channel_id=1, source_target_pairs={{0,1},{1,2},{2,3},{3,0},{4,5},{5,6},{6,7},{7,4},{8,9},{9,10},{10,1... | collective-permute-start | bytes 344072 | tf_op jit(solution)/shard_map/ppermute | solution.py:50
  66.9 1.3 %project.6 = (bf16[64,896]{1,0:T(8,128)(2,1)S(1)}, bf16[64,896]{1,0:T(8,128)(2,1)S(1)}) custom-call(s32[15]{0:T(128)S(1)} %stack.59.spot_ref, bf16[128,512]{1,0:T(8,128)(2,1)S(1)} %join.1.mine_ref, bf16[64,512]{1,0:T(8,128)(2,1)S(1)} %collective-permute-done.12.theirs_ref, bf16[1024,7168]{1,0:T(8,128)(2,1)S(1)} %bitcast.15), custom_call_target="tpu_custom_call" | custom-call | flops 939524096 | bytes 4194304 | tf_op jit(solution)/shard_map/project/pallas_call | solution.py:389
  68.9 1.4 %collective-permute-start.18 = (bf16[64,896]{1,0:T(8,128)(2,1)S(1)}, bf16[64,896]{1,0:T(8,128)(2,1)S(1)}, u32[]{:S(2)}, u32[]{:S(2)}) collective-permute-start(bf16[64,896]{1,0:T(8,128)(2,1)S(1)} %get-tuple-element.102), channel_id=1, source_target_pairs={{0,3},{1,0},{2,1},{3,2},{4,7},{5,4},{6,5},{7,6},{8,11},{9,8},{10,9... | collective-permute-start | bytes 344072 | tf_op jit(solution)/shard_map/ppermute | solution.py:50
  70.3 1.6 %project.7 = (bf16[64,896]{1,0:T(8,128)(2,1)S(1)}, bf16[64,896]{1,0:T(8,128)(2,1)S(1)}, bf16[64,896]{1,0:T(8,128)(2,1)S(1)}) custom-call(s32[15]{0:T(128)S(1)} %stack.59.spot_ref, bf16[128,512]{1,0:T(8,128)(2,1)S(1)} %join.1.mine_ref, bf16[64,512]{1,0:T(8,128)(2,1)S(1)} %collective-permute-done.12.theirs_ref, bf16[1024,7168]{1,0:T(8,128)(2,1)S(1)} %bitcast.15), custom_call_target="tpu_custom_call" | custom-call | flops 1409286144 | bytes 6291456 | tf_op jit(solution)/shard_map/project/pallas_call | solution.py:389
  71.9 3.3 %collective-permute-start.13 = (bf16[64,896]{1,0:T(8,128)(2,1)S(1)}, bf16[64,896]{1,0:T(8,128)(2,1)S(1)}, u32[]{:S(2)}, u32[]{:S(2)}) collective-permute-start(bf16[64,896]{1,0:T(8,128)(2,1)S(1)} %get-tuple-element.99), channel_id=1, source_target_pairs={{0,2},{1,3},{2,0},{3,1},{4,6},{5,7},{6,4},{7,5},{8,10},{9,11},{10,... | collective-permute-start | bytes 344072 | tf_op jit(solution)/shard_map/ppermute | solution.py:50
  76.8 2.5 %collective-permute-done.15 = bf16[64,896]{1,0:T(8,128)(2,1)S(1)} collective-permute-done((bf16[64,896]{1,0:T(8,128)(2,1)S(1)}, bf16[64,896]{1,0:T(8,128)(2,1)S(1)}, u32[]{:S(2)}, u32[]{:S(2)}) %collective-permute-start.15) | collective-permute-done | bytes 114720 | tf_op jit(solution)/shard_map/ppermute | solution.py:50
  79.4 3.3 %collective-permute-done.19 = bf16[64,896]{1,0:T(8,128)(2,1)S(1)} collective-permute-done((bf16[64,896]{1,0:T(8,128)(2,1)S(1)}, bf16[64,896]{1,0:T(8,128)(2,1)S(1)}, u32[]{:S(2)}, u32[]{:S(2)}) %collective-permute-start.19) | collective-permute-done | bytes 114720 | tf_op jit(solution)/shard_map/ppermute | solution.py:50
  (46 shorter events, 8.4 us)
Async XLA Ops:
  0.0 8.4 %collective-permute-start.5 = (bf16[576,1024]{1,0:T(8,128)(2,1)}, bf16[576,1024]{1,0:T(8,128)(2,1)S(1)}, u32[]{:S(2)}, u32[]{:S(2)}) collective-permute-start(bf16[576,1024]{1,0:T(8,128)(2,1)} %cache_ref.3), channel_id=1, source_target_pairs={{0,8},{8,0},{16,24},{24,16},{32,40},{40,32},{48,56},{56,48},{64,72... | collective-permute-start | bytes 3538952 | tf_op jit(solution)/shard_map/ppermute | solution.py:46
  1.3 1.8 %collective-permute-start = (bf16[64,768]{1,0:T(8,128)(2,1)S(1)}, bf16[64,768]{1,0:T(8,128)(2,1)S(1)}, u32[]{:S(2)}, u32[]{:S(2)}) collective-permute-start(bf16[64,768]{1,0:T(8,128)(2,1)S(1)} %get-tuple-element.55), channel_id=1, source_target_pairs={{0,8},{8,0},{16,24},{24,16},{32,40},{40,32},{48,56},{56,48},{64,72... | collective-permute-start | bytes 294920 | tf_op jit(solution)/shard_map/ppermute | solution.py:46
  1.9 12.2 %collective-permute-start.4 = (bf16[576,256]{1,0:T(8,128)(2,1)S(1)}, bf16[576,256]{1,0:T(8,128)(2,1)S(1)}, u32[]{:S(2)}, u32[]{:S(2)}) collective-permute-start(bf16[576,256]{1,0:T(8,128)(2,1)S(1)} %get-tuple-element.56), channel_id=1, source_target_pairs={{0,16},{8,24},{16,0},{24,8},{32,48},{40,56},{48,32},{56,40},{64,80... | collective-permute-start | bytes 884744 | tf_op jit(solution)/shard_map/ppermute | solution.py:46
  3.1 12.0 %collective-permute-start.3 = (bf16[128,768]{1,0:T(8,128)(2,1)S(1)}, bf16[128,768]{1,0:T(8,128)(2,1)S(1)}, u32[]{:S(2)}, u32[]{:S(2)}) collective-permute-start(bf16[128,768]{1,0:T(8,128)(2,1)S(1)} %constant_dynamic-update-slice_fusion.refs_0_), channel_id=1, source_target_pairs={{0,32},{8,40},{16,48},{24,56},{32,64},{40,72},{48,80},{56,88},{64,... | collective-permute-start | bytes 589832 | tf_op jit(solution)/shard_map/ppermute | solution.py:46
  4.8 10.3 %collective-permute-start.2 = (bf16[128,768]{1,0:T(8,128)(2,1)S(1)}, bf16[128,768]{1,0:T(8,128)(2,1)S(1)}, u32[]{:S(2)}, u32[]{:S(2)}) collective-permute-start(bf16[128,768]{1,0:T(8,128)(2,1)S(1)} %constant_dynamic-update-slice_fusion.refs_0_), channel_id=1, source_target_pairs={{0,96},{8,104},{16,112},{24,120},{32,0},{40,8},{48,16},{56,24},{64... | collective-permute-start | bytes 589832 | tf_op jit(solution)/shard_map/ppermute | solution.py:46
  6.4 10.4 %collective-permute-start.1 = (bf16[128,768]{1,0:T(8,128)(2,1)S(1)}, bf16[128,768]{1,0:T(8,128)(2,1)S(1)}, u32[]{:S(2)}, u32[]{:S(2)}) collective-permute-start(bf16[128,768]{1,0:T(8,128)(2,1)S(1)} %constant_dynamic-update-slice_fusion.refs_0_), channel_id=1, source_target_pairs={{0,64},{8,72},{16,80},{24,88},{32,96},{40,104},{48,112},{56,120},{... | collective-permute-start | bytes 589832 | tf_op jit(solution)/shard_map/ppermute | solution.py:46
  8.4 15.4 %collective-permute-start.7 = (bf16[576,512]{1,0:T(8,128)(2,1)S(1)}, bf16[576,512]{1,0:T(8,128)(2,1)S(1)}, u32[]{:S(2)}, u32[]{:S(2)}) collective-permute-start(bf16[576,512]{1,0:T(8,128)(2,1)S(1)} %get-tuple-element.66), channel_id=1, source_target_pairs={{0,16},{8,24},{16,0},{24,8},{32,48},{40,56},{48,32},{56,40},{64,80... | collective-permute-start | bytes 1769480 | tf_op jit(solution)/shard_map/ppermute | solution.py:46
  14.2 9.6 %collective-permute-start.6 = (bf16[576,256]{1,0:T(8,128)(2,1)S(1)}, bf16[576,256]{1,0:T(8,128)(2,1)S(1)}, u32[]{:S(2)}, u32[]{:S(2)}) collective-permute-start(bf16[576,256]{1,0:T(8,128)(2,1)S(1)} %collective-permute-done.4), channel_id=1, source_target_pairs={{0,1},{1,0},{2,3},{3,2},{4,5},{5,4},{6,7},{7,6},{8,9},{9,8},{10,11... | collective-permute-start | bytes 884744 | tf_op jit(solution)/shard_map/ppermute | solution.py:50
  16.8 44.2 %slice-start = ((s8[14680064]{0:T(1024)(128)(4,1)}), s8[2097152]{0:T(1024)(128)(4,1)S(1)}, s32[]{:S(2)}) async-start(s8[14680064]{0:T(1024)(128)(4,1)} %bitcast.14), calls=%async_computation | async-start | bytes 4194304
  16.8 44.2 %slice-start.1 = ((s8[14680064]{0:T(1024)(128)(4,1)}), s8[4194304]{0:T(1024)(128)(4,1)S(1)}, s32[]{:S(2)}) async-start(s8[14680064]{0:T(1024)(128)(4,1)} %bitcast.14), calls=%async_computation.1 | async-start | bytes 8388608
  24.0 37.0 %slice-start.2 = ((s8[14680064]{0:T(1024)(128)(4,1)}), s8[4194304]{0:T(1024)(128)(4,1)S(1)}, s32[]{:S(2)}) async-start(s8[14680064]{0:T(1024)(128)(4,1)} %bitcast.14), calls=%async_computation.2 | async-start | bytes 8388608
  24.0 11.6 %collective-permute-start.8 = (bf16[576,1024]{1,0:T(8,128)(2,1)S(1)}, bf16[576,1024]{1,0:T(8,128)(2,1)S(1)}, u32[]{:S(2)}, u32[]{:S(2)}) collective-permute-start(bf16[576,1024]{1,0:T(8,128)(2,1)S(1)} %constant_dynamic-update-slice_fusion.2.cache), channel_id=1, source_target_pairs={{0,8},{8,0},{16,24},{24,16},{32,40},{40,32},{48,56},{56,48},{64,72... | collective-permute-start | bytes 3538952 | tf_op jit(solution)/shard_map/ppermute | solution.py:46
  35.6 25.4 %slice-start.3 = ((s8[14680064]{0:T(1024)(128)(4,1)}), s8[4194304]{0:T(1024)(128)(4,1)S(1)}, s32[]{:S(2)}) async-start(s8[14680064]{0:T(1024)(128)(4,1)} %bitcast.14), calls=%async_computation.3 | async-start | bytes 8388608
  48.3 8.3 %collective-permute-start.9 = (bf16[144,512]{1,0:T(8,128)(2,1)S(1)}, bf16[144,512]{1,0:T(8,128)(2,1)S(1)}, u32[]{:S(2)}, u32[]{:S(2)}) collective-permute-start(bf16[144,512]{1,0:T(8,128)(2,1)S(1)} %get-tuple-element.90), channel_id=1, source_target_pairs={{0,64},{8,72},{16,80},{24,88},{32,96},{40,104},{48,112},{56,120},{... | collective-permute-start | bytes 442376 | tf_op jit(solution)/shard_map/ppermute | solution.py:46
  48.3 10.7 %collective-permute-start.10 = (bf16[144,512]{1,0:T(8,128)(2,1)S(1)}, bf16[144,512]{1,0:T(8,128)(2,1)S(1)}, u32[]{:S(2)}, u32[]{:S(2)}) collective-permute-start(bf16[144,512]{1,0:T(8,128)(2,1)S(1)} %get-tuple-element.91), channel_id=1, source_target_pairs={{0,32},{8,40},{16,48},{24,56},{32,64},{40,72},{48,80},{56,88},{64,... | collective-permute-start | bytes 442376 | tf_op jit(solution)/shard_map/ppermute | solution.py:46
  48.4 10.6 %collective-permute-start.11 = (bf16[144,512]{1,0:T(8,128)(2,1)S(1)}, bf16[144,512]{1,0:T(8,128)(2,1)S(1)}, u32[]{:S(2)}, u32[]{:S(2)}) collective-permute-start(bf16[144,512]{1,0:T(8,128)(2,1)S(1)} %get-tuple-element.92), channel_id=1, source_target_pairs={{0,96},{8,104},{16,112},{24,120},{32,0},{40,8},{48,16},{56,24},{64... | collective-permute-start | bytes 442376 | tf_op jit(solution)/shard_map/ppermute | solution.py:46
  59.6 1.3 %collective-permute-start.12 = (bf16[64,512]{1,0:T(8,128)(2,1)S(1)}, bf16[64,512]{1,0:T(8,128)(2,1)S(1)}, u32[]{:S(2)}, u32[]{:S(2)}) collective-permute-start(bf16[64,512]{1,0:T(8,128)(2,1)S(1)} %slice.4), channel_id=1, source_target_pairs={{0,8},{8,0},{16,24},{24,16},{32,40},{40,32},{48,56},{56,48},{64,72... | collective-permute-start | bytes 196616 | tf_op jit(solution)/shard_map/ppermute | solution.py:46
  62.0 9.9 %collective-permute-start.16 = (bf16[64,896]{1,0:T(8,128)(2,1)S(1)}, bf16[64,896]{1,0:T(8,128)(2,1)S(1)}, u32[]{:S(2)}, u32[]{:S(2)}) collective-permute-start(bf16[64,896]{1,0:T(8,128)(2,1)S(1)} %project.4), channel_id=1, source_target_pairs={{0,2},{1,3},{2,0},{3,1},{4,6},{5,7},{6,4},{7,5},{8,10},{9,11},{10,... | collective-permute-start | bytes 344072 | tf_op jit(solution)/shard_map/ppermute | solution.py:50
  64.8 11.4 %collective-permute-start.17 = (bf16[64,896]{1,0:T(8,128)(2,1)S(1)}, bf16[64,896]{1,0:T(8,128)(2,1)S(1)}, u32[]{:S(2)}, u32[]{:S(2)}) collective-permute-start(bf16[64,896]{1,0:T(8,128)(2,1)S(1)} %get-tuple-element.94), channel_id=1, source_target_pairs={{0,1},{1,2},{2,3},{3,0},{4,5},{5,6},{6,7},{7,4},{8,9},{9,10},{10,1... | collective-permute-start | bytes 344072 | tf_op jit(solution)/shard_map/ppermute | solution.py:50
  68.2 11.2 %collective-permute-start.14 = (bf16[64,896]{1,0:T(8,128)(2,1)S(1)}, bf16[64,896]{1,0:T(8,128)(2,1)S(1)}, u32[]{:S(2)}, u32[]{:S(2)}) collective-permute-start(bf16[64,896]{1,0:T(8,128)(2,1)S(1)} %get-tuple-element.96), channel_id=1, source_target_pairs={{0,1},{1,2},{2,3},{3,0},{4,5},{5,6},{6,7},{7,4},{8,9},{9,10},{10,1... | collective-permute-start | bytes 344072 | tf_op jit(solution)/shard_map/ppermute | solution.py:50
  68.9 7.3 %collective-permute-start.18 = (bf16[64,896]{1,0:T(8,128)(2,1)S(1)}, bf16[64,896]{1,0:T(8,128)(2,1)S(1)}, u32[]{:S(2)}, u32[]{:S(2)}) collective-permute-start(bf16[64,896]{1,0:T(8,128)(2,1)S(1)} %get-tuple-element.102), channel_id=1, source_target_pairs={{0,3},{1,0},{2,1},{3,2},{4,7},{5,4},{6,5},{7,6},{8,11},{9,8},{10,9... | collective-permute-start | bytes 344072 | tf_op jit(solution)/shard_map/ppermute | solution.py:50
  70.3 9.1 %collective-permute-start.15 = (bf16[64,896]{1,0:T(8,128)(2,1)S(1)}, bf16[64,896]{1,0:T(8,128)(2,1)S(1)}, u32[]{:S(2)}, u32[]{:S(2)}) collective-permute-start(bf16[64,896]{1,0:T(8,128)(2,1)S(1)} %get-tuple-element.100), channel_id=1, source_target_pairs={{0,3},{1,0},{2,1},{3,2},{4,7},{5,4},{6,5},{7,6},{8,11},{9,8},{10,9... | collective-permute-start | bytes 344072 | tf_op jit(solution)/shard_map/ppermute | solution.py:50
  71.9 7.4 %collective-permute-start.13 = (bf16[64,896]{1,0:T(8,128)(2,1)S(1)}, bf16[64,896]{1,0:T(8,128)(2,1)S(1)}, u32[]{:S(2)}, u32[]{:S(2)}) collective-permute-start(bf16[64,896]{1,0:T(8,128)(2,1)S(1)} %get-tuple-element.99), channel_id=1, source_target_pairs={{0,2},{1,3},{2,0},{3,1},{4,6},{5,7},{6,4},{7,5},{8,10},{9,11},{10,... | collective-permute-start | bytes 344072 | tf_op jit(solution)/shard_map/ppermute | solution.py:50
  76.2 6.4 %collective-permute-start.19 = (bf16[64,896]{1,0:T(8,128)(2,1)S(1)}, bf16[64,896]{1,0:T(8,128)(2,1)S(1)}, u32[]{:S(2)}, u32[]{:S(2)}) collective-permute-start(bf16[64,896]{1,0:T(8,128)(2,1)S(1)} %add_convert_fusion.1), channel_id=1, source_target_pairs={{0,4},{1,5},{2,6},{3,7},{4,0},{5,1},{6,2},{7,3},{8,12},{9,13},{10,... | collective-permute-start | bytes 344072 | tf_op jit(solution)/shard_map/ppermute | solution.py:50
